TPU v7x, 256 devices: a whole 4x4x8 slice. The times are simulated.
256 devices in a mesh: layer: 4 (over z_hi, core), lat: 64 (over z_lo, x, y).
Axes of the slice: x: 4, y: 4, z: 8 (z_hi: 2, z_lo: 4; z = z_hi * 4 + z_lo), core: 2. Of those that a mesh axis runs over, the one named last changes fastest.
Arguments:
- resid_in: bfloat16 [128, 2, 4, 2304], P('lat', None, 'layer'), may hold values from -6 to 6
- enc_weight: bfloat16 [2, 4, 2304, 8192], P(None, 'layer', None, 'lat'), may hold values from -0.125 to 0.125
- enc_bias: bfloat16 [2, 4, 8192], P(None, 'layer', 'lat'), may hold values from -4 to 4
- dec_weight: bfloat16 [4, 9, 8192, 2304], P('layer', None, 'lat'), may hold values from -0.0625 to 0.0625
- dec_bias: bfloat16 [8, 2304], P('layer'), may hold values from -3 to 3
- act_blocks: int32 [2, 4, 2, 16], P(None, 'layer'), may hold values from 0 to 63, all different within a row
- tile_order: int32 [2], replicated, may hold values from 0 to 1, each once
- targets: bfloat16 [128, 8, 2304], P('lat', 'layer'), may hold values from -6 to 6
Outputs:
- recon_error: bfloat16 [128, 8, 2304], P('lat', 'layer')
- dec_grad: bfloat16 [4, 9, 8192, 2304], P('layer', None, 'lat')
Inputs may be any that keep to these rules, and one draw needn't show every extreme that they name: `act_blocks`: each row lists 16 different latent blocks, and every block is listed by some row. `tile_order`: a permutation of the 2 token tiles.
All inputs are finite; a program needn't handle non-finite values.
Results may differ from a plain program's by a relative error of at most 0.0037.
Values may be sent and summed in bfloat16 or wider, within the bound.
No kernel may reach another device: no remote copies, remote signals or barrier semaphores. Data moves between devices by JAX's collectives and lax.ppermute only.
A program may use at most 128 MiB of HBM per device.

v0:
```python
import jax
import jax.numpy as jnp
from jax import lax
from jax.sharding import PartitionSpec as P

BLK = 128
TILE = 64


def local(resid_in, enc_weight, enc_bias, dec_weight, dec_bias, act_blocks, tile_order, targets):
    owner_idx = lax.axis_index("layer")
    lat_index = lax.axis_index("lat")
    layers = 2 * lax.axis_size("layer")
    pairs = dec_weight.shape[1]
    local_width = enc_weight.shape[3]
    feat_width = dec_weight.shape[3]
    blocks_dev = local_width // BLK
    n_tiles = tile_order.shape[0]
    my_blocks = lat_index * blocks_dev + jnp.arange(blocks_dev, dtype=jnp.int32)
    block_hits = jnp.any(act_blocks[:, 0, :, :, None] == my_blocks[None, None, None, :], axis=2)
    order_hit = tile_order[:, None] == jnp.arange(n_tiles, dtype=jnp.int32)[None, :]
    row_tiles = jnp.any(order_hit[None, :, :, None] & block_hits[:, None, :, :], axis=2)
    shard_rows = lax.all_gather(resid_in, "lat", axis=0, tiled=True)
    row_count = shard_rows.shape[0]
    tile_ids = jnp.arange(row_count, dtype=jnp.int32) // TILE
    tile_hit = tile_ids[:, None] == jnp.arange(n_tiles, dtype=jnp.int32)[None, :]
    row_mask = jnp.any(tile_hit[:, None, :, None] & row_tiles[None], axis=2)
    lat_mask = jnp.repeat(row_mask, BLK, axis=2)
    pre_act = (
        jnp.einsum(
            "rhd,hdf->rhf",
            shard_rows[:, :, 0, :],
            enc_weight[:, 0],
            preferred_element_type=jnp.float32,
        )
        + enc_bias[:, 0].astype(jnp.float32)[None]
    )
    latents = jnp.where(lat_mask, jnp.maximum(pre_act, 0.0), 0.0).astype(jnp.bfloat16)
    slot_ids = jnp.arange(pairs, dtype=jnp.int32)
    first_src = slot_ids < layers - owner_idx
    target_ids = jnp.arange(layers, dtype=jnp.int32)

    def pick_latents(rows_lat):
        return jnp.where(first_src[None, :, None], rows_lat[:, 0:1, :], rows_lat[:, 1:2, :])

    contrib = jnp.einsum(
        "rkf,kfd->rkd", pick_latents(latents), dec_weight[0], preferred_element_type=jnp.float32
    )
    row_count = contrib.shape[0]
    padded = jnp.concatenate(
        [jnp.zeros((row_count, layers, feat_width), jnp.float32), contrib], axis=1
    )
    own_part = lax.dynamic_slice_in_dim(padded, layers - owner_idx, layers, 1)
    late_part = jnp.where(
        (target_ids + 1 >= layers - owner_idx)[None, :, None], contrib[:, 1:, :], 0.0
    )
    projected = own_part + late_part
    by_target = lax.psum_scatter(projected, "layer", scatter_dimension=1, tiled=True)
    recon_sum = lax.psum_scatter(by_target, "lat", scatter_dimension=0, tiled=True)
    recon_error = (
        recon_sum + dec_bias.astype(jnp.float32)[None] - targets.astype(jnp.float32)
    ).astype(jnp.bfloat16)
    grad_scale = latents.shape[0] ** (-0.5)
    all_tokens = lax.all_gather(recon_error, "lat", axis=0, tiled=True)
    full_error = lax.all_gather(all_tokens, "layer", axis=1, tiled=True)
    row_count = full_error.shape[0]
    extended = jnp.concatenate(
        [full_error, jnp.zeros((row_count, layers, feat_width), jnp.bfloat16)], axis=1
    )
    err_ahead = lax.dynamic_slice_in_dim(extended, owner_idx, pairs, 1)
    behind = jnp.concatenate(
        [jnp.zeros((row_count, 1, feat_width), jnp.bfloat16), full_error], axis=1
    )
    slot_errors = jnp.where(first_src[None, :, None], err_ahead, behind)
    grad_sum = jnp.einsum(
        "rkf,rkd->kfd", pick_latents(latents), slot_errors, preferred_element_type=jnp.float32
    )
    dec_grad = (grad_sum * grad_scale).astype(jnp.bfloat16)[None]
    return (recon_error, dec_grad)


def solution(mesh):
    return jax.shard_map(
        local,
        mesh=mesh,
        in_specs=(
            P("lat", None, "layer", None),
            P(None, "layer", None, "lat"),
            P(None, "layer", "lat"),
            P("layer", None, "lat", None),
            P("layer", None),
            P(None, "layer", None, None),
            P(),
            P("lat", "layer", None),
        ),
        out_specs=(P("lat", "layer", None), P("layer", None, "lat", None)),
        check_vma=False,
    )
```

profile of v0, /device:TPU:1, one launch (start us, length us, event | category | flops | bytes accessed | tf_op | source)
XLA Modules:
  0.0 1668.4 jit_solution(9054431123426871180)
XLA Ops:
  7.2 0.0 all-gather.4.cloned.1.call-start
  7.2 0.7 all-gather.4.cloned.1.call-update
  7.9 0.0 reduce-scatter.3.cloned.1.call-start
  8.0 0.8 compare_reduce_fusion
  8.8 0.7 iota_compare_fusion
  9.6 0.1 and_reduce_fusion.1
  9.7 0.1 and_reduce_fusion
  9.8 0.7 bitcast_convert_fusion
  10.5 305.9 %all-gather.4.cloned.1.call-done = bf16[128,2,1,2304]{3,1,2,0:T(2,128)(2,1)} async-done(((bf16[2,2,1,2304]{3,1,2,0:T(2,128)(2,1)}), bf16[128,2,1,2304]{3,1,2,0:T(2,128)(2,1)}) %all-gather.4.cloned.1.call-update) | async-done | bytes 1179664 | tf_op jit(solution)/shard_map/all_gather | solution.py:23
  316.4 1.8 fusion.33
  318.2 8.2 convolution_bitcast_fusion
  326.4 10.8 fusion
  337.3 0.0 all-reduce.6.cloned.1.call-start
  337.3 188.2 %reduce-scatter.3.cloned.1.call-done = f32[128,2,2304]{2,0,1:T(8,128)} async-done(((f32[128,8,2304]{2,0,1:T(8,128)}), f32[128,2,2304]{2,0,1:T(8,128)}) %reduce-scatter.3.cloned.1.call-update) | async-done | bytes 2359312 | tf_op jit(solution)/shard_map/reduce_scatter | solution.py:58
  525.5 0.0 all-gather.6.cloned.1.call-start
  525.6 0.6 dynamic-slice
  526.9 666.0 %all-reduce.6.cloned.1.call-done = f32[128,2,2304]{2,0,1:T(8,128)} async-done(((f32[128,2,2304]{2,0,1:T(8,128)}), f32[128,2,2304]{2,0,1:T(8,128)}) %all-reduce.6.cloned.1.call-update) | async-done | bytes 2359312
  1192.9 1.0 fusion.47
  1193.9 0.6 copy.28
  1194.5 0.0 all-gather.8.cloned.1.call-start
  1194.6 341.2 %all-gather.6.cloned.1.call-done = bf16[128,2,2304]{2,1,0:T(2,128)(2,1)} async-done(((bf16[2,2,2304]{2,1,0:T(2,128)(2,1)}), bf16[128,2,2304]{2,1,0:T(2,128)(2,1)}) %all-gather.6.cloned.1.call-update) | async-done | bytes 1179664 | tf_op jit(solution)/shard_map/all_gather | solution.py:64
  1535.7 2.4 copy.27
  1538.1 115.7 %all-gather.8.cloned.1.call-done = bf16[128,8,2304]{2,0,1:T(8,128)(2,1)} async-done(((bf16[128,2,2304]{2,0,1:T(8,128)(2,1)}), bf16[128,8,2304]{2,0,1:T(8,128)(2,1)}) %all-gather.8.cloned.1.call-update) | async-done | bytes 4718608 | tf_op jit(solution)/shard_map/all_gather | solution.py:65
  1653.8 8.1 fusion.6
  (18 shorter events, 0.1 us)
Async XLA Ops:
  7.2 309.2 %copy-start = (bf16[2,1,2304,128]{3,2,1,0:T(8,128)(2,1)S(1)}, bf16[2,1,2304,128]{3,2,1,0:T(8,128)(2,1)}, u32[]{:S(2)}) copy-start(bf16[2,1,2304,128]{3,2,1,0:T(8,128)(2,1)} %param.9) | copy-start | bytes 3538948
  7.2 309.2 %all-gather.4.cloned.1.call-start = ((), (), s32[]{:S(2)}) async-start(), calls=%async_computation.1 | async-start | bytes 1198080 | tf_op jit(solution)/shard_map/all_gather | solution.py:23
  7.9 517.6 %reduce-scatter.3.cloned.1.call-start = ((), (), s32[]{:S(2)}) async-start(), calls=%async_computation.2 | async-start | bytes 11796480 | tf_op jit(solution)/shard_map/reduce_scatter | solution.py:58
  337.2 188.3 %copy-start.2 = (bf16[2,2304]{1,0:T(2,128)(2,1)S(1)}, bf16[2,2304]{1,0:T(2,128)(2,1)}, u32[]{:S(2)}) copy-start(bf16[2,2304]{1,0:T(2,128)(2,1)} %param.12) | copy-start | bytes 27652
  337.3 188.4 %copy-start.3 = (u32[256]{0:T(256)S(1)}, u32[256]{0:T(256)}, u32[]{:S(2)}) copy-start(u32[256]{0:T(256)} %constant.62) | copy-start | bytes 3076
  337.3 855.7 %copy-start.1 = (bf16[2,2,2304]{2,1,0:T(2,128)(2,1)S(1)}, bf16[2,2,2304]{2,1,0:T(2,128)(2,1)}, u32[]{:S(2)}) copy-start(bf16[2,2,2304]{2,1,0:T(2,128)(2,1)} %param.15) | copy-start | bytes 55300
  337.3 855.6 %all-reduce.6.cloned.1.call-start = ((), (), s32[]{:S(2)}) async-start(), calls=%async_computation.5 | async-start | bytes 4718592
  525.5 1010.2 %all-gather.6.cloned.1.call-start = ((), (), s32[]{:S(2)}) async-start(), calls=%async_computation.3 | async-start | bytes 1198080 | tf_op jit(solution)/shard_map/all_gather | solution.py:64
  1194.5 459.3 %all-gather.8.cloned.1.call-start = ((), (), s32[]{:S(2)}) async-start(), calls=%async_computation.4 | async-start | bytes 5898240 | tf_op jit(solution)/shard_map/all_gather | solution.py:65
Sparse Core Ops, SparseCore 0:
  9.8 306.5 all-gather.3
  337.4 188.0 reduce-scatter.2
  528.1 664.7 all-reduce.5
  1195.3 340.4 all-gather.5
  1538.3 115.5 all-gather.7
where the time goes:
time: 1670 us
  waiting for transfers between devices  1620 us (97%)
  matrix products  18.1 us (1%)
    unnamed x6, waiting for transfers between devices  667 us
    all_gather x1, waiting for transfers between devices, local(): all_tokens = lax.all_gather(recon_error, 'lat', axis=0, tiled=True)  341 us
    all_gather x1, waiting for transfers between devices, local(): shard_rows = lax.all_gather(resid_in, 'lat', axis=0, tiled=True)  306 us
    reduce_scatter x1, waiting for transfers between devices, local(): lax.psum_scatter(projected, 'layer', scatter_dimension=1, tiled=True)  188 us
    all_gather x1, waiting for transfers between devices, local(): full_error = lax.all_gather(all_tokens, 'layer', axis=1, tiled=True)  116 us
  transfers between devices with their start and end apart: 5, of which 5 were waited for; matrix products, arithmetic and copies ran while one was open for 0% of the time, Pallas kernels for 0%

commit v1 on v0

v1 whole, which is shorter than its diff:
```python
import functools

import jax
import jax.numpy as jnp
from jax import lax
from jax.experimental import pallas as pl
from jax.experimental.pallas import tpu as pltpu
from jax.sharding import Mesh
from jax.sharding import PartitionSpec as P

BLK = 128
D = 2304
DC = 768
PAIRS = 9
LAYERS = 8
SEND = 2.0**-5
VMEM = 48 * 1024 * 1024
XY = ("x", "y")
Z = ("zh", "zl")
LAT = ("zl", "x", "y")
LAYER = ("zh", "co")


def enc_kernel(pos, act, order, rows, weight, bias, out):
    lat_index = pos[2]
    g = rows[...]
    tile_row = lax.broadcasted_iota(jnp.int32, (256, BLK), 0) // 8 % 2
    q = lax.broadcasted_iota(jnp.int32, (256, 256), 0)
    c = lax.broadcasted_iota(jnp.int32, (256, 256), 1)
    for h in range(2):
        pre = jnp.dot(g, weight[h], preferred_element_type=jnp.float32)
        pre = pre + bias[h].astype(jnp.float32)
        hits = []
        for tile in range(2):
            hit = jnp.int32(0)
            for j in range(16):
                hit = hit | (act[h, order[tile], j] == lat_index).astype(jnp.int32)
            hits.append(hit)
        on = jnp.where(tile_row == 0, hits[0], hits[1]) > 0
        lat = jnp.where(on, jnp.maximum(pre, 0.0), 0.0).astype(jnp.bfloat16)
        for tt in range(2):
            pick = (q // 2 == c // 2) & (q % 2 == tt) & (c % 2 == h)
            out[h, tt] = jnp.dot(
                pick.astype(jnp.bfloat16), lat, preferred_element_type=jnp.float32
            ).astype(jnp.bfloat16)


def encode(pos, act, order, rows, weight, bias):
    return pl.pallas_call(
        enc_kernel,
        grid_spec=pltpu.PrefetchScalarGridSpec(
            num_scalar_prefetch=3,
            grid=(1,),
            in_specs=[
                pl.BlockSpec((256, D), lambda *_: (0, 0)),
                pl.BlockSpec((2, D, BLK), lambda *_: (0, 0, 0)),
                pl.BlockSpec((2, 1, BLK), lambda *_: (0, 0, 0)),
            ],
            out_specs=pl.BlockSpec((2, 2, 256, BLK), lambda *_: (0, 0, 0, 0)),
        ),
        out_shape=jax.ShapeDtypeStruct((2, 2, 256, BLK), jnp.bfloat16),
        compiler_params=pltpu.CompilerParams(vmem_limit_bytes=VMEM),
        name="encode",
    )(pos, act, order, rows, weight, bias)


def dec_kernel(mine, pos, lat, w00, w01, w10, w11, out):
    owner = pos[0]
    core = pos[1] if mine else 1 - pos[1]
    first = 2 * (2 * pl.program_id(1) + core)

    def half(h, weights):
        cols = []
        for tt in range(2):
            target = first + tt
            valid = (target >= owner) if h == 0 else (target + 1 >= LAYERS - owner)
            cols.append(lat[h, tt] * valid.astype(jnp.bfloat16))
        return jnp.dot(
            jnp.concatenate(cols, axis=1),
            jnp.concatenate([w[0] for w in weights], axis=0),
            preferred_element_type=jnp.float32,
        )

    total = (half(0, (w00, w01)) + half(1, (w10, w11))) * SEND
    out[...] = total.reshape(16, 1, 16, DC)


def decode(mine, pos, lat, weight):
    def slot(h, tt):
        def index(d, zh, pos):
            core = pos[1] if mine else 1 - pos[1]
            target = 2 * (2 * zh + core) + tt
            if h == 0:
                k = jnp.maximum(target - pos[0], 0)
            else:
                k = jnp.maximum(target + 1, LAYERS - pos[0])
            return (k, 0, d)

        return pl.BlockSpec((1, BLK, DC), index)

    piece = pl.BlockSpec((16, 1, 16, DC), lambda d, zh, pos: (0, zh, 0, d))
    return pl.pallas_call(
        functools.partial(dec_kernel, mine),
        grid_spec=pltpu.PrefetchScalarGridSpec(
            num_scalar_prefetch=1,
            grid=(D // DC, 2),
            in_specs=[pl.BlockSpec((2, 2, 256, BLK), lambda *_: (0, 0, 0, 0))]
            + [slot(0, 0), slot(0, 1), slot(1, 0), slot(1, 1)],
            out_specs=piece,
        ),
        out_shape=jax.ShapeDtypeStruct((16, 2, 16, D), jnp.float32),
        compiler_params=pltpu.CompilerParams(vmem_limit_bytes=VMEM),
        name="decode",
    )(pos, lat, weight, weight, weight, weight)


def grad_kernel(pos, lat, own, other, out):
    owner = pos[0]
    k = pl.program_id(1)
    late = (k >= LAYERS - owner).astype(jnp.int32)
    target = jnp.where(late == 1, k - 1, owner + k)
    pair = target // 2
    lhs = lat[late, target % 2]

    def put(err):
        rows = err[:, pl.ds(pair // 2, 1)].reshape(256, DC)
        total = lax.dot_general(
            lhs, rows, (((0,), (0,)), ((), ())), preferred_element_type=jnp.float32
        )
        out[0] = (total * (BLK**-0.5)).astype(jnp.bfloat16)

    is_own = pair % 2 == pos[1]

    @pl.when(is_own)
    def _():
        put(own)

    @pl.when(jnp.logical_not(is_own))
    def _():
        put(other)


def gradients(pos, lat, own, other):
    errs = pl.BlockSpec((16, 2, 16, DC), lambda d, k, pos: (0, 0, 0, d))
    return pl.pallas_call(
        grad_kernel,
        grid_spec=pltpu.PrefetchScalarGridSpec(
            num_scalar_prefetch=1,
            grid=(D // DC, PAIRS),
            in_specs=[pl.BlockSpec((2, 2, 256, BLK), lambda *_: (0, 0, 0, 0)), errs, errs],
            out_specs=pl.BlockSpec((1, BLK, DC), lambda d, k, pos: (k, 0, d)),
        ),
        out_shape=jax.ShapeDtypeStruct((PAIRS, BLK, D), jnp.bfloat16),
        compiler_params=pltpu.CompilerParams(vmem_limit_bytes=VMEM),
        name="gradients",
    )(pos, lat, own, other)


def spread(block, axes, n):
    copies = jnp.broadcast_to(block[None], (n,) + block.shape)
    return lax.all_to_all(copies, axes, 0, 0, tiled=True)


def local(resid_in, enc_weight, enc_bias, dec_weight, dec_bias, act_blocks, tile_order, targets):
    pos = jnp.stack([lax.axis_index(LAYER), lax.axis_index("co"), lax.axis_index(LAT)]).astype(jnp.int32)
    swap = [(0, 1), (1, 0)]
    rows = spread(resid_in.reshape(4, D), "zl", 4).reshape(16, D)
    rows = spread(rows, XY, 16).reshape(256, D)
    lat = encode(pos, act_blocks[:, 0], tile_order, rows, enc_weight[:, 0], enc_bias)
    away = decode(False, pos, lat, dec_weight[0])
    received = lax.ppermute(away.astype(jnp.float16), "co", swap)
    partial = decode(True, pos, lat, dec_weight[0]) + received.astype(jnp.float32)
    parts = lax.all_to_all(partial.astype(jnp.float16).reshape(16, 32, D), XY, 0, 0, tiled=True)
    column = jnp.sum(parts.astype(jnp.float32), axis=0).reshape(8, 4, D)
    column = lax.all_to_all(column, Z, 0, 0, tiled=True)
    recon = jnp.sum(column, axis=0).reshape(2, 2, D) * (1.0 / SEND)
    recon_error = (
        recon + dec_bias.astype(jnp.float32)[None] - targets.astype(jnp.float32)
    ).astype(jnp.bfloat16)
    errs = spread(recon_error.reshape(4, D), Z, 8).reshape(32, D)
    own = spread(errs, XY, 16).reshape(16, 2, 16, D)
    other = lax.ppermute(own, "co", swap)
    return (recon_error, gradients(pos, lat, own, other)[None])


def solution(mesh):
    fine = Mesh(mesh.devices.reshape(2, 2, 4, 4, 4), ("zh", "co", "zl", "x", "y"))
    return jax.shard_map(
        local,
        mesh=fine,
        in_specs=(
            P(LAT, None, LAYER, None),
            P(None, LAYER, None, LAT),
            P(None, LAYER, LAT),
            P(LAYER, None, LAT, None),
            P(LAYER, None),
            P(None, LAYER, None, None),
            P(),
            P(LAT, LAYER, None),
        ),
        out_specs=(P(LAT, LAYER, None), P(LAYER, None, LAT, None)),
        check_vma=False,
    )
```

time: 1670 us -> 171 us (0.10)
  waiting for transfers between devices: 1620 us -> 29.9 us
  blocking collectives: 0 us -> 86.1 us
  Pallas kernels: 0 us -> 27.8 us
  starting transfers between devices: 0.2 us -> 21.3 us
  matrix products: 18.1 us -> 0 us
    all_gather x3 -> x0, waiting for transfers between devices: 763 us -> none  [the longest x1 341 us: local(): all_tokens = lax.all_gather(recon_error, 'lat', axis=0, tiled=True)]
    unnamed x6 -> x0, waiting for transfers between devices: 667 us -> none
    reduce_scatter x1 -> x0, waiting for transfers between devices: 188 us -> none  [local(): lax.psum_scatter(projected, 'layer', scatter_dimension=1, tiled=True)]
    all_to_all x0 -> x4, blocking collectives: none -> 86.1 us  [the longest x3 52.6 us: spread(): return lax.all_to_all(copies, axes, 0, 0, tiled=True)]
    pallas_call x0 -> x4, Pallas kernels: none -> 27.8 us  [the longest x1 13.7 us: gradients(): pl.pallas_call(grad_kernel, grid_spec=pltpu.PrefetchScalarGridSpec(num_sc...]
    all_to_all x0 -> x2, waiting for transfers between devices: none -> 25.7 us  [the longest x1 15.8 us: spread(): return lax.all_to_all(copies, axes, 0, 0, tiled=True)]
    dot_general x3 -> x0, matrix products: 18.1 us -> none  [the longest x1 8.17 us: local(): jnp.einsum('rkf,kfd->rkd', pick_latents(latents), dec_weight[0], preferre...]
  transfers between devices with their start and end apart: 5 -> 4, of which waited for: 5 -> 3; matrix products, arithmetic and copies ran while one was open for 0% -> 0% of each run, Pallas kernels for 0% -> 4%
where the time goes in v1:
time: 171 us
  blocking collectives  86.1 us (50%)
  waiting for transfers between devices  29.9 us (17%)
  Pallas kernels  27.8 us (16%)
  starting transfers between devices  21.3 us (12%)
  local copies, waits for them, and re-layouts  3.15 us (2%)
    all_to_all x3, blocking collectives, spread(): return lax.all_to_all(copies, axes, 0, 0, tiled=True)  52.6 us
    all_to_all x1, blocking collectives, local(): lax.all_to_all(partial.astype(jnp.float16).reshape(16, 32, D), XY, 0, 0,...  33.5 us
    all_to_all x1, waiting for transfers between devices, spread(): return lax.all_to_all(copies, axes, 0, 0, tiled=True)  15.8 us
    pallas_call x1, Pallas kernels, gradients(): pl.pallas_call(grad_kernel, grid_spec=pltpu.PrefetchScalarGridSpec(num_sc...  13.7 us
    pallas_call x2, Pallas kernels, decode(): pl.pallas_call(functools.partial(dec_kernel, mine), grid_spec=pltpu.Prefe...  12.2 us
    all_to_all x1, waiting for transfers between devices, local(): column = lax.all_to_all(column, Z, 0, 0, tiled=True)  9.99 us
    all_to_all x1, starting transfers between devices, spread(): return lax.all_to_all(copies, axes, 0, 0, tiled=True)  6.75 us
    all_to_all x1, starting transfers between devices, local(): column = lax.all_to_all(column, Z, 0, 0, tiled=True)  5.49 us
  transfers between devices with their start and end apart: 4, of which 3 were waited for; matrix products, arithmetic and copies ran while one was open for 0% of the time, Pallas kernels for 4%

profile of v1, /device:TPU:1, one launch (start us, length us, event | category | flops | bytes accessed | tf_op | source)
XLA Modules:
  0.0 170.6 jit_solution(6452016260717712566)
XLA Ops:
  0.7 0.8 broadcast_in_dim.32
  1.5 10.9 %all_to_all.30 = bf16[4,4,2304]{2,1,0:T(4,128)(2,1)S(1)} all-to-all(bf16[4,4,2304]{2,1,0:T(4,128)(2,1)S(1)} %broadcast_in_dim.33), channel_id=1, replica_groups=mesh['zh'=2,'co'=2,'zl'=4,'x'=4,'y'=4] {'zl'}, dimensions={0} | all-to-all | bytes 147456 | tf_op jit(solution)/shard_map/all_to_all | solution.py:161
  12.4 1.1 broadcast_in_dim.35
  13.5 6.8 %all-to-all-start.1 = ((bf16[16,16,2304]{2,1,0:T(8,128)(2,1)}), bf16[16,16,2304]{2,1,0:T(8,128)(2,1)S(1)}, u32[]{:S(2)}, u32[]{:S(2)}) async-start(bf16[16,16,2304]{2,1,0:T(8,128)(2,1)} %broadcast_in_dim.35), calls=%async_computation.1 | async-start | bytes 2359296 | tf_op jit(solution)/shard_map/all_to_all | solution.py:161
  20.3 0.1 pad_add_fusion.pos
  20.4 15.8 %all-to-all-done.1 = bf16[16,16,2304]{2,1,0:T(8,128)(2,1)S(1)} async-done(((bf16[16,16,2304]{2,1,0:T(8,128)(2,1)}), bf16[16,16,2304]{2,1,0:T(8,128)(2,1)S(1)}, u32[]{:S(2)}, u32[]{:S(2)}) %all-to-all-start.1) | async-done | bytes 1179680 | tf_op jit(solution)/shard_map/all_to_all | solution.py:161
  36.2 1.8 %encode.1.lat = bf16[2,2,256,128]{3,2,1,0:T(8,128)(2,1)S(1)} custom-call(s32[3]{0:T(128)S(1)} %pad_add_fusion.pos, s32[2,2,16]{2,1,0:T(2,128)S(1)} %bitcast.16, s32[2]{0:T(128)S(1)} %copy-done.2, bf16[256,2304]{1,0:T(8,128)(2,1)S(1)} %bitcast.14, bf16[2,2304,128]{2,1,0:T(8,128)(2,1)S(1)} %bitcast.15, bf16[2,1,128]{2,1,0:T(2,128)(2,1)S(1)} %copy.12.bias), custom_call_target="tpu_custom_call" | custom-call | tf_op jit(solution)/shard_map/encode/pallas_call | solution.py:49
  38.0 6.1 %decode.3 = f32[16,2,16,2304]{3,2,1,0:T(8,128)S(1)} custom-call(s32[3]{0:T(128)S(1)} %pad_add_fusion.pos, bf16[2,2,256,128]{3,2,1,0:T(8,128)(2,1)S(1)} %encode.1.lat, bf16[9,128,2304]{2,1,0:T(8,128)(2,1)} %bitcast.17, bf16[9,128,2304]{2,1,0:T(8,128)(2,1)} %bitcast.18, bf16[9,128,2304]{2,1,0:T(8,128)(2,1)} %bitcast.19, bf16[9,128,2304]{2,1,0:T(8,128)(2,1)} %bitcast.20), custom_call_target="tpu_custom_call" | custom-call | tf_op jit(solution)/shard_map/decode/pallas_call | solution.py:102
  44.1 0.3 convert_element_type.21
  44.5 3.7 %collective-permute-start = (f16[16,2,16,2304]{3,2,1,0:T(8,128)(2,1)S(1)}, f16[16,2,16,2304]{3,2,1,0:T(8,128)(2,1)S(1)}, u32[]{:S(2)}, u32[]{:S(2)}) collective-permute-start(f16[16,2,16,2304]{3,2,1,0:T(8,128)(2,1)S(1)} %convert_element_type.21), channel_id=1, source_target_pairs={{0,64},{64,0},{1,65},{65,1},{2,66},{66,2},{3,67},{67,3},{4,68},{68... | collective-permute-start | bytes 7077896 | tf_op jit(solution)/shard_map/ppermute | solution.py:171
  48.2 6.1 %decode.2 = f32[16,2,16,2304]{3,2,1,0:T(8,128)S(1)} custom-call(s32[3]{0:T(128)S(1)} %pad_add_fusion.pos, bf16[2,2,256,128]{3,2,1,0:T(8,128)(2,1)S(1)} %encode.1.lat, bf16[9,128,2304]{2,1,0:T(8,128)(2,1)} %bitcast.21, bf16[9,128,2304]{2,1,0:T(8,128)(2,1)} %bitcast.22, bf16[9,128,2304]{2,1,0:T(8,128)(2,1)} %bitcast.23, bf16[9,128,2304]{2,1,0:T(8,128)(2,1)} %bitcast.24), custom_call_target="tpu_custom_call" | custom-call | tf_op jit(solution)/shard_map/decode/pallas_call | solution.py:102
  54.3 0.7 add_convert_fusion
  55.0 33.5 %all_to_all.31 = f16[16,32,2304]{2,1,0:T(8,128)(2,1)S(1)} all-to-all(f16[16,32,2304]{2,1,0:T(8,128)(2,1)S(1)} %bitcast.25), channel_id=1, replica_groups=mesh['zh'=2,'co'=2,'zl'=4,'x'=4,'y'=4] {'x','y'}, dimensions={0} | all-to-all | bytes 4718592 | tf_op jit(solution)/shard_map/all_to_all | solution.py:173
  88.5 0.3 convert_reduce_fusion
  88.8 0.8 reshape.26
  89.6 5.5 %all-to-all-start.3 = ((f32[8,4,2304]{2,1,0:T(4,128)}), f32[8,4,2304]{2,1,0:T(4,128)S(1)}, u32[]{:S(2)}, u32[]{:S(2)}) async-start(f32[8,4,2304]{2,1,0:T(4,128)} %reshape.26), calls=%async_computation.3 | async-start | bytes 589824 | tf_op jit(solution)/shard_map/all_to_all | solution.py:175
  95.1 10.0 %all-to-all-done.3 = f32[8,4,2304]{2,1,0:T(4,128)S(1)} async-done(((f32[8,4,2304]{2,1,0:T(4,128)}), f32[8,4,2304]{2,1,0:T(4,128)S(1)}, u32[]{:S(2)}, u32[]{:S(2)}) %all-to-all-start.3) | async-done | bytes 294944 | tf_op jit(solution)/shard_map/all_to_all | solution.py:175
  105.1 0.1 reduce_sum.19
  105.4 11.2 %all_to_all.32 = bf16[8,4,2304]{2,1,0:T(4,128)(2,1)S(1)} all-to-all(bf16[8,4,2304]{2,1,0:T(4,128)(2,1)S(1)} %broadcast_in_dim.37), channel_id=1, replica_groups=mesh['zh'=2,'co'=2,'zl'=4,'x'=4,'y'=4] {'zh','zl'}, dimensions={0} | all-to-all | bytes 294912 | tf_op jit(solution)/shard_map/all_to_all | solution.py:161
  116.6 0.2 broadcast_in_dim.39
  116.9 30.5 %all_to_all.33 = bf16[16,32,2304]{2,1,0:T(8,128)(2,1)S(1)} all-to-all(bf16[16,32,2304]{2,1,0:T(8,128)(2,1)S(1)} %broadcast_in_dim.39), channel_id=1, replica_groups=mesh['zh'=2,'co'=2,'zl'=4,'x'=4,'y'=4] {'x','y'}, dimensions={0} | all-to-all | bytes 4718592 | tf_op jit(solution)/shard_map/all_to_all | solution.py:161
  147.4 5.4 %collective-permute-start.1 = (bf16[16,2,16,2304]{3,2,1,0:T(8,128)(2,1)S(1)}, bf16[16,2,16,2304]{3,2,1,0:T(8,128)(2,1)S(1)}, u32[]{:S(2)}, u32[]{:S(2)}) collective-permute-start(bf16[16,2,16,2304]{3,2,1,0:T(8,128)(2,1)S(1)} %bitcast.12), channel_id=1, source_target_pairs={{0,64},{64,0},{1,65},{65,1},{2,66},{66,2},{3,67},{67,3},{4,68},{68... | collective-permute-start | bytes 7077896 | tf_op jit(solution)/shard_map/ppermute | solution.py:182
  152.7 4.2 %collective-permute-done.1.other = bf16[16,2,16,2304]{3,2,1,0:T(8,128)(2,1)S(1)} collective-permute-done((bf16[16,2,16,2304]{3,2,1,0:T(8,128)(2,1)S(1)}, bf16[16,2,16,2304]{3,2,1,0:T(8,128)(2,1)S(1)}, u32[]{:S(2)}, u32[]{:S(2)}) %collective-permute-start.1) | collective-permute-done | bytes 2359328 | tf_op jit(solution)/shard_map/ppermute | solution.py:182
  156.9 13.7 %gradients.1 = bf16[9,128,2304]{2,1,0:T(8,128)(2,1)} custom-call(s32[3]{0:T(128)S(1)} %pad_add_fusion.pos, bf16[2,2,256,128]{3,2,1,0:T(8,128)(2,1)S(1)} %encode.1.lat, bf16[16,2,16,2304]{3,2,1,0:T(8,128)(2,1)S(1)} %bitcast.13, bf16[16,2,16,2304]{3,2,1,0:T(8,128)(2,1)S(1)} %collective-permute-done.1.other), custom_call_target="tpu_custom_call" | custom-call | tf_op jit(solution)/shard_map/gradients/pallas_call | solution.py:145
  (25 shorter events, 0.3 us)
Async XLA Ops:
  0.6 19.7 %copy-start.6 = (bf16[2,1,128]{2,0,1:T(2,128)(2,1)S(1)}, bf16[2,1,128]{2,0,1:T(2,128)(2,1)}, u32[]{:S(2)}) copy-start(bf16[2,1,128]{2,0,1:T(2,128)(2,1)} %param.10) | copy-start | bytes 1540
  0.6 35.5 %copy-start.2 = (s32[2]{0:T(128)S(1)}, s32[2]{0:T(128)}, u32[]{:S(2)}) copy-start(s32[2]{0:T(128)} %order.1) | copy-start | bytes 28
  0.7 35.5 %copy-start.1 = (s32[2,1,2,16]{3,2,1,0:T(2,128)S(1)}, s32[2,1,2,16]{3,2,1,0:T(2,128)}, u32[]{:S(2)}) copy-start(s32[2,1,2,16]{3,2,1,0:T(2,128)} %param.13) | copy-start | bytes 772
  0.7 35.5 %copy-start = (bf16[2,1,2304,128]{3,2,1,0:T(8,128)(2,1)S(1)}, bf16[2,1,2304,128]{3,2,1,0:T(8,128)(2,1)}, u32[]{:S(2)}) copy-start(bf16[2,1,2304,128]{3,2,1,0:T(8,128)(2,1)} %param.9) | copy-start | bytes 3538948
  13.5 22.6 %all-to-all-start.1 = ((bf16[16,16,2304]{2,1,0:T(8,128)(2,1)}), bf16[16,16,2304]{2,1,0:T(8,128)(2,1)S(1)}, u32[]{:S(2)}, u32[]{:S(2)}) async-start(bf16[16,16,2304]{2,1,0:T(8,128)(2,1)} %broadcast_in_dim.35), calls=%async_computation.1 | async-start | bytes 2359296 | tf_op jit(solution)/shard_map/all_to_all | solution.py:161
  44.5 9.8 %collective-permute-start = (f16[16,2,16,2304]{3,2,1,0:T(8,128)(2,1)S(1)}, f16[16,2,16,2304]{3,2,1,0:T(8,128)(2,1)S(1)}, u32[]{:S(2)}, u32[]{:S(2)}) collective-permute-start(f16[16,2,16,2304]{3,2,1,0:T(8,128)(2,1)S(1)} %convert_element_type.21), channel_id=1, source_target_pairs={{0,64},{64,0},{1,65},{65,1},{2,66},{66,2},{3,67},{67,3},{4,68},{68... | collective-permute-start | bytes 7077896 | tf_op jit(solution)/shard_map/ppermute | solution.py:171
  88.5 6.6 %copy-start.5 = (bf16[2,2304]{1,0:T(2,128)(2,1)S(1)}, bf16[2,2304]{1,0:T(2,128)(2,1)}, u32[]{:S(2)}) copy-start(bf16[2,2304]{1,0:T(2,128)(2,1)} %param.12) | copy-start | bytes 27652
  88.5 16.7 %copy-start.4 = (bf16[2,2,2304]{2,1,0:T(2,128)(2,1)S(1)}, bf16[2,2,2304]{2,1,0:T(2,128)(2,1)}, u32[]{:S(2)}) copy-start(bf16[2,2,2304]{2,1,0:T(2,128)(2,1)} %param.15) | copy-start | bytes 55300
  89.6 15.5 %all-to-all-start.3 = ((f32[8,4,2304]{2,1,0:T(4,128)}), f32[8,4,2304]{2,1,0:T(4,128)S(1)}, u32[]{:S(2)}, u32[]{:S(2)}) async-start(f32[8,4,2304]{2,1,0:T(4,128)} %reshape.26), calls=%async_computation.3 | async-start | bytes 589824 | tf_op jit(solution)/shard_map/all_to_all | solution.py:175
  105.3 42.1 %copy-start.3 = (bf16[2,2,2304]{2,1,0:T(2,128)(2,1)}, bf16[2,2,2304]{2,1,0:T(2,128)(2,1)S(1)}, u32[]{:S(2)}) copy-start(bf16[2,2,2304]{2,1,0:T(2,128)(2,1)S(1)} %subtract_convert_fusion) | copy-start | bytes 55300
  147.4 9.5 %collective-permute-start.1 = (bf16[16,2,16,2304]{3,2,1,0:T(8,128)(2,1)S(1)}, bf16[16,2,16,2304]{3,2,1,0:T(8,128)(2,1)S(1)}, u32[]{:S(2)}, u32[]{:S(2)}) collective-permute-start(bf16[16,2,16,2304]{3,2,1,0:T(8,128)(2,1)S(1)} %bitcast.12), channel_id=1, source_target_pairs={{0,64},{64,0},{1,65},{65,1},{2,66},{66,2},{3,67},{67,3},{4,68},{68... | collective-permute-start | bytes 7077896 | tf_op jit(solution)/shard_map/ppermute | solution.py:182

commit v2 on v1

v2 whole, which is shorter than its diff:
```python
import functools

import jax
import jax.numpy as jnp
import numpy as np
from jax import lax
from jax.experimental import pallas as pl
from jax.experimental.pallas import tpu as pltpu
from jax.sharding import Mesh
from jax.sharding import PartitionSpec as P

BLK = 128
D = 2304
DC = 768
PAIRS = 9
LAYERS = 8
SEND = 2.0**-5
VMEM = 24 * 1024 * 1024
XY = ("x", "y")
Z = ("zh", "zl")
LAT = ("zl", "x", "y")
LAYER = ("zh", "co")


def enc_kernel(pos, act, order, rows, weight, bias, out):
    lat_index = pos[2]
    g = rows[...]
    tile_row = lax.broadcasted_iota(jnp.int32, (256, BLK), 0) // 8 % 2
    q = lax.broadcasted_iota(jnp.int32, (256, 256), 0)
    c = lax.broadcasted_iota(jnp.int32, (256, 256), 1)
    for h in range(2):
        pre = jnp.dot(g, weight[h], preferred_element_type=jnp.float32)
        pre = pre + bias[h].astype(jnp.float32)
        hits = []
        for tile in range(2):
            hit = jnp.int32(0)
            for j in range(16):
                hit = hit | (act[h, order[tile], j] == lat_index).astype(jnp.int32)
            hits.append(hit)
        on = jnp.where(tile_row == 0, hits[0], hits[1]) > 0
        lat = jnp.where(on, jnp.maximum(pre, 0.0), 0.0).astype(jnp.bfloat16)
        for tt in range(2):
            pick = (q // 2 == c // 2) & (q % 2 == tt) & (c % 2 == h)
            out[h, tt] = jnp.dot(
                pick.astype(jnp.bfloat16), lat, preferred_element_type=jnp.float32
            ).astype(jnp.bfloat16)


def encode(pos, act, order, rows, weight, bias):
    return pl.pallas_call(
        enc_kernel,
        grid_spec=pltpu.PrefetchScalarGridSpec(
            num_scalar_prefetch=3,
            grid=(1,),
            in_specs=[
                pl.BlockSpec((256, D), lambda *_: (0, 0)),
                pl.BlockSpec((2, D, BLK), lambda *_: (0, 0, 0)),
                pl.BlockSpec((2, 1, BLK), lambda *_: (0, 0, 0)),
            ],
            out_specs=pl.BlockSpec((2, 2, 256, BLK), lambda *_: (0, 0, 0, 0)),
        ),
        out_shape=jax.ShapeDtypeStruct((2, 2, 256, BLK), jnp.bfloat16),
        compiler_params=pltpu.CompilerParams(vmem_limit_bytes=VMEM),
        name="encode",
    )(pos, act, order, rows, weight, bias)


def dec_kernel(mine, pos, lat, weight, out):
    owner = pos[0]
    core = pos[1] if mine else 1 - pos[1]
    for zh in range(2):
        first = 2 * (2 * zh + core)
        left, slots = [], []
        for h in range(2):
            cols = []
            for tt in range(2):
                target = first + tt
                if h == 0:
                    valid = target >= owner
                    slots.append(jnp.maximum(target - owner, 0))
                else:
                    valid = target + 1 >= LAYERS - owner
                    slots.append(jnp.maximum(target + 1, LAYERS - owner))
                cols.append(lat[h, tt] * valid.astype(jnp.bfloat16))
            left.append(jnp.concatenate(cols, axis=1))
        for d in range(0, D, DC):
            total = jnp.zeros((256, DC), jnp.float32)
            for h in range(2):
                right = [weight[slots[2 * h + tt], :, d : d + DC] for tt in range(2)]
                total += jnp.dot(
                    left[h], jnp.concatenate(right, axis=0), preferred_element_type=jnp.float32
                )
            out[:, zh, :, d : d + DC] = (total * SEND).reshape(16, 16, DC)


def decode(mine, pos, lat, weight):
    return pl.pallas_call(
        functools.partial(dec_kernel, mine),
        in_specs=[
            pl.BlockSpec(memory_space=pltpu.SMEM),
            pl.BlockSpec(memory_space=pltpu.VMEM),
            pl.BlockSpec(memory_space=pltpu.VMEM),
        ],
        out_specs=pl.BlockSpec(memory_space=pltpu.VMEM),
        out_shape=jax.ShapeDtypeStruct((16, 2, 16, D), jnp.float32),
        cost_estimate=pl.CostEstimate(
            flops=4 * 2 * 256 * 256 * D, bytes_accessed=10 * 2**20, transcendentals=0
        ),
        compiler_params=pltpu.CompilerParams(vmem_limit_bytes=VMEM),
        name="decode",
    )(pos, lat, weight)


def grad_kernel(which, pos, table, lat, errs, *rest):
    out = rest[-1]
    entry = ((pos[0] * 2 + which) * 6 + pl.program_id(0)) * 4
    rows = errs[:, pl.ds(table[entry + 2], 1)].reshape(256, D)
    total = lax.dot_general(
        lat[table[entry + 1], table[entry + 3]],
        rows,
        (((0,), (0,)), ((), ())),
        preferred_element_type=jnp.float32,
    )
    out[0] = (total * (BLK**-0.5)).astype(jnp.bfloat16)


def gradients(which, pos, lat, errs, *before):
    def slot(j, pos, table):
        return (table[((pos[0] * 2 + which) * 6 + j) * 4], 0, 0)

    return pl.pallas_call(
        functools.partial(grad_kernel, which),
        grid_spec=pltpu.PrefetchScalarGridSpec(
            num_scalar_prefetch=2,
            grid=(6,),
            in_specs=[
                pl.BlockSpec(memory_space=pltpu.VMEM),
                pl.BlockSpec(memory_space=pltpu.VMEM),
            ]
            + [pl.BlockSpec(memory_space=pl.ANY)] * len(before),
            out_specs=pl.BlockSpec((1, BLK, D), slot),
        ),
        out_shape=jax.ShapeDtypeStruct((PAIRS, BLK, D), jnp.bfloat16),
        input_output_aliases={4: 0} if before else {},
        cost_estimate=pl.CostEstimate(
            flops=6 * 2 * BLK * 256 * D, bytes_accessed=10 * 2**20, transcendentals=0
        ),
        compiler_params=pltpu.CompilerParams(vmem_limit_bytes=VMEM),
        name="gradients",
    )(pos, jnp.asarray(slot_table()), lat, errs, *before)


def slot_table():
    table = np.zeros((4, 2, 6, 4), np.int32)
    for owner in range(4):
        for which in range(2):
            entries = []
            for k in range(PAIRS):
                late = int(k >= LAYERS - owner)
                target = k - 1 if late else owner + k
                if (target // 2 % 2 == owner % 2) == (which == 0):
                    entries.append((k, late, target // 4, target % 2))
            table[owner, which] = (entries + [entries[-1]] * 6)[:6]
    return table.reshape(-1)


def spread(block, axes, n):
    copies = jnp.broadcast_to(block[None], (n,) + block.shape)
    return lax.all_to_all(copies, axes, 0, 0, tiled=True)


def local(resid_in, enc_weight, enc_bias, dec_weight, dec_bias, act_blocks, tile_order, targets):
    pos = jnp.stack([lax.axis_index(LAYER), lax.axis_index("co"), lax.axis_index(LAT)]).astype(jnp.int32)
    swap = [(0, 1), (1, 0)]
    rows = spread(resid_in.reshape(4, D), "zl", 4).reshape(16, D)
    rows = spread(rows, XY, 16).reshape(256, D)
    lat = encode(pos, act_blocks[:, 0], tile_order, rows, enc_weight[:, 0], enc_bias)
    away = decode(False, pos, lat, dec_weight[0])
    received = lax.ppermute(away.astype(jnp.float16), "co", swap)
    partial = decode(True, pos, lat, dec_weight[0]) + received.astype(jnp.float32)
    parts = lax.all_to_all(partial.astype(jnp.float16).reshape(16, 32, D), XY, 0, 0, tiled=True)
    column = jnp.sum(parts.astype(jnp.float32), axis=0).astype(jnp.float16).reshape(8, 4, D)
    column = lax.all_to_all(column, Z, 0, 0, tiled=True).astype(jnp.float32)
    recon = jnp.sum(column, axis=0).reshape(2, 2, D) * (1.0 / SEND)
    recon_error = (
        recon + dec_bias.astype(jnp.float32)[None] - targets.astype(jnp.float32)
    ).astype(jnp.bfloat16)
    errs = spread(recon_error.reshape(4, D), Z, 8).reshape(32, D)
    own = spread(errs, XY, 16).reshape(16, 2, 16, D)
    other = lax.ppermute(own, "co", swap)
    dec_grad = gradients(0, pos, lat, own)
    dec_grad = gradients(1, pos, lat, other, dec_grad)
    return (recon_error, dec_grad[None])


def solution(mesh):
    fine = Mesh(mesh.devices.reshape(2, 2, 4, 4, 4), ("zh", "co", "zl", "x", "y"))
    return jax.shard_map(
        local,
        mesh=fine,
        in_specs=(
            P(LAT, None, LAYER, None),
            P(None, LAYER, None, LAT),
            P(None, LAYER, LAT),
            P(LAYER, None, LAT, None),
            P(LAYER, None),
            P(None, LAYER, None, None),
            P(),
            P(LAT, LAYER, None),
        ),
        out_specs=(P(LAT, LAYER, None), P(LAYER, None, LAT, None)),
        check_vma=False,
    )
```

time: 171 us -> 156 us (0.912)
  Pallas kernels: 27.8 us -> 14.2 us
  waiting for transfers between devices: 29.9 us -> 26.1 us
  local copies, waits for them, and re-layouts: 3.15 us -> 6.77 us
  blocking collectives: 86.1 us -> 84.1 us
    pallas_call x3 -> x4, Pallas kernels: 26 us -> 12.4 us  [the longest x2 8.49 us: gradients(): pl.pallas_call(functools.partial(grad_kernel, which), grid_spec=pltpu.Pre...]
    ppermute x1, waiting for transfers between devices: 4.16 us -> 0.01 us  [local(): other = lax.ppermute(own, 'co', swap)]
    unnamed x15 -> x23, local copies, waits for them, and re-layouts: 0.04 us -> 3.82 us
    ppermute x1, waiting for transfers between devices: 0.01 us -> 2.19 us  [local(): received = lax.ppermute(away.astype(jnp.float16), 'co', swap)]
    all_to_all x1, waiting for transfers between devices: 9.99 us -> 8.18 us  [local(): column = lax.all_to_all(column, Z, 0, 0, tiled=True).astype(jnp.float32)]
    all_to_all x3, blocking collectives: 52.6 us -> 50.8 us  [spread(): return lax.all_to_all(copies, axes, 0, 0, tiled=True)]
where the time goes in v2:
time: 156 us
  blocking collectives  84.1 us (54%)
  waiting for transfers between devices  26.1 us (17%)
  starting transfers between devices  21.9 us (14%)
  Pallas kernels  14.2 us (9%)
  local copies, waits for them, and re-layouts  6.77 us (4%)
  other arithmetic  1.6 us (1%)
    all_to_all x3, blocking collectives, spread(): return lax.all_to_all(copies, axes, 0, 0, tiled=True)  50.8 us
    all_to_all x1, blocking collectives, local(): lax.all_to_all(partial.astype(jnp.float16).reshape(16, 32, D), XY, 0, 0,...  33.3 us
    all_to_all x1, waiting for transfers between devices, spread(): return lax.all_to_all(copies, axes, 0, 0, tiled=True)  15.8 us
    pallas_call x2, Pallas kernels, gradients(): pl.pallas_call(functools.partial(grad_kernel, which), grid_spec=pltpu.Pre...  8.49 us
    all_to_all x1, waiting for transfers between devices, local(): column = lax.all_to_all(column, Z, 0, 0, tiled=True).astype(jnp.float32)  8.18 us
    all_to_all x1, starting transfers between devices, spread(): return lax.all_to_all(copies, axes, 0, 0, tiled=True)  6.89 us
    ppermute x1, starting transfers between devices, local(): other = lax.ppermute(own, 'co', swap)  5.81 us
    all_to_all x1, starting transfers between devices, local(): column = lax.all_to_all(column, Z, 0, 0, tiled=True).astype(jnp.float32)  5.49 us
  transfers between devices with their start and end apart: 4, of which 3 were waited for; matrix products, arithmetic and copies ran while one was open for 0% of the time, Pallas kernels for 4%

profile of v2, /device:TPU:1, one launch (start us, length us, event | category | flops | bytes accessed | tf_op | source)
XLA Modules:
  0.0 155.6 jit_solution(17815709321123712801)
XLA Ops:
  0.7 0.8 broadcast_in_dim.32
  1.4 10.9 %all_to_all.30 = bf16[4,4,2304]{2,1,0:T(4,128)(2,1)S(1)} all-to-all(bf16[4,4,2304]{2,1,0:T(4,128)(2,1)S(1)} %broadcast_in_dim.33), channel_id=1, replica_groups=mesh['zh'=2,'co'=2,'zl'=4,'x'=4,'y'=4] {'zl'}, dimensions={0} | all-to-all | bytes 147456 | tf_op jit(solution)/shard_map/all_to_all | solution.py:169
  12.3 1.1 broadcast_in_dim.35
  13.4 6.9 %all-to-all-start.1 = ((bf16[16,16,2304]{2,1,0:T(8,128)(2,1)}), bf16[16,16,2304]{2,1,0:T(8,128)(2,1)S(1)}, u32[]{:S(2)}, u32[]{:S(2)}) async-start(bf16[16,16,2304]{2,1,0:T(8,128)(2,1)} %broadcast_in_dim.35), calls=%async_computation.1 | async-start | bytes 2359296 | tf_op jit(solution)/shard_map/all_to_all | solution.py:169
  20.4 15.8 %all-to-all-done.1 = bf16[16,16,2304]{2,1,0:T(8,128)(2,1)S(1)} async-done(((bf16[16,16,2304]{2,1,0:T(8,128)(2,1)}), bf16[16,16,2304]{2,1,0:T(8,128)(2,1)S(1)}, u32[]{:S(2)}, u32[]{:S(2)}) %all-to-all-start.1) | async-done | bytes 1179680 | tf_op jit(solution)/shard_map/all_to_all | solution.py:169
  36.2 1.3 copy-done.1
  37.5 1.8 %encode.1.lat = bf16[2,2,256,128]{3,2,1,0:T(8,128)(2,1)S(1)} custom-call(s32[3]{0:T(128)S(1)} %pad_add_fusion.pos, s32[2,2,16]{2,1,0:T(2,128)S(1)} %bitcast.20, s32[2]{0:T(128)S(1)} %copy-done.4, bf16[256,2304]{1,0:T(8,128)(2,1)S(1)} %bitcast.18, bf16[2,2304,128]{2,1,0:T(8,128)(2,1)S(1)} %bitcast.19, bf16[2,1,128]{2,1,0:T(2,128)(2,1)S(1)} %copy.19.bias), custom_call_target="tpu_custom_call" | custom-call | tf_op jit(solution)/shard_map/encode/pallas_call | solution.py:50
  39.3 2.5 %copy-done = bf16[1,9,128,2304]{3,2,1,0:T(8,128)(2,1)S(1)} copy-done((bf16[1,9,128,2304]{3,2,1,0:T(8,128)(2,1)S(1)}, bf16[1,9,128,2304]{3,2,1,0:T(8,128)(2,1)}, u32[]{:S(2)}) %copy-start) | copy-done | bytes 5308440
  41.8 1.9 %decode.3 = f32[16,2,16,2304]{3,2,1,0:T(8,128)S(1)} custom-call(s32[3]{0:T(128)S(1)} %pad_add_fusion.pos, bf16[2,2,256,128]{3,2,1,0:T(8,128)(2,1)S(1)} %encode.1.lat, bf16[9,128,2304]{2,1,0:T(8,128)(2,1)S(1)} %bitcast.12), custom_call_target="tpu_custom_call" | custom-call | flops 1207959552 | bytes 10485760 | tf_op jit(solution)/shard_map/decode/pallas_call | solution.py:97
  43.8 0.3 convert_element_type.31
  44.1 3.7 %collective-permute-start = (f16[16,2,16,2304]{3,2,1,0:T(8,128)(2,1)S(1)}, f16[16,2,16,2304]{3,2,1,0:T(8,128)(2,1)S(1)}, u32[]{:S(2)}, u32[]{:S(2)}) collective-permute-start(f16[16,2,16,2304]{3,2,1,0:T(8,128)(2,1)S(1)} %convert_element_type.31), channel_id=1, source_target_pairs={{0,64},{64,0},{1,65},{65,1},{2,66},{66,2},{3,67},{67,3},{4,68},{68... | collective-permute-start | bytes 7077896 | tf_op jit(solution)/shard_map/ppermute | solution.py:179
  47.8 2.0 %decode.2 = f32[16,2,16,2304]{3,2,1,0:T(8,128)S(1)} custom-call(s32[3]{0:T(128)S(1)} %pad_add_fusion.pos, bf16[2,2,256,128]{3,2,1,0:T(8,128)(2,1)S(1)} %encode.1.lat, bf16[9,128,2304]{2,1,0:T(8,128)(2,1)S(1)} %bitcast.15), custom_call_target="tpu_custom_call" | custom-call | flops 1207959552 | bytes 10485760 | tf_op jit(solution)/shard_map/decode/pallas_call | solution.py:97
  49.8 2.2 %collective-permute-done = f16[16,2,16,2304]{3,2,1,0:T(8,128)(2,1)S(1)} collective-permute-done((f16[16,2,16,2304]{3,2,1,0:T(8,128)(2,1)S(1)}, f16[16,2,16,2304]{3,2,1,0:T(8,128)(2,1)S(1)}, u32[]{:S(2)}, u32[]{:S(2)}) %collective-permute-start) | collective-permute-done | bytes 2359328 | tf_op jit(solution)/shard_map/ppermute | solution.py:179
  52.0 0.7 add_convert_fusion
  52.7 33.3 %all_to_all.31 = f16[16,32,2304]{2,1,0:T(8,128)(2,1)S(1)} all-to-all(f16[16,32,2304]{2,1,0:T(8,128)(2,1)S(1)} %bitcast.22), channel_id=1, replica_groups=mesh['zh'=2,'co'=2,'zl'=4,'x'=4,'y'=4] {'x','y'}, dimensions={0} | all-to-all | bytes 4718592 | tf_op jit(solution)/shard_map/all_to_all | solution.py:181
  86.0 0.3 convert_reduce_fusion
  86.4 0.7 convert_element_type.36
  87.1 5.5 %all-to-all-start.3 = ((f16[8,4,2304]{2,1,0:T(4,128)(2,1)}), f16[8,4,2304]{2,1,0:T(4,128)(2,1)S(1)}, u32[]{:S(2)}, u32[]{:S(2)}) async-start(f16[8,4,2304]{2,1,0:T(4,128)(2,1)} %convert_element_type.36), calls=%async_computation.3 | async-start | bytes 294912 | tf_op jit(solution)/shard_map/all_to_all | solution.py:183
  92.6 8.2 %all-to-all-done.3 = f16[8,4,2304]{2,1,0:T(4,128)(2,1)S(1)} async-done(((f16[8,4,2304]{2,1,0:T(4,128)(2,1)}), f16[8,4,2304]{2,1,0:T(4,128)(2,1)S(1)}, u32[]{:S(2)}, u32[]{:S(2)}) %all-to-all-start.3) | async-done | bytes 147488 | tf_op jit(solution)/shard_map/all_to_all | solution.py:183
  101.1 10.6 %all_to_all.32 = bf16[8,4,2304]{2,1,0:T(4,128)(2,1)S(1)} all-to-all(bf16[8,4,2304]{2,1,0:T(4,128)(2,1)S(1)} %broadcast_in_dim.37), channel_id=1, replica_groups=mesh['zh'=2,'co'=2,'zl'=4,'x'=4,'y'=4] {'zh','zl'}, dimensions={0} | all-to-all | bytes 294912 | tf_op jit(solution)/shard_map/all_to_all | solution.py:169
  112.0 29.3 %all_to_all.33 = bf16[16,32,2304]{2,1,0:T(8,128)(2,1)S(1)} all-to-all(bf16[16,32,2304]{2,1,0:T(8,128)(2,1)S(1)} %broadcast_in_dim.39), channel_id=1, replica_groups=mesh['zh'=2,'co'=2,'zl'=4,'x'=4,'y'=4] {'x','y'}, dimensions={0} | all-to-all | bytes 4718592 | tf_op jit(solution)/shard_map/all_to_all | solution.py:169
  141.3 5.8 %collective-permute-start.1 = (bf16[16,2,16,2304]{3,2,1,0:T(8,128)(2,1)S(1)}, bf16[16,2,16,2304]{3,2,1,0:T(8,128)(2,1)S(1)}, u32[]{:S(2)}, u32[]{:S(2)}) collective-permute-start(bf16[16,2,16,2304]{3,2,1,0:T(8,128)(2,1)S(1)} %bitcast.16), channel_id=1, source_target_pairs={{0,64},{64,0},{1,65},{65,1},{2,66},{66,2},{3,67},{67,3},{4,68},{68... | collective-permute-start | bytes 7077896 | tf_op jit(solution)/shard_map/ppermute | solution.py:190
  147.1 4.5 %gradients.2.rest_0_ = bf16[9,128,2304]{2,1,0:T(8,128)(2,1)} custom-call(s32[3]{0:T(128)S(1)} %pad_add_fusion.pos, s32[192]{0:T(256)S(1)} %copy-done.2, bf16[2,2,256,128]{3,2,1,0:T(8,128)(2,1)S(1)} %encode.1.lat, bf16[16,2,16,2304]{3,2,1,0:T(8,128)(2,1)S(1)} %bitcast.17), custom_call_target="tpu_custom_call" | custom-call | flops 905969664 | bytes 10485760 | tf_op jit(solution)/shard_map/gradients/pallas_call | solution.py:131
  151.6 4.0 %gradients.3 = bf16[9,128,2304]{2,1,0:T(8,128)(2,1)} custom-call(s32[3]{0:T(128)S(1)} %pad_add_fusion.pos, s32[192]{0:T(256)S(1)} %copy-done.2, bf16[2,2,256,128]{3,2,1,0:T(8,128)(2,1)S(1)} %encode.1.lat, bf16[16,2,16,2304]{3,2,1,0:T(8,128)(2,1)S(1)} %collective-permute-done.1.errs, ...), custom_call_target="tpu_custom_call", output_to_operand_aliasing={{}: (4, {})} | custom-call | flops 905969664 | bytes 10485760 | tf_op jit(solution)/shard_map/gradients/pallas_call | solution.py:131
  (36 shorter events, 0.7 us)
Async XLA Ops:
  0.6 19.7 %copy-start.8 = (bf16[2,1,128]{2,0,1:T(2,128)(2,1)S(1)}, bf16[2,1,128]{2,0,1:T(2,128)(2,1)}, u32[]{:S(2)}) copy-start(bf16[2,1,128]{2,0,1:T(2,128)(2,1)} %param.12) | copy-start | bytes 1540
  0.6 35.6 %copy-start.4 = (s32[2]{0:T(128)S(1)}, s32[2]{0:T(128)}, u32[]{:S(2)}) copy-start(s32[2]{0:T(128)} %order.1) | copy-start | bytes 28
  0.7 35.6 %copy-start.3 = (s32[2,1,2,16]{3,2,1,0:T(2,128)S(1)}, s32[2,1,2,16]{3,2,1,0:T(2,128)}, u32[]{:S(2)}) copy-start(s32[2,1,2,16]{3,2,1,0:T(2,128)} %param.15) | copy-start | bytes 772
  13.4 34.4 %slice-start = ((s8[5308416]{0:T(1024)(128)(4,1)}), s8[1114112]{0:T(1024)(128)(4,1)S(1)}, s32[]{:S(2)}) async-start(s8[5308416]{0:T(1024)(128)(4,1)} %bitcast.13), calls=%async_computation.6 | async-start | bytes 2228224
  13.4 22.8 %all-to-all-start.1 = ((bf16[16,16,2304]{2,1,0:T(8,128)(2,1)}), bf16[16,16,2304]{2,1,0:T(8,128)(2,1)S(1)}, u32[]{:S(2)}, u32[]{:S(2)}) async-start(bf16[16,16,2304]{2,1,0:T(8,128)(2,1)} %broadcast_in_dim.35), calls=%async_computation.1 | async-start | bytes 2359296 | tf_op jit(solution)/shard_map/all_to_all | solution.py:169
  36.2 1.3 copy-start.1
  39.3 2.5 %copy-start = (bf16[1,9,128,2304]{3,2,1,0:T(8,128)(2,1)S(1)}, bf16[1,9,128,2304]{3,2,1,0:T(8,128)(2,1)}, u32[]{:S(2)}) copy-start(bf16[1,9,128,2304]{3,2,1,0:T(8,128)(2,1)} %param.13) | copy-start | bytes 15925252
  41.8 6.0 %slice-start.1 = ((s8[5308416]{0:T(1024)(128)(4,1)}), s8[4194304]{0:T(1024)(128)(4,1)S(1)}, s32[]{:S(2)}) async-start(s8[5308416]{0:T(1024)(128)(4,1)} %bitcast.13), calls=%async_computation.7 | async-start | bytes 8388608
  44.1 7.8 %collective-permute-start = (f16[16,2,16,2304]{3,2,1,0:T(8,128)(2,1)S(1)}, f16[16,2,16,2304]{3,2,1,0:T(8,128)(2,1)S(1)}, u32[]{:S(2)}, u32[]{:S(2)}) collective-permute-start(f16[16,2,16,2304]{3,2,1,0:T(8,128)(2,1)S(1)} %convert_element_type.31), channel_id=1, source_target_pairs={{0,64},{64,0},{1,65},{65,1},{2,66},{66,2},{3,67},{67,3},{4,68},{68... | collective-permute-start | bytes 7077896 | tf_op jit(solution)/shard_map/ppermute | solution.py:179
  86.0 6.6 %copy-start.7 = (bf16[2,2304]{1,0:T(2,128)(2,1)S(1)}, bf16[2,2304]{1,0:T(2,128)(2,1)}, u32[]{:S(2)}) copy-start(bf16[2,2304]{1,0:T(2,128)(2,1)} %param.14) | copy-start | bytes 27652
  86.0 14.9 %copy-start.6 = (bf16[2,2,2304]{2,1,0:T(2,128)(2,1)S(1)}, bf16[2,2,2304]{2,1,0:T(2,128)(2,1)}, u32[]{:S(2)}) copy-start(bf16[2,2,2304]{2,1,0:T(2,128)(2,1)} %param.17) | copy-start | bytes 55300
  87.1 13.7 %all-to-all-start.3 = ((f16[8,4,2304]{2,1,0:T(4,128)(2,1)}), f16[8,4,2304]{2,1,0:T(4,128)(2,1)S(1)}, u32[]{:S(2)}, u32[]{:S(2)}) async-start(f16[8,4,2304]{2,1,0:T(4,128)(2,1)} %convert_element_type.36), calls=%async_computation.3 | async-start | bytes 294912 | tf_op jit(solution)/shard_map/all_to_all | solution.py:183
  101.0 40.3 %copy-start.5 = (bf16[2,2,2304]{2,1,0:T(2,128)(2,1)}, bf16[2,2,2304]{2,1,0:T(2,128)(2,1)S(1)}, u32[]{:S(2)}) copy-start(bf16[2,2,2304]{2,1,0:T(2,128)(2,1)S(1)} %subtract_convert_fusion) | copy-start | bytes 55300
  111.9 35.2 %copy-start.2 = (s32[192]{0:T(256)S(1)}, s32[192]{0:T(256)}, u32[]{:S(2)}) copy-start(s32[192]{0:T(256)} %constant.33.clone.table) | copy-start | bytes 2308
  141.3 10.3 %collective-permute-start.1 = (bf16[16,2,16,2304]{3,2,1,0:T(8,128)(2,1)S(1)}, bf16[16,2,16,2304]{3,2,1,0:T(8,128)(2,1)S(1)}, u32[]{:S(2)}, u32[]{:S(2)}) collective-permute-start(bf16[16,2,16,2304]{3,2,1,0:T(8,128)(2,1)S(1)} %bitcast.16), channel_id=1, source_target_pairs={{0,64},{64,0},{1,65},{65,1},{2,66},{66,2},{3,67},{67,3},{4,68},{68... | collective-permute-start | bytes 7077896 | tf_op jit(solution)/shard_map/ppermute | solution.py:190

commit v3 on v2

v3 whole, which is shorter than its diff:
```python
import functools

import jax
import jax.numpy as jnp
from jax import lax
from jax.experimental import pallas as pl
from jax.experimental.pallas import tpu as pltpu
from jax.sharding import Mesh
from jax.sharding import PartitionSpec as P

BLK = 128
D = 2304
DC = 768
PAIRS = 9
LAYERS = 8
SEND = 2.0**-5
VMEM = 24 * 1024 * 1024
LARGE = 44 * 1024 * 1024
Z = ("zh", "zl")
LAT = ("zl", "x", "y")
LAYER = ("zh", "co")


def product(zh, core, owner, lat, weight, put):
    first = 2 * (2 * zh + core)
    left = []
    for h in range(2):
        cols = []
        for tt in range(2):
            target = first + tt
            valid = (target >= owner) if h == 0 else (target + 1 >= LAYERS - owner)
            cols.append(lat[h, tt] * valid.astype(jnp.bfloat16))
        left.append(jnp.concatenate(cols, axis=1))
    for d in range(0, D, DC):
        total = jnp.zeros((256, DC), jnp.float32)
        for h in range(2):
            right = [weight[4 * zh + 2 * h + tt, :, d : d + DC] for tt in range(2)]
            total += jnp.dot(
                left[h], jnp.concatenate(right, axis=0), preferred_element_type=jnp.float32
            )
        put(d, (total * SEND).reshape(16, 16, DC))


def decoder_slots(zh, core, owner):
    slots = []
    for h in range(2):
        for tt in range(2):
            target = 2 * (2 * zh + core) + tt
            if h == 0:
                slots.append(jnp.maximum(target - owner, 0))
            else:
                slots.append(jnp.maximum(target + 1, LAYERS - owner))
    return slots


def fetch(zh, core, owner, weight, held, sems):
    copies = []
    for j, slot in enumerate(decoder_slots(zh, core, owner)):
        j += 4 * zh
        copies.append(pltpu.make_async_copy(weight.at[slot], held.at[j], sems.at[j]))
    return copies


def decode_pairs(core, owner, lat, held, copies, out):
    for zh in range(2):
        for copy in copies[zh]:
            copy.wait()

        def put(d, block):
            out[:, zh, :, d : d + DC] = block

        product(zh, core, owner, lat, held, put)


def away_kernel(pos, act, order, enc, bias, dec, g0, g1, g2, g3, lat, out, enc_held, held, enc_sems, sems):
    owner, core, lat_index, zl = (pos[j] for j in range(4))
    enc_copies = [pltpu.make_async_copy(enc.at[h], enc_held.at[h], enc_sems.at[h]) for h in range(2)]
    dec_copies = [fetch(zh, 1 - core, owner, dec, held, sems) for zh in range(2)]
    for copy in enc_copies + dec_copies[0] + dec_copies[1]:
        copy.start()
    g = jnp.concatenate([g0[...], g1[...], g2[...], g3[...]], axis=0)
    tile_row = (lax.broadcasted_iota(jnp.int32, (256, BLK), 0) // 4 + zl) % 4 // 2
    q = lax.broadcasted_iota(jnp.int32, (256, 256), 0)
    c = lax.broadcasted_iota(jnp.int32, (256, 256), 1)
    same = (q // 4 % 4 == (c // 4 + zl) % 4) & (q // 2 % 2 == c // 2 % 2)
    own = same & (q // 16 == c // 16)
    other = same & (c // 64 == q // 16 % 4) & (c // 16 % 4 == q // 64)
    for h in range(2):
        enc_copies[h].wait()
        pre = jnp.dot(g, enc_held[h], preferred_element_type=jnp.float32)
        pre = pre + bias[0, h : h + 1].astype(jnp.float32)
        hits = []
        for tile in range(2):
            hit = jnp.int32(0)
            for j in range(16):
                hit = hit | (act[h, order[tile], j] == lat_index).astype(jnp.int32)
            hits.append(hit)
        on = jnp.where(tile_row == 0, hits[0], hits[1]) > 0
        value = jnp.where(on, jnp.maximum(pre, 0.0), 0.0).astype(jnp.bfloat16)
        for tt in range(2):
            half = (q % 2 == tt) & (c % 2 == h)
            for which, place in enumerate((own, other)):
                lat[which, h, tt] = jnp.dot(
                    (place & half).astype(jnp.bfloat16), value, preferred_element_type=jnp.float32
                ).astype(jnp.bfloat16)
    decode_pairs(1 - core, owner, lat.at[1], held, dec_copies, out)


def mine_kernel(pos, lat, dec, dec_bias, targets, out, base, held, sems):
    owner, core = pos[0], pos[1]
    copies = [fetch(zh, core, owner, dec, held, sems) for zh in range(2)]
    for copy in copies[0] + copies[1]:
        copy.start()
    for r in range(2):
        for tt in range(2):
            row = dec_bias[tt : tt + 1].astype(jnp.float32) - targets[r, tt : tt + 1].astype(jnp.float32)
            base[2 * r + tt : 2 * r + tt + 1] = row
    decode_pairs(core, owner, lat.at[0], held, copies, out)


SM = pl.BlockSpec(memory_space=pltpu.SMEM)
VM = pl.BlockSpec(memory_space=pltpu.VMEM)
ANY = pl.BlockSpec(memory_space=pltpu.HBM)
PARTIAL = jax.ShapeDtypeStruct((16, 2, 16, D), jnp.float32)


HELD = [pltpu.VMEM((8, BLK, D), jnp.bfloat16)]
SEMS = [pltpu.SemaphoreType.DMA((8,))]


def away(pos, act, order, enc, bias, dec, rows):
    return pl.pallas_call(
        away_kernel,
        in_specs=[SM, SM, SM, ANY, VM, ANY, VM, VM, VM, VM],
        out_specs=(VM, VM),
        out_shape=(jax.ShapeDtypeStruct((2, 2, 2, 256, BLK), jnp.bfloat16), PARTIAL),
        scratch_shapes=[pltpu.VMEM((2, D, BLK), jnp.bfloat16)]
        + HELD
        + [pltpu.SemaphoreType.DMA((2,))]
        + SEMS,
        cost_estimate=pl.CostEstimate(
            flops=6 * 2 * 256 * 256 * D, bytes_accessed=12 * 2**20, transcendentals=0
        ),
        compiler_params=pltpu.CompilerParams(vmem_limit_bytes=LARGE),
        name="encode_and_decode_away",
    )(pos, act, order, enc, bias, dec, *rows)


def mine(pos, lat, dec, dec_bias, targets):
    return pl.pallas_call(
        mine_kernel,
        in_specs=[SM, VM, ANY, VM, VM],
        out_specs=(VM, VM),
        out_shape=(PARTIAL, jax.ShapeDtypeStruct((4, D), jnp.float32)),
        scratch_shapes=HELD + SEMS,
        cost_estimate=pl.CostEstimate(
            flops=4 * 2 * 256 * 256 * D, bytes_accessed=10 * 2**20, transcendentals=0
        ),
        compiler_params=pltpu.CompilerParams(vmem_limit_bytes=LARGE),
        name="decode_mine",
    )(pos, lat, dec, dec_bias, targets)


def grad_kernel(which, pos, lat, errs, *rest):
    out, held, sems = rest[-3:]
    owner = pos[0]
    core = pos[1] if which == 0 else 1 - pos[1]
    place = pos[4 + which]
    writes = []
    for zh in range(2):
        lhs = jnp.concatenate([lat[which, h, tt] for h in range(2) for tt in range(2)], axis=1)
        for d in range(0, D, DC):
            rows = [errs[(place + k) % 4, :, zh, :, d : d + DC].reshape(64, DC) for k in range(4)]
            total = lax.dot_general(
                lhs,
                jnp.concatenate(rows, axis=0),
                (((0,), (0,)), ((), ())),
                preferred_element_type=jnp.float32,
            )
            total = (total * (BLK**-0.5)).astype(jnp.bfloat16).reshape(4, BLK, DC)
            held[4 * zh : 4 * zh + 4, :, d : d + DC] = total
        for j, slot in enumerate(decoder_slots(zh, core, owner)):
            target = 2 * (2 * zh + core) + j % 2
            valid = (target >= owner) if j < 2 else (target + 1 >= LAYERS - owner)
            j += 4 * zh
            copy = pltpu.make_async_copy(held.at[j], out.at[slot], sems.at[j])
            pl.when(valid)(copy.start)
            writes.append((valid, copy))
    for valid, copy in writes:
        pl.when(valid)(copy.wait)


def gradients(which, pos, lat, errs, *before):
    return pl.pallas_call(
        functools.partial(grad_kernel, which),
        in_specs=[SM, VM, VM] + [ANY] * len(before),
        out_specs=ANY,
        out_shape=jax.ShapeDtypeStruct((PAIRS, BLK, D), jnp.bfloat16),
        scratch_shapes=HELD + SEMS,
        input_output_aliases={3: 0} if before else {},
        cost_estimate=pl.CostEstimate(
            flops=4 * 2 * 256 * 256 * D, bytes_accessed=8 * 2**20, transcendentals=0
        ),
        compiler_params=pltpu.CompilerParams(vmem_limit_bytes=VMEM),
        name="gradients",
    )(pos, lat, errs, *before)


ALL = ("zh", "co", "zl", "x", "y")


def lines(wide):
    groups = []
    for outer in range(16):
        for other in range(4):
            along_x = (outer // 4 % 2 == 0) == wide
            groups.append(
                [outer * 16 + (k * 4 + other if along_x else other * 4 + k) for k in range(4)]
            )
    return groups


def shift(block, groups, k):
    perm = [(line[i], line[(i + k) % 4]) for line in groups for i in range(4)]
    return lax.ppermute(block, ALL, perm)


def gather4(block, groups):
    return [block] + [shift(block, groups, -k) for k in (1, 2, 3)]


def reduce4(pieces, groups):
    total = pieces[0].astype(jnp.float32)
    for k in (1, 2, 3):
        total = total + shift(pieces[k], groups, k).astype(jnp.float32)
    return total


def local(resid_in, enc_weight, enc_bias, dec_weight, dec_bias, act_blocks, tile_order, targets):
    core, x, y = lax.axis_index("co"), lax.axis_index("x"), lax.axis_index("y")
    at_wide, at_narrow = jnp.where(core == 0, x, y), jnp.where(core == 0, y, x)
    pos = [lax.axis_index(LAYER), core, lax.axis_index(LAT), lax.axis_index("zl"), at_wide, at_narrow]
    pos = jnp.stack(pos).astype(jnp.int32)
    swap = [(0, 1), (1, 0)]
    wide, narrow = lines(True), lines(False)
    z_lines = [[o // 16 * 64 + k * 16 + o % 16 for k in range(4)] for o in range(64)]
    rows = jnp.concatenate(gather4(resid_in.reshape(4, D), z_lines))
    rows = gather4(jnp.concatenate(gather4(rows, narrow)), wide)
    bias = jnp.swapaxes(enc_bias, 0, 1)
    lat, sent = away(pos, act_blocks[:, 0], tile_order, enc_weight[:, 0], bias, dec_weight[0], rows)
    received = lax.ppermute(sent.astype(jnp.float16), "co", swap)
    partial, base = mine(pos, lat, dec_weight[0], dec_bias, targets)
    partial = (partial + received.astype(jnp.float32)).astype(jnp.float16).reshape(4, 128, D)
    partial = reduce4([partial[k] for k in range(4)], wide).astype(jnp.float16).reshape(4, 32, D)
    column = reduce4([partial[k] for k in range(4)], narrow).astype(jnp.float16).reshape(8, 4, D)
    column = lax.all_to_all(column, Z, 0, 0, tiled=True).astype(jnp.float32)
    errs = (jnp.sum(column, axis=0) * (1.0 / SEND) + base).astype(jnp.bfloat16)
    recon_error = errs.reshape(2, 2, D)
    errs = lax.all_to_all(jnp.broadcast_to(errs[None], (8, 4, D)), Z, 0, 0, tiled=True)
    errs = jnp.concatenate(gather4(errs.reshape(32, D), narrow))
    own = jnp.broadcast_to(errs[None], (4, 128, D))
    own = lax.all_to_all(own, ALL, 0, 0, axis_index_groups=wide, tiled=True).reshape(4, 4, 2, 16, D)
    other = lax.ppermute(own, "co", swap)
    dec_grad = gradients(0, pos, lat, own)
    dec_grad = gradients(1, pos, lat, other, dec_grad)
    return (recon_error, dec_grad[None])


def solution(mesh):
    fine = Mesh(mesh.devices.reshape(2, 2, 4, 4, 4), ALL)
    return jax.shard_map(
        local,
        mesh=fine,
        in_specs=(
            P(LAT, None, LAYER, None),
            P(None, LAYER, None, LAT),
            P(None, LAYER, LAT),
            P(LAYER, None, LAT, None),
            P(LAYER, None),
            P(None, LAYER, None, None),
            P(),
            P(LAT, LAYER, None),
        ),
        out_specs=(P(LAT, LAYER, None), P(LAYER, None, LAT, None)),
        check_vma=False,
    )
```

time: 156 us -> 145 us (0.929)
  blocking collectives: 84.1 us -> 44.3 us
  starting transfers between devices: 21.9 us -> 39.9 us
  waiting for transfers between devices: 26.1 us -> 35.5 us
  Pallas kernels: 14.2 us -> 16.7 us
    all_to_all x4 -> x3, blocking collectives: 84.1 us -> 44.3 us  [the longest x1 19.5 us: local(): lax.all_to_all(own, ALL, 0, 0, axis_index_groups=wide, tiled=True)]
    ppermute x1 -> x19, waiting for transfers between devices: 2.19 us -> 35.3 us  [the longest x18 35.3 us: shift(): return lax.ppermute(block, ALL, perm)]
    ppermute x1 -> x19, starting transfers between devices: 3.68 us -> 31.1 us  [the longest x18 25.8 us: shift(): return lax.ppermute(block, ALL, perm)]
    all_to_all x2 -> x0, waiting for transfers between devices: 23.9 us -> none  [the longest x1 15.8 us: spread(): return lax.all_to_all(copies, axes, 0, 0, tiled=True)]
    all_to_all x2 -> x0, starting transfers between devices: 12.4 us -> none  [the longest x1 6.89 us: spread(): return lax.all_to_all(copies, axes, 0, 0, tiled=True)]
    ppermute x1, starting transfers between devices: 5.81 us -> 8.82 us  [local(): other = lax.ppermute(own, 'co', swap)]
    pallas_call x5 -> x4, Pallas kernels: 14.2 us -> 16.7 us  [the longest x2 7.67 us: gradients(): pl.pallas_call(functools.partial(grad_kernel, which), in_specs=[SM, VM, V...]
    broadcast_in_dim x8 -> x2, local copies, waits for them, and re-layouts: 2.2 us -> 0.2 us  [the longest x1 0.15 us: local(): own = jnp.broadcast_to(errs[None], (4, 128, D))]
  transfers between devices with their start and end apart: 4 -> 20, of which waited for: 3 -> 16; matrix products, arithmetic and copies ran while one was open for 0% -> 0% of each run, Pallas kernels for 4% -> 5%
where the time goes in v3:
time: 145 us
  blocking collectives  44.3 us (31%)
  starting transfers between devices  39.9 us (28%)
  waiting for transfers between devices  35.5 us (24%)
  Pallas kernels  16.7 us (12%)
  local copies, waits for them, and re-layouts  5.61 us (4%)
  other arithmetic  1.92 us (1%)
    ppermute x18, waiting for transfers between devices, shift(): return lax.ppermute(block, ALL, perm)  35.3 us
    ppermute x18, starting transfers between devices, shift(): return lax.ppermute(block, ALL, perm)  25.8 us
    all_to_all x1, blocking collectives, local(): lax.all_to_all(own, ALL, 0, 0, axis_index_groups=wide, tiled=True)  19.5 us
    all_to_all x1, blocking collectives, local(): column = lax.all_to_all(column, Z, 0, 0, tiled=True).astype(jnp.float32)  14.2 us
    all_to_all x1, blocking collectives, local(): lax.all_to_all(jnp.broadcast_to(errs[None], (8, 4, D)), Z, 0, 0, tiled=True)  10.5 us
    ppermute x1, starting transfers between devices, local(): other = lax.ppermute(own, 'co', swap)  8.82 us
    pallas_call x2, Pallas kernels, gradients(): pl.pallas_call(functools.partial(grad_kernel, which), in_specs=[SM, VM, V...  7.67 us
    ppermute x1, starting transfers between devices, local(): received = lax.ppermute(sent.astype(jnp.float16), 'co', swap)  5.21 us
  transfers between devices with their start and end apart: 20, of which 16 were waited for; matrix products, arithmetic and copies ran while one was open for 0% of the time, Pallas kernels for 5%

profile of v3, /device:TPU:1, one launch (start us, length us, event | category | flops | bytes accessed | tf_op | source)
XLA Modules:
  0.0 144.9 jit_solution(13775802069259542624)
XLA Ops:
  1.4 2.5 %collective-permute-start.2 = (bf16[4,2304]{1,0:T(4,128)(2,1)S(1)}, bf16[4,2304]{1,0:T(4,128)(2,1)S(1)}, u32[]{:S(2)}, u32[]{:S(2)}) collective-permute-start(bf16[4,2304]{1,0:T(4,128)(2,1)S(1)} %reshape.41), channel_id=1, source_target_pairs={{0,16},{16,32},{32,48},{48,0},{1,17},{17,33},{33,49},{49,1},{2,18}... | collective-permute-start | bytes 55304 | tf_op jit(solution)/shard_map/ppermute | solution.py:225
  3.9 3.0 %collective-permute-start.1 = (bf16[4,2304]{1,0:T(4,128)(2,1)S(1)}, bf16[4,2304]{1,0:T(4,128)(2,1)S(1)}, u32[]{:S(2)}, u32[]{:S(2)}) collective-permute-start(bf16[4,2304]{1,0:T(4,128)(2,1)S(1)} %reshape.41), channel_id=1, source_target_pairs={{0,32},{16,48},{32,0},{48,16},{1,33},{17,49},{33,1},{49,17},{2,34}... | collective-permute-start | bytes 55304 | tf_op jit(solution)/shard_map/ppermute | solution.py:225
  8.1 1.8 %collective-permute-done = bf16[4,2304]{1,0:T(4,128)(2,1)S(1)} collective-permute-done((bf16[4,2304]{1,0:T(4,128)(2,1)S(1)}, bf16[4,2304]{1,0:T(4,128)(2,1)S(1)}, u32[]{:S(2)}, u32[]{:S(2)}) %collective-permute-start) | collective-permute-done | bytes 18464 | tf_op jit(solution)/shard_map/ppermute | solution.py:225
  10.9 2.5 %collective-permute-start.4 = (bf16[16,2304]{1,0:T(8,128)(2,1)S(1)}, bf16[16,2304]{1,0:T(8,128)(2,1)S(1)}, u32[]{:S(2)}, u32[]{:S(2)}) collective-permute-start(bf16[16,2304]{1,0:T(8,128)(2,1)S(1)} %pad_maximum_fusion.1), channel_id=1, source_target_pairs={{0,2},{1,3},{2,0},{3,1},{4,6},{5,7},{6,4},{7,5},{8,10},{9,11},{10,... | collective-permute-start | bytes 221192 | tf_op jit(solution)/shard_map/ppermute | solution.py:225
  18.0 2.9 %collective-permute-start.7 = (bf16[64,2304]{1,0:T(8,128)(2,1)S(1)}, bf16[64,2304]{1,0:T(8,128)(2,1)S(1)}, u32[]{:S(2)}, u32[]{:S(2)}) collective-permute-start(bf16[64,2304]{1,0:T(8,128)(2,1)S(1)} %concatenate.11.g0), channel_id=1, source_target_pairs={{0,8},{4,12},{8,0},{12,4},{1,9},{5,13},{9,1},{13,5},{2,10},{6,14},... | collective-permute-start | bytes 884744 | tf_op jit(solution)/shard_map/ppermute | solution.py:225
  21.8 2.1 %collective-permute-done.8.g3 = bf16[64,2304]{1,0:T(8,128)(2,1)S(1)} collective-permute-done((bf16[64,2304]{1,0:T(8,128)(2,1)S(1)}, bf16[64,2304]{1,0:T(8,128)(2,1)S(1)}, u32[]{:S(2)}, u32[]{:S(2)}) %collective-permute-start.8) | collective-permute-done | bytes 294944 | tf_op jit(solution)/shard_map/ppermute | solution.py:225
  23.8 4.3 %collective-permute-done.7.g2 = bf16[64,2304]{1,0:T(8,128)(2,1)S(1)} collective-permute-done((bf16[64,2304]{1,0:T(8,128)(2,1)S(1)}, bf16[64,2304]{1,0:T(8,128)(2,1)S(1)}, u32[]{:S(2)}, u32[]{:S(2)}) %collective-permute-start.7) | collective-permute-done | bytes 294944 | tf_op jit(solution)/shard_map/ppermute | solution.py:225
  31.4 4.6 %encode_and_decode_away.1 = (bf16[2,2,2,256,128]{4,3,2,1,0:T(8,128)(2,1)S(1)}, f32[16,2,16,2304]{3,2,1,0:T(8,128)S(1)}) custom-call(s32[6]{0:T(128)S(1)} %stack.27.pos, s32[2,2,16]{2,1,0:T(2,128)S(1)} %bitcast.23, s32[2]{0:T(128)S(1)} %copy-done.4, bf16[2,2304,128]{2,1,0:T(8,128)(2,1)S(1)} %bitcast.22, bf16[1,2,128]{2,1,0:T(2,128)(2,1)S(1)} %bitcast.24, ...), custom_call_target="tpu_custom_call" | custom-call | flops 1811939328 | bytes 12582912 | tf_op jit(solution)/shard_map/encode_and_decode_away/pallas_call | solution.py:132
  36.4 5.2 %collective-permute-start.9 = (f16[16,2,16,2304]{3,2,1,0:T(8,128)(2,1)S(1)}, f16[16,2,16,2304]{3,2,1,0:T(8,128)(2,1)S(1)}, u32[]{:S(2)}, u32[]{:S(2)}) collective-permute-start(f16[16,2,16,2304]{3,2,1,0:T(8,128)(2,1)S(1)} %convert_element_type.48), channel_id=1, source_target_pairs={{0,64},{64,0},{1,65},{65,1},{2,66},{66,2},{3,67},{67,3},{4,68},{68... | collective-permute-start | bytes 7077896 | tf_op jit(solution)/shard_map/ppermute | solution.py:251
  41.6 4.5 %decode_mine.1 = (f32[16,2,16,2304]{3,2,1,0:T(8,128)S(1)}, f32[4,2304]{1,0:T(4,128)S(1)}) custom-call(s32[6]{0:T(128)S(1)} %stack.27.pos, bf16[2,2,2,256,128]{4,3,2,1,0:T(8,128)(2,1)S(1)} %get-tuple-element.6.lat, bf16[9,128,2304]{2,1,0:T(8,128)(2,1)} %bitcast.26, bf16[2,2304]{1,0:T(2,128)(2,1)S(1)} %copy-done.2, bf16[2,2,2304]{2,1,0:T(2,128)(2,1)S(1)} %copy-done.1), custom_call_target="tpu_custom_call" | custom-call | flops 1207959552 | bytes 10485760 | tf_op jit(solution)/shard_map/decode_mine/pallas_call | solution.py:150
  47.4 2.3 %collective-permute-start.12 = (f16[128,2304]{1,0:T(8,128)(2,1)S(1)}, f16[128,2304]{1,0:T(8,128)(2,1)S(1)}, u32[]{:S(2)}, u32[]{:S(2)}) collective-permute-start(f16[128,2304]{1,0:T(8,128)(2,1)S(1)} %bitcast.30), channel_id=1, source_target_pairs={{0,12},{4,0},{8,4},{12,8},{1,13},{5,1},{9,5},{13,9},{2,14},{6,2},{... | collective-permute-start | bytes 1769480 | tf_op jit(solution)/shard_map/ppermute | solution.py:225
  50.5 12.5 %collective-permute-done.12 = f16[128,2304]{1,0:T(8,128)(2,1)S(1)} collective-permute-done((f16[128,2304]{1,0:T(8,128)(2,1)S(1)}, f16[128,2304]{1,0:T(8,128)(2,1)S(1)}, u32[]{:S(2)}, u32[]{:S(2)}) %collective-permute-start.12) | collective-permute-done | bytes 589856 | tf_op jit(solution)/shard_map/ppermute | solution.py:225
  62.9 3.4 %collective-permute-done.10 = f16[128,2304]{1,0:T(8,128)(2,1)S(1)} collective-permute-done((f16[128,2304]{1,0:T(8,128)(2,1)S(1)}, f16[128,2304]{1,0:T(8,128)(2,1)S(1)}, u32[]{:S(2)}, u32[]{:S(2)}) %collective-permute-start.10) | collective-permute-done | bytes 589856 | tf_op jit(solution)/shard_map/ppermute | solution.py:225
  66.9 1.4 collective-permute-start.13
  72.6 2.5 %collective-permute-done.14 = f16[32,2304]{1,0:T(8,128)(2,1)S(1)} collective-permute-done((f16[32,2304]{1,0:T(8,128)(2,1)S(1)}, f16[32,2304]{1,0:T(8,128)(2,1)S(1)}, u32[]{:S(2)}, u32[]{:S(2)}) %collective-permute-start.14) | collective-permute-done | bytes 147488 | tf_op jit(solution)/shard_map/ppermute | solution.py:225
  75.3 14.2 %all_to_all.15 = f16[8,4,2304]{2,1,0:T(4,128)(2,1)S(1)} all-to-all(f16[8,4,2304]{2,1,0:T(4,128)(2,1)S(1)} %reshape.42), channel_id=1, replica_groups=mesh['zh'=2,'co'=2,'zl'=4,'x'=4,'y'=4] {'zh','zl'}, dimensions={0} | all-to-all | bytes 294912 | tf_op jit(solution)/shard_map/all_to_all | solution.py:256
  89.7 10.5 %all_to_all.16 = bf16[8,4,2304]{2,1,0:T(4,128)(2,1)S(1)} all-to-all(bf16[8,4,2304]{2,1,0:T(4,128)(2,1)S(1)} %broadcast_in_dim.6), channel_id=1, replica_groups=mesh['zh'=2,'co'=2,'zl'=4,'x'=4,'y'=4] {'zh','zl'}, dimensions={0} | all-to-all | bytes 294912 | tf_op jit(solution)/shard_map/all_to_all | solution.py:259
  100.3 2.9 %collective-permute-start.17 = (bf16[32,2304]{1,0:T(8,128)(2,1)S(1)}, bf16[32,2304]{1,0:T(8,128)(2,1)S(1)}, u32[]{:S(2)}, u32[]{:S(2)}) collective-permute-start(bf16[32,2304]{1,0:T(8,128)(2,1)S(1)} %reshape.44), channel_id=1, source_target_pairs={{0,2},{1,3},{2,0},{3,1},{4,6},{5,7},{6,4},{7,5},{8,10},{9,11},{10,... | collective-permute-start | bytes 442376 | tf_op jit(solution)/shard_map/ppermute | solution.py:225
  103.5 2.0 %collective-permute-done.18 = bf16[32,2304]{1,0:T(8,128)(2,1)S(1)} collective-permute-done((bf16[32,2304]{1,0:T(8,128)(2,1)S(1)}, bf16[32,2304]{1,0:T(8,128)(2,1)S(1)}, u32[]{:S(2)}, u32[]{:S(2)}) %collective-permute-start.18) | collective-permute-done | bytes 147488 | tf_op jit(solution)/shard_map/ppermute | solution.py:225
  105.5 1.8 %collective-permute-done.17 = bf16[32,2304]{1,0:T(8,128)(2,1)S(1)} collective-permute-done((bf16[32,2304]{1,0:T(8,128)(2,1)S(1)}, bf16[32,2304]{1,0:T(8,128)(2,1)S(1)}, u32[]{:S(2)}, u32[]{:S(2)}) %collective-permute-start.17) | collective-permute-done | bytes 147488 | tf_op jit(solution)/shard_map/ppermute | solution.py:225
  107.8 19.5 %all_to_all.17 = bf16[4,128,2304]{2,1,0:T(8,128)(2,1)S(1)} all-to-all(bf16[4,128,2304]{2,1,0:T(8,128)(2,1)S(1)} %broadcast_in_dim.7), channel_id=1, replica_groups={{0,4,8,12},{1,5,9,13},{2,6,10,14},{3,7,11,15},{16,20,24,28},{17,21,25,2..., dimensions={0} | all-to-all | bytes 4718592 | tf_op jit(solution)/shard_map/all_to_all | solution.py:262
  127.4 8.8 %collective-permute-start.19 = (bf16[4,4,2,16,2304]{4,3,2,1,0:T(8,128)(2,1)S(1)}, bf16[4,4,2,16,2304]{4,3,2,1,0:T(8,128)(2,1)}, u32[]{:S(2)}, u32[]{:S(2)}) collective-permute-start(bf16[4,4,2,16,2304]{4,3,2,1,0:T(8,128)(2,1)S(1)} %bitcast.20), channel_id=1, source_target_pairs={{0,64},{64,0},{1,65},{65,1},{2,66},{66,2},{3,67},{67,3},{4,68},{68... | collective-permute-start | bytes 7077896 | tf_op jit(solution)/shard_map/ppermute | solution.py:263
  136.8 3.5 %gradients.2.rest_0_ = bf16[9,128,2304]{2,1,0:T(8,128)(2,1)} custom-call(s32[6]{0:T(128)S(1)} %stack.27.pos, bf16[2,2,2,256,128]{4,3,2,1,0:T(8,128)(2,1)S(1)} %get-tuple-element.6.lat, bf16[4,4,2,16,2304]{4,3,2,1,0:T(8,128)(2,1)S(1)} %bitcast.21), custom_call_target="tpu_custom_call" | custom-call | flops 1207959552 | bytes 8388608 | tf_op jit(solution)/shard_map/gradients/pallas_call | solution.py:194
  140.5 4.2 %gradients.3 = bf16[9,128,2304]{2,1,0:T(8,128)(2,1)} custom-call(s32[6]{0:T(128)S(1)} %stack.27.pos, bf16[2,2,2,256,128]{4,3,2,1,0:T(8,128)(2,1)S(1)} %get-tuple-element.6.lat, bf16[4,4,2,16,2304]{4,3,2,1,0:T(8,128)(2,1)} %collective-permute-done.19.errs, bf16[9,128,2304]{2,1,0:T(8,128)(2,1)} %gradients.2.rest_0_), custom_call_target="tpu_custom_call", output_to_operand_aliasing={{}: (3, {})} | custom-call | flops 1207959552 | bytes 8388608 | tf_op jit(solution)/shard_map/gradients/pallas_call | solution.py:194
  (53 shorter events, 21.0 us)
Async XLA Ops:
  1.4 6.4 %collective-permute-start.2 = (bf16[4,2304]{1,0:T(4,128)(2,1)S(1)}, bf16[4,2304]{1,0:T(4,128)(2,1)S(1)}, u32[]{:S(2)}, u32[]{:S(2)}) collective-permute-start(bf16[4,2304]{1,0:T(4,128)(2,1)S(1)} %reshape.41), channel_id=1, source_target_pairs={{0,16},{16,32},{32,48},{48,0},{1,17},{17,33},{33,49},{49,1},{2,18}... | collective-permute-start | bytes 55304 | tf_op jit(solution)/shard_map/ppermute | solution.py:225
  3.9 4.1 %collective-permute-start.1 = (bf16[4,2304]{1,0:T(4,128)(2,1)S(1)}, bf16[4,2304]{1,0:T(4,128)(2,1)S(1)}, u32[]{:S(2)}, u32[]{:S(2)}) collective-permute-start(bf16[4,2304]{1,0:T(4,128)(2,1)S(1)} %reshape.41), channel_id=1, source_target_pairs={{0,32},{16,48},{32,0},{48,16},{1,33},{17,49},{33,1},{49,17},{2,34}... | collective-permute-start | bytes 55304 | tf_op jit(solution)/shard_map/ppermute | solution.py:225
  6.9 2.9 %collective-permute-start = (bf16[4,2304]{1,0:T(4,128)(2,1)S(1)}, bf16[4,2304]{1,0:T(4,128)(2,1)S(1)}, u32[]{:S(2)}, u32[]{:S(2)}) collective-permute-start(bf16[4,2304]{1,0:T(4,128)(2,1)S(1)} %reshape.41), channel_id=1, source_target_pairs={{0,48},{16,0},{32,16},{48,32},{1,49},{17,1},{33,17},{49,33},{2,50}... | collective-permute-start | bytes 55304 | tf_op jit(solution)/shard_map/ppermute | solution.py:225
  9.9 4.6 %collective-permute-start.5 = (bf16[16,2304]{1,0:T(8,128)(2,1)S(1)}, bf16[16,2304]{1,0:T(8,128)(2,1)S(1)}, u32[]{:S(2)}, u32[]{:S(2)}) collective-permute-start(bf16[16,2304]{1,0:T(8,128)(2,1)S(1)} %pad_maximum_fusion.1), channel_id=1, source_target_pairs={{0,1},{1,2},{2,3},{3,0},{4,5},{5,6},{6,7},{7,4},{8,9},{9,10},{10,1... | collective-permute-start | bytes 221192 | tf_op jit(solution)/shard_map/ppermute | solution.py:225
  10.9 5.0 %collective-permute-start.4 = (bf16[16,2304]{1,0:T(8,128)(2,1)S(1)}, bf16[16,2304]{1,0:T(8,128)(2,1)S(1)}, u32[]{:S(2)}, u32[]{:S(2)}) collective-permute-start(bf16[16,2304]{1,0:T(8,128)(2,1)S(1)} %pad_maximum_fusion.1), channel_id=1, source_target_pairs={{0,2},{1,3},{2,0},{3,1},{4,6},{5,7},{6,4},{7,5},{8,10},{9,11},{10,... | collective-permute-start | bytes 221192 | tf_op jit(solution)/shard_map/ppermute | solution.py:225
  13.3 3.5 %collective-permute-start.3 = (bf16[16,2304]{1,0:T(8,128)(2,1)S(1)}, bf16[16,2304]{1,0:T(8,128)(2,1)S(1)}, u32[]{:S(2)}, u32[]{:S(2)}) collective-permute-start(bf16[16,2304]{1,0:T(8,128)(2,1)S(1)} %pad_maximum_fusion.1), channel_id=1, source_target_pairs={{0,3},{1,0},{2,1},{3,2},{4,7},{5,4},{6,5},{7,6},{8,11},{9,8},{10,9... | collective-permute-start | bytes 221192 | tf_op jit(solution)/shard_map/ppermute | solution.py:225
  16.9 6.9 %collective-permute-start.8 = (bf16[64,2304]{1,0:T(8,128)(2,1)S(1)}, bf16[64,2304]{1,0:T(8,128)(2,1)S(1)}, u32[]{:S(2)}, u32[]{:S(2)}) collective-permute-start(bf16[64,2304]{1,0:T(8,128)(2,1)S(1)} %concatenate.11.g0), channel_id=1, source_target_pairs={{0,4},{4,8},{8,12},{12,0},{1,5},{5,9},{9,13},{13,1},{2,6},{6,10},{... | collective-permute-start | bytes 884744 | tf_op jit(solution)/shard_map/ppermute | solution.py:225
  18.0 10.2 %collective-permute-start.7 = (bf16[64,2304]{1,0:T(8,128)(2,1)S(1)}, bf16[64,2304]{1,0:T(8,128)(2,1)S(1)}, u32[]{:S(2)}, u32[]{:S(2)}) collective-permute-start(bf16[64,2304]{1,0:T(8,128)(2,1)S(1)} %concatenate.11.g0), channel_id=1, source_target_pairs={{0,8},{4,12},{8,0},{12,4},{1,9},{5,13},{9,1},{13,5},{2,10},{6,14},... | collective-permute-start | bytes 884744 | tf_op jit(solution)/shard_map/ppermute | solution.py:225
  20.9 7.3 %collective-permute-start.6 = (bf16[64,2304]{1,0:T(8,128)(2,1)S(1)}, bf16[64,2304]{1,0:T(8,128)(2,1)S(1)}, u32[]{:S(2)}, u32[]{:S(2)}) collective-permute-start(bf16[64,2304]{1,0:T(8,128)(2,1)S(1)} %concatenate.11.g0), channel_id=1, source_target_pairs={{0,12},{4,0},{8,4},{12,8},{1,13},{5,1},{9,5},{13,9},{2,14},{6,2},{... | collective-permute-start | bytes 884744 | tf_op jit(solution)/shard_map/ppermute | solution.py:225
  28.2 1.3 copy-start
  29.4 0.7 copy-start.3
  36.1 5.6 %copy-start.1 = (bf16[2,2,2304]{2,1,0:T(2,128)(2,1)S(1)}, bf16[2,2,2304]{2,1,0:T(2,128)(2,1)}, u32[]{:S(2)}) copy-start(bf16[2,2,2304]{2,1,0:T(2,128)(2,1)} %targets.1) | copy-start | bytes 55300
  36.1 5.6 %copy-start.2 = (bf16[2,2304]{1,0:T(2,128)(2,1)S(1)}, bf16[2,2304]{1,0:T(2,128)(2,1)}, u32[]{:S(2)}) copy-start(bf16[2,2304]{1,0:T(2,128)(2,1)} %dec_bias.1) | copy-start | bytes 27652
  36.4 9.7 %collective-permute-start.9 = (f16[16,2,16,2304]{3,2,1,0:T(8,128)(2,1)S(1)}, f16[16,2,16,2304]{3,2,1,0:T(8,128)(2,1)S(1)}, u32[]{:S(2)}, u32[]{:S(2)}) collective-permute-start(f16[16,2,16,2304]{3,2,1,0:T(8,128)(2,1)S(1)} %convert_element_type.48), channel_id=1, source_target_pairs={{0,64},{64,0},{1,65},{65,1},{2,66},{66,2},{3,67},{67,3},{4,68},{68... | collective-permute-start | bytes 7077896 | tf_op jit(solution)/shard_map/ppermute | solution.py:251
  47.4 15.5 %collective-permute-start.12 = (f16[128,2304]{1,0:T(8,128)(2,1)S(1)}, f16[128,2304]{1,0:T(8,128)(2,1)S(1)}, u32[]{:S(2)}, u32[]{:S(2)}) collective-permute-start(f16[128,2304]{1,0:T(8,128)(2,1)S(1)} %bitcast.30), channel_id=1, source_target_pairs={{0,12},{4,0},{8,4},{12,8},{1,13},{5,1},{9,5},{13,9},{2,14},{6,2},{... | collective-permute-start | bytes 1769480 | tf_op jit(solution)/shard_map/ppermute | solution.py:225
  49.8 13.2 %collective-permute-start.11 = (f16[128,2304]{1,0:T(8,128)(2,1)S(1)}, f16[128,2304]{1,0:T(8,128)(2,1)S(1)}, u32[]{:S(2)}, u32[]{:S(2)}) collective-permute-start(f16[128,2304]{1,0:T(8,128)(2,1)S(1)} %bitcast.29), channel_id=1, source_target_pairs={{0,8},{4,12},{8,0},{12,4},{1,9},{5,13},{9,1},{13,5},{2,10},{6,14},... | collective-permute-start | bytes 1769480 | tf_op jit(solution)/shard_map/ppermute | solution.py:225
  49.8 16.6 %collective-permute-start.10 = (f16[128,2304]{1,0:T(8,128)(2,1)S(1)}, f16[128,2304]{1,0:T(8,128)(2,1)S(1)}, u32[]{:S(2)}, u32[]{:S(2)}) collective-permute-start(f16[128,2304]{1,0:T(8,128)(2,1)S(1)} %bitcast.28), channel_id=1, source_target_pairs={{0,4},{4,8},{8,12},{12,0},{1,5},{5,9},{9,13},{13,1},{2,6},{6,10},{... | collective-permute-start | bytes 1769480 | tf_op jit(solution)/shard_map/ppermute | solution.py:225
  66.9 5.3 %collective-permute-start.13 = (f16[32,2304]{1,0:T(8,128)(2,1)S(1)}, f16[32,2304]{1,0:T(8,128)(2,1)S(1)}, u32[]{:S(2)}, u32[]{:S(2)}) collective-permute-start(f16[32,2304]{1,0:T(8,128)(2,1)S(1)} %get-tuple-element.14), channel_id=1, source_target_pairs={{0,1},{1,2},{2,3},{3,0},{4,5},{5,6},{6,7},{7,4},{8,9},{9,10},{10,1... | collective-permute-start | bytes 442376 | tf_op jit(solution)/shard_map/ppermute | solution.py:225
  68.3 4.3 %collective-permute-start.15 = (f16[32,2304]{1,0:T(8,128)(2,1)S(1)}, f16[32,2304]{1,0:T(8,128)(2,1)S(1)}, u32[]{:S(2)}, u32[]{:S(2)}) collective-permute-start(f16[32,2304]{1,0:T(8,128)(2,1)S(1)} %get-tuple-element.15), channel_id=1, source_target_pairs={{0,3},{1,0},{2,1},{3,2},{4,7},{5,4},{6,5},{7,6},{8,11},{9,8},{10,9... | collective-permute-start | bytes 442376 | tf_op jit(solution)/shard_map/ppermute | solution.py:225
  69.7 5.5 %collective-permute-start.14 = (f16[32,2304]{1,0:T(8,128)(2,1)S(1)}, f16[32,2304]{1,0:T(8,128)(2,1)S(1)}, u32[]{:S(2)}, u32[]{:S(2)}) collective-permute-start(f16[32,2304]{1,0:T(8,128)(2,1)S(1)} %get-tuple-element.16), channel_id=1, source_target_pairs={{0,2},{1,3},{2,0},{3,1},{4,6},{5,7},{6,4},{7,5},{8,10},{9,11},{10,... | collective-permute-start | bytes 442376 | tf_op jit(solution)/shard_map/ppermute | solution.py:225
  100.2 5.3 %collective-permute-start.18 = (bf16[32,2304]{1,0:T(8,128)(2,1)S(1)}, bf16[32,2304]{1,0:T(8,128)(2,1)S(1)}, u32[]{:S(2)}, u32[]{:S(2)}) collective-permute-start(bf16[32,2304]{1,0:T(8,128)(2,1)S(1)} %reshape.44), channel_id=1, source_target_pairs={{0,1},{1,2},{2,3},{3,0},{4,5},{5,6},{6,7},{7,4},{8,9},{9,10},{10,1... | collective-permute-start | bytes 442376 | tf_op jit(solution)/shard_map/ppermute | solution.py:225
  100.3 7.0 %collective-permute-start.17 = (bf16[32,2304]{1,0:T(8,128)(2,1)S(1)}, bf16[32,2304]{1,0:T(8,128)(2,1)S(1)}, u32[]{:S(2)}, u32[]{:S(2)}) collective-permute-start(bf16[32,2304]{1,0:T(8,128)(2,1)S(1)} %reshape.44), channel_id=1, source_target_pairs={{0,2},{1,3},{2,0},{3,1},{4,6},{5,7},{6,4},{7,5},{8,10},{9,11},{10,... | collective-permute-start | bytes 442376 | tf_op jit(solution)/shard_map/ppermute | solution.py:225
  103.2 4.5 %collective-permute-start.16 = (bf16[32,2304]{1,0:T(8,128)(2,1)S(1)}, bf16[32,2304]{1,0:T(8,128)(2,1)S(1)}, u32[]{:S(2)}, u32[]{:S(2)}) collective-permute-start(bf16[32,2304]{1,0:T(8,128)(2,1)S(1)} %reshape.44), channel_id=1, source_target_pairs={{0,3},{1,0},{2,1},{3,2},{4,7},{5,4},{6,5},{7,6},{8,11},{9,8},{10,9... | collective-permute-start | bytes 442376 | tf_op jit(solution)/shard_map/ppermute | solution.py:225
  127.4 13.1 %collective-permute-start.19 = (bf16[4,4,2,16,2304]{4,3,2,1,0:T(8,128)(2,1)S(1)}, bf16[4,4,2,16,2304]{4,3,2,1,0:T(8,128)(2,1)}, u32[]{:S(2)}, u32[]{:S(2)}) collective-permute-start(bf16[4,4,2,16,2304]{4,3,2,1,0:T(8,128)(2,1)S(1)} %bitcast.20), channel_id=1, source_target_pairs={{0,64},{64,0},{1,65},{65,1},{2,66},{66,2},{3,67},{67,3},{4,68},{68... | collective-permute-start | bytes 7077896 | tf_op jit(solution)/shard_map/ppermute | solution.py:263
  (2 other events, 1.3 us)

commit v4 on v3

--- a/solution.py
+++ b/solution.py
@@ -14,7 +14,7 @@
 PAIRS = 9
 LAYERS = 8
 SEND = 2.0**-5
-VMEM = 24 * 1024 * 1024
+VMEM = 14 * 1024 * 1024
 LARGE = 44 * 1024 * 1024
 Z = ("zh", "zl")
 LAT = ("zl", "x", "y")
@@ -23,22 +23,28 @@
 
 def product(zh, core, owner, lat, weight, put):
     first = 2 * (2 * zh + core)
-    left = []
-    for h in range(2):
-        cols = []
-        for tt in range(2):
-            target = first + tt
-            valid = (target >= owner) if h == 0 else (target + 1 >= LAYERS - owner)
-            cols.append(lat[h, tt] * valid.astype(jnp.bfloat16))
-        left.append(jnp.concatenate(cols, axis=1))
-    for d in range(0, D, DC):
-        total = jnp.zeros((256, DC), jnp.float32)
-        for h in range(2):
-            right = [weight[4 * zh + 2 * h + tt, :, d : d + DC] for tt in range(2)]
-            total += jnp.dot(
-                left[h], jnp.concatenate(right, axis=0), preferred_element_type=jnp.float32
-            )
-        put(d, (total * SEND).reshape(16, 16, DC))
+    late = first + 2 >= LAYERS - owner
+
+    def halves(count):
+        left = []
+        for h in range(count):
+            cols = []
+            for tt in range(2):
+                target = first + tt
+                valid = (target >= owner) if h == 0 else (target + 1 >= LAYERS - owner)
+                cols.append(lat[h, tt] * valid.astype(jnp.bfloat16))
+            left.append(jnp.concatenate(cols, axis=1))
+        for d in range(0, D, DC):
+            total = jnp.zeros((256, DC), jnp.float32)
+            for h in range(count):
+                right = [weight[4 * zh + 2 * h + tt, :, d : d + DC] for tt in range(2)]
+                total += jnp.dot(
+                    left[h], jnp.concatenate(right, axis=0), preferred_element_type=jnp.float32
+                )
+            put(d, (total * SEND).reshape(16, 16, DC))
+
+    pl.when(late)(lambda: halves(2))
+    pl.when(jnp.logical_not(late))(lambda: halves(1))
 
 
 def decoder_slots(zh, core, owner):
@@ -72,8 +78,8 @@
         product(zh, core, owner, lat, held, put)
 
 
-def away_kernel(pos, act, order, enc, bias, dec, g0, g1, g2, g3, lat, out, enc_held, held, enc_sems, sems):
-    owner, core, lat_index, zl = (pos[j] for j in range(4))
+def away_kernel(pos, enc, bias, dec, g0, g1, g2, g3, lat, out, enc_held, held, enc_sems, sems):
+    owner, core, zl = (pos[j] for j in range(3))
     enc_copies = [pltpu.make_async_copy(enc.at[h], enc_held.at[h], enc_sems.at[h]) for h in range(2)]
     dec_copies = [fetch(zh, 1 - core, owner, dec, held, sems) for zh in range(2)]
     for copy in enc_copies + dec_copies[0] + dec_copies[1]:
@@ -88,14 +94,8 @@
     for h in range(2):
         enc_copies[h].wait()
         pre = jnp.dot(g, enc_held[h], preferred_element_type=jnp.float32)
-        pre = pre + bias[0, h : h + 1].astype(jnp.float32)
-        hits = []
-        for tile in range(2):
-            hit = jnp.int32(0)
-            for j in range(16):
-                hit = hit | (act[h, order[tile], j] == lat_index).astype(jnp.int32)
-            hits.append(hit)
-        on = jnp.where(tile_row == 0, hits[0], hits[1]) > 0
+        pre = pre + bias[h : h + 1]
+        on = jnp.where(tile_row == 0, pos[5 + 2 * h], pos[6 + 2 * h]) > 0
         value = jnp.where(on, jnp.maximum(pre, 0.0), 0.0).astype(jnp.bfloat16)
         for tt in range(2):
             half = (q % 2 == tt) & (c % 2 == h)
@@ -128,10 +128,10 @@
 SEMS = [pltpu.SemaphoreType.DMA((8,))]
 
 
-def away(pos, act, order, enc, bias, dec, rows):
+def away(pos, enc, bias, dec, rows):
     return pl.pallas_call(
         away_kernel,
-        in_specs=[SM, SM, SM, ANY, VM, ANY, VM, VM, VM, VM],
+        in_specs=[SM, ANY, VM, ANY, VM, VM, VM, VM],
         out_specs=(VM, VM),
         out_shape=(jax.ShapeDtypeStruct((2, 2, 2, 256, BLK), jnp.bfloat16), PARTIAL),
         scratch_shapes=[pltpu.VMEM((2, D, BLK), jnp.bfloat16)]
@@ -143,7 +143,7 @@
         ),
         compiler_params=pltpu.CompilerParams(vmem_limit_bytes=LARGE),
         name="encode_and_decode_away",
-    )(pos, act, order, enc, bias, dec, *rows)
+    )(pos, enc, bias, dec, *rows)
 
 
 def mine(pos, lat, dec, dec_bias, targets):
@@ -165,27 +165,38 @@
     out, held, sems = rest[-3:]
     owner = pos[0]
     core = pos[1] if which == 0 else 1 - pos[1]
-    place = pos[4 + which]
+    place = pos[3 + which]
     writes = []
     for zh in range(2):
-        lhs = jnp.concatenate([lat[which, h, tt] for h in range(2) for tt in range(2)], axis=1)
-        for d in range(0, D, DC):
-            rows = [errs[(place + k) % 4, :, zh, :, d : d + DC].reshape(64, DC) for k in range(4)]
-            total = lax.dot_general(
-                lhs,
-                jnp.concatenate(rows, axis=0),
-                (((0,), (0,)), ((), ())),
-                preferred_element_type=jnp.float32,
-            )
-            total = (total * (BLK**-0.5)).astype(jnp.bfloat16).reshape(4, BLK, DC)
-            held[4 * zh : 4 * zh + 4, :, d : d + DC] = total
-        for j, slot in enumerate(decoder_slots(zh, core, owner)):
-            target = 2 * (2 * zh + core) + j % 2
-            valid = (target >= owner) if j < 2 else (target + 1 >= LAYERS - owner)
-            j += 4 * zh
-            copy = pltpu.make_async_copy(held.at[j], out.at[slot], sems.at[j])
-            pl.when(valid)(copy.start)
-            writes.append((valid, copy))
+        first = 2 * (2 * zh + core)
+        slots = decoder_slots(zh, core, owner)
+        for h in range(2):
+            copies = []
+            for tt in range(2):
+                target, j = first + tt, 4 * zh + 2 * h + tt
+                valid = (target >= owner) if h == 0 else (target + 1 >= LAYERS - owner)
+                copy = pltpu.make_async_copy(held.at[j], out.at[slots[2 * h + tt]], sems.at[j])
+                copies.append((valid, copy))
+            writes += copies
+
+            @pl.when(copies[1][0])
+            def _():
+                lhs = jnp.concatenate([lat[which, h, 0], lat[which, h, 1]], axis=1)
+                for d in range(0, D, DC):
+                    rows = [
+                        errs[(place + k) % 4, :, zh, :, d : d + DC].reshape(64, DC) for k in range(4)
+                    ]
+                    total = lax.dot_general(
+                        lhs,
+                        jnp.concatenate(rows, axis=0),
+                        (((0,), (0,)), ((), ())),
+                        preferred_element_type=jnp.float32,
+                    )
+                    total = (total * (BLK**-0.5)).astype(jnp.bfloat16).reshape(2, BLK, DC)
+                    held[4 * zh + 2 * h : 4 * zh + 2 * h + 2, :, d : d + DC] = total
+                for valid, copy in copies:
+                    pl.when(valid)(copy.start)
+
     for valid, copy in writes:
         pl.when(valid)(copy.wait)
 
@@ -239,15 +250,17 @@
 def local(resid_in, enc_weight, enc_bias, dec_weight, dec_bias, act_blocks, tile_order, targets):
     core, x, y = lax.axis_index("co"), lax.axis_index("x"), lax.axis_index("y")
     at_wide, at_narrow = jnp.where(core == 0, x, y), jnp.where(core == 0, y, x)
-    pos = [lax.axis_index(LAYER), core, lax.axis_index(LAT), lax.axis_index("zl"), at_wide, at_narrow]
-    pos = jnp.stack(pos).astype(jnp.int32)
+    pos = [lax.axis_index(LAYER), core, lax.axis_index("zl"), at_wide, at_narrow]
+    listed = jnp.any(act_blocks[:, 0] == lax.axis_index(LAT), axis=2)
+    hits = jnp.where(tile_order[None] == 0, listed[:, :1], listed[:, 1:])
+    pos = jnp.concatenate([jnp.stack(pos).astype(jnp.int32), hits.reshape(4).astype(jnp.int32)])
     swap = [(0, 1), (1, 0)]
     wide, narrow = lines(True), lines(False)
     z_lines = [[o // 16 * 64 + k * 16 + o % 16 for k in range(4)] for o in range(64)]
     rows = jnp.concatenate(gather4(resid_in.reshape(4, D), z_lines))
     rows = gather4(jnp.concatenate(gather4(rows, narrow)), wide)
-    bias = jnp.swapaxes(enc_bias, 0, 1)
-    lat, sent = away(pos, act_blocks[:, 0], tile_order, enc_weight[:, 0], bias, dec_weight[0], rows)
+    bias = enc_bias[:, 0].astype(jnp.float32)
+    lat, sent = away(pos, enc_weight[:, 0], bias, dec_weight[0], rows)
     received = lax.ppermute(sent.astype(jnp.float16), "co", swap)
     partial, base = mine(pos, lat, dec_weight[0], dec_bias, targets)
     partial = (partial + received.astype(jnp.float32)).astype(jnp.float16).reshape(4, 128, D)

time: 145 us -> 143 us (0.986)
  waiting for transfers between devices: 35.5 us -> 33.2 us
  other arithmetic: 1.92 us -> 4.14 us
  local copies, waits for them, and re-layouts: 5.61 us -> 3.88 us
  Pallas kernels: 16.7 us -> 15.1 us
    ppermute x18, waiting for transfers between devices: 35.3 us -> 32.8 us  [shift(): return lax.ppermute(block, ALL, perm)]
    unnamed x12 -> x6, local copies, waits for them, and re-layouts: 3.27 us -> 1.28 us
  transfers between devices with their start and end apart: 20 -> 20, of which waited for: 16 -> 14; matrix products, arithmetic and copies ran while one was open for 0% -> 2% of each run, Pallas kernels for 5% -> 5%
where the time goes in v4:
time: 143 us; the launch traced here: 142 us
  blocking collectives  43.8 us (31%)
  starting transfers between devices  41.3 us (29%)
  waiting for transfers between devices  33.2 us (23%)
  Pallas kernels  15.1 us (11%)
  other arithmetic  4.14 us (3%)
  local copies, waits for them, and re-layouts  3.88 us (3%)
    ppermute x18, waiting for transfers between devices, shift(): return lax.ppermute(block, ALL, perm)  32.8 us
    ppermute x18, starting transfers between devices, shift(): return lax.ppermute(block, ALL, perm)  25.8 us
    all_to_all x1, blocking collectives, local(): lax.all_to_all(own, ALL, 0, 0, axis_index_groups=wide, tiled=True)  19.2 us
    all_to_all x1, blocking collectives, local(): column = lax.all_to_all(column, Z, 0, 0, tiled=True).astype(jnp.float32)  14 us
    all_to_all x1, blocking collectives, local(): lax.all_to_all(jnp.broadcast_to(errs[None], (8, 4, D)), Z, 0, 0, tiled=True)  10.5 us
    ppermute x1, starting transfers between devices, local(): other = lax.ppermute(own, 'co', swap)  10.2 us
    pallas_call x2, Pallas kernels, gradients(): pl.pallas_call(functools.partial(grad_kernel, which), in_specs=[SM, VM, V...  7.21 us
    ppermute x1, starting transfers between devices, local(): received = lax.ppermute(sent.astype(jnp.float16), 'co', swap)  5.33 us
  transfers between devices with their start and end apart: 20, of which 14 were waited for; matrix products, arithmetic and copies ran while one was open for 2% of the time, Pallas kernels for 5%

profile of v4, /device:TPU:1, one launch (start us, length us, event | category | flops | bytes accessed | tf_op | source)
XLA Modules:
  0.0 142.4 jit_solution(6608415902507443681)
XLA Ops:
  1.4 2.5 %collective-permute-start.2 = (bf16[4,2304]{1,0:T(4,128)(2,1)S(1)}, bf16[4,2304]{1,0:T(4,128)(2,1)S(1)}, u32[]{:S(2)}, u32[]{:S(2)}) collective-permute-start(bf16[4,2304]{1,0:T(4,128)(2,1)S(1)} %reshape.54), channel_id=1, source_target_pairs={{0,16},{16,32},{32,48},{48,0},{1,17},{17,33},{33,49},{49,1},{2,18}... | collective-permute-start | bytes 55304 | tf_op jit(solution)/shard_map/ppermute | solution.py:236
  3.9 3.0 %collective-permute-start.1 = (bf16[4,2304]{1,0:T(4,128)(2,1)S(1)}, bf16[4,2304]{1,0:T(4,128)(2,1)S(1)}, u32[]{:S(2)}, u32[]{:S(2)}) collective-permute-start(bf16[4,2304]{1,0:T(4,128)(2,1)S(1)} %reshape.54), channel_id=1, source_target_pairs={{0,32},{16,48},{32,0},{48,16},{1,33},{17,49},{33,1},{49,17},{2,34}... | collective-permute-start | bytes 55304 | tf_op jit(solution)/shard_map/ppermute | solution.py:236
  10.9 2.5 %collective-permute-start.4 = (bf16[16,2304]{1,0:T(8,128)(2,1)S(1)}, bf16[16,2304]{1,0:T(8,128)(2,1)S(1)}, u32[]{:S(2)}, u32[]{:S(2)}) collective-permute-start(bf16[16,2304]{1,0:T(8,128)(2,1)S(1)} %pad_maximum_fusion.1), channel_id=1, source_target_pairs={{0,2},{1,3},{2,0},{3,1},{4,6},{5,7},{6,4},{7,5},{8,10},{9,11},{10,... | collective-permute-start | bytes 221192 | tf_op jit(solution)/shard_map/ppermute | solution.py:236
  18.0 2.9 %collective-permute-start.7 = (bf16[64,2304]{1,0:T(8,128)(2,1)S(1)}, bf16[64,2304]{1,0:T(8,128)(2,1)S(1)}, u32[]{:S(2)}, u32[]{:S(2)}) collective-permute-start(bf16[64,2304]{1,0:T(8,128)(2,1)S(1)} %concatenate.15.g0), channel_id=1, source_target_pairs={{0,8},{4,12},{8,0},{12,4},{1,9},{5,13},{9,1},{13,5},{2,10},{6,14},... | collective-permute-start | bytes 884744 | tf_op jit(solution)/shard_map/ppermute | solution.py:236
  23.8 4.3 %collective-permute-done.7.g2 = bf16[64,2304]{1,0:T(8,128)(2,1)S(1)} collective-permute-done((bf16[64,2304]{1,0:T(8,128)(2,1)S(1)}, bf16[64,2304]{1,0:T(8,128)(2,1)S(1)}, u32[]{:S(2)}, u32[]{:S(2)}) %collective-permute-start.7) | collective-permute-done | bytes 294944 | tf_op jit(solution)/shard_map/ppermute | solution.py:236
  28.2 1.3 copy-done
  29.4 3.8 %encode_and_decode_away.1 = (bf16[2,2,2,256,128]{4,3,2,1,0:T(8,128)(2,1)S(1)}, f32[16,2,16,2304]{3,2,1,0:T(8,128)S(1)}) custom-call(s32[9]{0:T(128)S(1)} %concatenate.13.pos, bf16[2,2304,128]{2,1,0:T(8,128)(2,1)S(1)} %bitcast.22, f32[2,128]{1,0:T(2,128)S(1)} %bitcast_convert_fusion.bias, bf16[9,128,2304]{2,1,0:T(8,128)(2,1)} %bitcast.23, ...), custom_call_target="tpu_custom_call" | custom-call | flops 1811939328 | bytes 12582912 | tf_op jit(solution)/shard_map/encode_and_decode_away/pallas_call | solution.py:132
  33.7 5.3 %collective-permute-start.9 = (f16[16,2,16,2304]{3,2,1,0:T(8,128)(2,1)S(1)}, f16[16,2,16,2304]{3,2,1,0:T(8,128)(2,1)S(1)}, u32[]{:S(2)}, u32[]{:S(2)}) collective-permute-start(f16[16,2,16,2304]{3,2,1,0:T(8,128)(2,1)S(1)} %convert_element_type.63), channel_id=1, source_target_pairs={{0,64},{64,0},{1,65},{65,1},{2,66},{66,2},{3,67},{67,3},{4,68},{68... | collective-permute-start | bytes 7077896 | tf_op jit(solution)/shard_map/ppermute | solution.py:264
  39.0 4.0 %decode_mine.1 = (f32[16,2,16,2304]{3,2,1,0:T(8,128)S(1)}, f32[4,2304]{1,0:T(4,128)S(1)}) custom-call(s32[9]{0:T(128)S(1)} %concatenate.13.pos, bf16[2,2,2,256,128]{4,3,2,1,0:T(8,128)(2,1)S(1)} %get-tuple-element.6.lat, bf16[9,128,2304]{2,1,0:T(8,128)(2,1)} %bitcast.24, bf16[2,2304]{1,0:T(2,128)(2,1)S(1)} %copy-done.2, bf16[2,2,2304]{2,1,0:T(2,128)(2,1)S(1)} %copy-done.1), custom_call_target="tpu_custom_call" | custom-call | flops 1207959552 | bytes 10485760 | tf_op jit(solution)/shard_map/decode_mine/pallas_call | solution.py:150
  44.5 2.3 %collective-permute-start.12 = (f16[128,2304]{1,0:T(8,128)(2,1)S(1)}, f16[128,2304]{1,0:T(8,128)(2,1)S(1)}, u32[]{:S(2)}, u32[]{:S(2)}) collective-permute-start(f16[128,2304]{1,0:T(8,128)(2,1)S(1)} %bitcast.28), channel_id=1, source_target_pairs={{0,12},{4,0},{8,4},{12,8},{1,13},{5,1},{9,5},{13,9},{2,14},{6,2},{... | collective-permute-start | bytes 1769480 | tf_op jit(solution)/shard_map/ppermute | solution.py:236
  47.5 12.5 %collective-permute-done.12 = f16[128,2304]{1,0:T(8,128)(2,1)S(1)} collective-permute-done((f16[128,2304]{1,0:T(8,128)(2,1)S(1)}, f16[128,2304]{1,0:T(8,128)(2,1)S(1)}, u32[]{:S(2)}, u32[]{:S(2)}) %collective-permute-start.12) | collective-permute-done | bytes 589856 | tf_op jit(solution)/shard_map/ppermute | solution.py:236
  60.0 3.4 %collective-permute-done.10 = f16[128,2304]{1,0:T(8,128)(2,1)S(1)} collective-permute-done((f16[128,2304]{1,0:T(8,128)(2,1)S(1)}, f16[128,2304]{1,0:T(8,128)(2,1)S(1)}, u32[]{:S(2)}, u32[]{:S(2)}) %collective-permute-start.10) | collective-permute-done | bytes 589856 | tf_op jit(solution)/shard_map/ppermute | solution.py:236
  63.9 1.4 collective-permute-start.13
  65.3 1.3 collective-permute-start.15
  67.9 1.4 collective-permute-done.13
  69.6 2.5 %collective-permute-done.14 = f16[32,2304]{1,0:T(8,128)(2,1)S(1)} collective-permute-done((f16[32,2304]{1,0:T(8,128)(2,1)S(1)}, f16[32,2304]{1,0:T(8,128)(2,1)S(1)}, u32[]{:S(2)}, u32[]{:S(2)}) %collective-permute-start.14) | collective-permute-done | bytes 147488 | tf_op jit(solution)/shard_map/ppermute | solution.py:236
  72.3 14.0 %all_to_all.15 = f16[8,4,2304]{2,1,0:T(4,128)(2,1)S(1)} all-to-all(f16[8,4,2304]{2,1,0:T(4,128)(2,1)S(1)} %reshape.55), channel_id=1, replica_groups=mesh['zh'=2,'co'=2,'zl'=4,'x'=4,'y'=4] {'zh','zl'}, dimensions={0} | all-to-all | bytes 294912 | tf_op jit(solution)/shard_map/all_to_all | solution.py:269
  86.5 10.5 %all_to_all.16 = bf16[8,4,2304]{2,1,0:T(4,128)(2,1)S(1)} all-to-all(bf16[8,4,2304]{2,1,0:T(4,128)(2,1)S(1)} %broadcast_in_dim.49), channel_id=1, replica_groups=mesh['zh'=2,'co'=2,'zl'=4,'x'=4,'y'=4] {'zh','zl'}, dimensions={0} | all-to-all | bytes 294912 | tf_op jit(solution)/shard_map/all_to_all | solution.py:272
  97.3 2.3 %collective-permute-start.17 = (bf16[32,2304]{1,0:T(8,128)(2,1)S(1)}, bf16[32,2304]{1,0:T(8,128)(2,1)S(1)}, u32[]{:S(2)}, u32[]{:S(2)}) collective-permute-start(bf16[32,2304]{1,0:T(8,128)(2,1)S(1)} %reshape.57), channel_id=1, source_target_pairs={{0,2},{1,3},{2,0},{3,1},{4,6},{5,7},{6,4},{7,5},{8,10},{9,11},{10,... | collective-permute-start | bytes 442376 | tf_op jit(solution)/shard_map/ppermute | solution.py:236
  100.3 3.6 %collective-permute-done.18 = bf16[32,2304]{1,0:T(8,128)(2,1)S(1)} collective-permute-done((bf16[32,2304]{1,0:T(8,128)(2,1)S(1)}, bf16[32,2304]{1,0:T(8,128)(2,1)S(1)}, u32[]{:S(2)}, u32[]{:S(2)}) %collective-permute-start.18) | collective-permute-done | bytes 147488 | tf_op jit(solution)/shard_map/ppermute | solution.py:236
  104.7 19.2 %all_to_all.17 = bf16[4,128,2304]{2,1,0:T(8,128)(2,1)S(1)} all-to-all(bf16[4,128,2304]{2,1,0:T(8,128)(2,1)S(1)} %broadcast_in_dim.50), channel_id=1, replica_groups={{0,4,8,12},{1,5,9,13},{2,6,10,14},{3,7,11,15},{16,20,24,28},{17,21,25,2..., dimensions={0} | all-to-all | bytes 4718592 | tf_op jit(solution)/shard_map/all_to_all | solution.py:275
  123.9 10.2 %collective-permute-start.19 = (bf16[4,4,2,16,2304]{4,3,2,1,0:T(8,128)(2,1)S(1)}, bf16[4,4,2,16,2304]{4,3,2,1,0:T(8,128)(2,1)}, u32[]{:S(2)}, u32[]{:S(2)}) collective-permute-start(bf16[4,4,2,16,2304]{4,3,2,1,0:T(8,128)(2,1)S(1)} %bitcast.20), channel_id=1, source_target_pairs={{0,64},{64,0},{1,65},{65,1},{2,66},{66,2},{3,67},{67,3},{4,68},{68... | collective-permute-start | bytes 7077896 | tf_op jit(solution)/shard_map/ppermute | solution.py:276
  134.7 3.4 %gradients.2.rest_0_ = bf16[9,128,2304]{2,1,0:T(8,128)(2,1)} custom-call(s32[9]{0:T(128)S(1)} %concatenate.13.pos, bf16[2,2,2,256,128]{4,3,2,1,0:T(8,128)(2,1)S(1)} %get-tuple-element.6.lat, bf16[4,4,2,16,2304]{4,3,2,1,0:T(8,128)(2,1)S(1)} %bitcast.21), custom_call_target="tpu_custom_call" | custom-call | flops 1207959552 | bytes 8388608 | tf_op jit(solution)/shard_map/gradients/pallas_call | solution.py:205
  138.4 3.8 %gradients.3 = bf16[9,128,2304]{2,1,0:T(8,128)(2,1)} custom-call(s32[9]{0:T(128)S(1)} %concatenate.13.pos, bf16[2,2,2,256,128]{4,3,2,1,0:T(8,128)(2,1)S(1)} %get-tuple-element.6.lat, bf16[4,4,2,16,2304]{4,3,2,1,0:T(8,128)(2,1)} %collective-permute-done.19.errs, bf16[9,128,2304]{2,1,0:T(8,128)(2,1)} %gradients.2.rest_0_), custom_call_target="tpu_custom_call", output_to_operand_aliasing={{}: (3, {})} | custom-call | flops 1207959552 | bytes 8388608 | tf_op jit(solution)/shard_map/gradients/pallas_call | solution.py:205
  (53 shorter events, 19.8 us)
Async XLA Ops:
  1.4 7.8 %collective-permute-start.2 = (bf16[4,2304]{1,0:T(4,128)(2,1)S(1)}, bf16[4,2304]{1,0:T(4,128)(2,1)S(1)}, u32[]{:S(2)}, u32[]{:S(2)}) collective-permute-start(bf16[4,2304]{1,0:T(4,128)(2,1)S(1)} %reshape.54), channel_id=1, source_target_pairs={{0,16},{16,32},{32,48},{48,0},{1,17},{17,33},{33,49},{49,1},{2,18}... | collective-permute-start | bytes 55304 | tf_op jit(solution)/shard_map/ppermute | solution.py:236
  3.9 5.2 %collective-permute-start.1 = (bf16[4,2304]{1,0:T(4,128)(2,1)S(1)}, bf16[4,2304]{1,0:T(4,128)(2,1)S(1)}, u32[]{:S(2)}, u32[]{:S(2)}) collective-permute-start(bf16[4,2304]{1,0:T(4,128)(2,1)S(1)} %reshape.54), channel_id=1, source_target_pairs={{0,32},{16,48},{32,0},{48,16},{1,33},{17,49},{33,1},{49,17},{2,34}... | collective-permute-start | bytes 55304 | tf_op jit(solution)/shard_map/ppermute | solution.py:236
  6.9 2.9 %collective-permute-start = (bf16[4,2304]{1,0:T(4,128)(2,1)S(1)}, bf16[4,2304]{1,0:T(4,128)(2,1)S(1)}, u32[]{:S(2)}, u32[]{:S(2)}) collective-permute-start(bf16[4,2304]{1,0:T(4,128)(2,1)S(1)} %reshape.54), channel_id=1, source_target_pairs={{0,48},{16,0},{32,16},{48,32},{1,49},{17,1},{33,17},{49,33},{2,50}... | collective-permute-start | bytes 55304 | tf_op jit(solution)/shard_map/ppermute | solution.py:236
  9.9 4.8 %collective-permute-start.5 = (bf16[16,2304]{1,0:T(8,128)(2,1)S(1)}, bf16[16,2304]{1,0:T(8,128)(2,1)S(1)}, u32[]{:S(2)}, u32[]{:S(2)}) collective-permute-start(bf16[16,2304]{1,0:T(8,128)(2,1)S(1)} %pad_maximum_fusion.1), channel_id=1, source_target_pairs={{0,1},{1,2},{2,3},{3,0},{4,5},{5,6},{6,7},{7,4},{8,9},{9,10},{10,1... | collective-permute-start | bytes 221192 | tf_op jit(solution)/shard_map/ppermute | solution.py:236
  10.9 5.0 %collective-permute-start.4 = (bf16[16,2304]{1,0:T(8,128)(2,1)S(1)}, bf16[16,2304]{1,0:T(8,128)(2,1)S(1)}, u32[]{:S(2)}, u32[]{:S(2)}) collective-permute-start(bf16[16,2304]{1,0:T(8,128)(2,1)S(1)} %pad_maximum_fusion.1), channel_id=1, source_target_pairs={{0,2},{1,3},{2,0},{3,1},{4,6},{5,7},{6,4},{7,5},{8,10},{9,11},{10,... | collective-permute-start | bytes 221192 | tf_op jit(solution)/shard_map/ppermute | solution.py:236
  13.3 3.5 %collective-permute-start.3 = (bf16[16,2304]{1,0:T(8,128)(2,1)S(1)}, bf16[16,2304]{1,0:T(8,128)(2,1)S(1)}, u32[]{:S(2)}, u32[]{:S(2)}) collective-permute-start(bf16[16,2304]{1,0:T(8,128)(2,1)S(1)} %pad_maximum_fusion.1), channel_id=1, source_target_pairs={{0,3},{1,0},{2,1},{3,2},{4,7},{5,4},{6,5},{7,6},{8,11},{9,8},{10,9... | collective-permute-start | bytes 221192 | tf_op jit(solution)/shard_map/ppermute | solution.py:236
  16.9 6.9 %collective-permute-start.8 = (bf16[64,2304]{1,0:T(8,128)(2,1)S(1)}, bf16[64,2304]{1,0:T(8,128)(2,1)S(1)}, u32[]{:S(2)}, u32[]{:S(2)}) collective-permute-start(bf16[64,2304]{1,0:T(8,128)(2,1)S(1)} %concatenate.15.g0), channel_id=1, source_target_pairs={{0,4},{4,8},{8,12},{12,0},{1,5},{5,9},{9,13},{13,1},{2,6},{6,10},{... | collective-permute-start | bytes 884744 | tf_op jit(solution)/shard_map/ppermute | solution.py:236
  18.0 10.2 %collective-permute-start.7 = (bf16[64,2304]{1,0:T(8,128)(2,1)S(1)}, bf16[64,2304]{1,0:T(8,128)(2,1)S(1)}, u32[]{:S(2)}, u32[]{:S(2)}) collective-permute-start(bf16[64,2304]{1,0:T(8,128)(2,1)S(1)} %concatenate.15.g0), channel_id=1, source_target_pairs={{0,8},{4,12},{8,0},{12,4},{1,9},{5,13},{9,1},{13,5},{2,10},{6,14},... | collective-permute-start | bytes 884744 | tf_op jit(solution)/shard_map/ppermute | solution.py:236
  20.9 7.3 %collective-permute-start.6 = (bf16[64,2304]{1,0:T(8,128)(2,1)S(1)}, bf16[64,2304]{1,0:T(8,128)(2,1)S(1)}, u32[]{:S(2)}, u32[]{:S(2)}) collective-permute-start(bf16[64,2304]{1,0:T(8,128)(2,1)S(1)} %concatenate.15.g0), channel_id=1, source_target_pairs={{0,12},{4,0},{8,4},{12,8},{1,13},{5,1},{9,5},{13,9},{2,14},{6,2},{... | collective-permute-start | bytes 884744 | tf_op jit(solution)/shard_map/ppermute | solution.py:236
  28.2 1.3 copy-start
  33.3 5.7 %copy-start.1 = (bf16[2,2,2304]{2,1,0:T(2,128)(2,1)S(1)}, bf16[2,2,2304]{2,1,0:T(2,128)(2,1)}, u32[]{:S(2)}) copy-start(bf16[2,2,2304]{2,1,0:T(2,128)(2,1)} %targets.1) | copy-start | bytes 55300
  33.3 5.7 %copy-start.2 = (bf16[2,2304]{1,0:T(2,128)(2,1)S(1)}, bf16[2,2304]{1,0:T(2,128)(2,1)}, u32[]{:S(2)}) copy-start(bf16[2,2304]{1,0:T(2,128)(2,1)} %dec_bias.1) | copy-start | bytes 27652
  33.7 9.5 %collective-permute-start.9 = (f16[16,2,16,2304]{3,2,1,0:T(8,128)(2,1)S(1)}, f16[16,2,16,2304]{3,2,1,0:T(8,128)(2,1)S(1)}, u32[]{:S(2)}, u32[]{:S(2)}) collective-permute-start(f16[16,2,16,2304]{3,2,1,0:T(8,128)(2,1)S(1)} %convert_element_type.63), channel_id=1, source_target_pairs={{0,64},{64,0},{1,65},{65,1},{2,66},{66,2},{3,67},{67,3},{4,68},{68... | collective-permute-start | bytes 7077896 | tf_op jit(solution)/shard_map/ppermute | solution.py:264
  44.5 15.5 %collective-permute-start.12 = (f16[128,2304]{1,0:T(8,128)(2,1)S(1)}, f16[128,2304]{1,0:T(8,128)(2,1)S(1)}, u32[]{:S(2)}, u32[]{:S(2)}) collective-permute-start(f16[128,2304]{1,0:T(8,128)(2,1)S(1)} %bitcast.28), channel_id=1, source_target_pairs={{0,12},{4,0},{8,4},{12,8},{1,13},{5,1},{9,5},{13,9},{2,14},{6,2},{... | collective-permute-start | bytes 1769480 | tf_op jit(solution)/shard_map/ppermute | solution.py:236
  46.8 13.2 %collective-permute-start.11 = (f16[128,2304]{1,0:T(8,128)(2,1)S(1)}, f16[128,2304]{1,0:T(8,128)(2,1)S(1)}, u32[]{:S(2)}, u32[]{:S(2)}) collective-permute-start(f16[128,2304]{1,0:T(8,128)(2,1)S(1)} %bitcast.27), channel_id=1, source_target_pairs={{0,8},{4,12},{8,0},{12,4},{1,9},{5,13},{9,1},{13,5},{2,10},{6,14},... | collective-permute-start | bytes 1769480 | tf_op jit(solution)/shard_map/ppermute | solution.py:236
  46.8 16.6 %collective-permute-start.10 = (f16[128,2304]{1,0:T(8,128)(2,1)S(1)}, f16[128,2304]{1,0:T(8,128)(2,1)S(1)}, u32[]{:S(2)}, u32[]{:S(2)}) collective-permute-start(f16[128,2304]{1,0:T(8,128)(2,1)S(1)} %bitcast.26), channel_id=1, source_target_pairs={{0,4},{4,8},{8,12},{12,0},{1,5},{5,9},{9,13},{13,1},{2,6},{6,10},{... | collective-permute-start | bytes 1769480 | tf_op jit(solution)/shard_map/ppermute | solution.py:236
  63.9 5.3 %collective-permute-start.13 = (f16[32,2304]{1,0:T(8,128)(2,1)S(1)}, f16[32,2304]{1,0:T(8,128)(2,1)S(1)}, u32[]{:S(2)}, u32[]{:S(2)}) collective-permute-start(f16[32,2304]{1,0:T(8,128)(2,1)S(1)} %get-tuple-element.16), channel_id=1, source_target_pairs={{0,1},{1,2},{2,3},{3,0},{4,5},{5,6},{6,7},{7,4},{8,9},{9,10},{10,1... | collective-permute-start | bytes 442376 | tf_op jit(solution)/shard_map/ppermute | solution.py:236
  65.3 4.3 %collective-permute-start.15 = (f16[32,2304]{1,0:T(8,128)(2,1)S(1)}, f16[32,2304]{1,0:T(8,128)(2,1)S(1)}, u32[]{:S(2)}, u32[]{:S(2)}) collective-permute-start(f16[32,2304]{1,0:T(8,128)(2,1)S(1)} %get-tuple-element.17), channel_id=1, source_target_pairs={{0,3},{1,0},{2,1},{3,2},{4,7},{5,4},{6,5},{7,6},{8,11},{9,8},{10,9... | collective-permute-start | bytes 442376 | tf_op jit(solution)/shard_map/ppermute | solution.py:236
  66.7 5.5 %collective-permute-start.14 = (f16[32,2304]{1,0:T(8,128)(2,1)S(1)}, f16[32,2304]{1,0:T(8,128)(2,1)S(1)}, u32[]{:S(2)}, u32[]{:S(2)}) collective-permute-start(f16[32,2304]{1,0:T(8,128)(2,1)S(1)} %get-tuple-element.18), channel_id=1, source_target_pairs={{0,2},{1,3},{2,0},{3,1},{4,6},{5,7},{6,4},{7,5},{8,10},{9,11},{10,... | collective-permute-start | bytes 442376 | tf_op jit(solution)/shard_map/ppermute | solution.py:236
  97.0 6.9 %collective-permute-start.18 = (bf16[32,2304]{1,0:T(8,128)(2,1)S(1)}, bf16[32,2304]{1,0:T(8,128)(2,1)S(1)}, u32[]{:S(2)}, u32[]{:S(2)}) collective-permute-start(bf16[32,2304]{1,0:T(8,128)(2,1)S(1)} %reshape.57), channel_id=1, source_target_pairs={{0,1},{1,2},{2,3},{3,0},{4,5},{5,6},{6,7},{7,4},{8,9},{9,10},{10,1... | collective-permute-start | bytes 442376 | tf_op jit(solution)/shard_map/ppermute | solution.py:236
  97.3 6.6 %collective-permute-start.17 = (bf16[32,2304]{1,0:T(8,128)(2,1)S(1)}, bf16[32,2304]{1,0:T(8,128)(2,1)S(1)}, u32[]{:S(2)}, u32[]{:S(2)}) collective-permute-start(bf16[32,2304]{1,0:T(8,128)(2,1)S(1)} %reshape.57), channel_id=1, source_target_pairs={{0,2},{1,3},{2,0},{3,1},{4,6},{5,7},{6,4},{7,5},{8,10},{9,11},{10,... | collective-permute-start | bytes 442376 | tf_op jit(solution)/shard_map/ppermute | solution.py:236
  99.6 4.9 %collective-permute-start.16 = (bf16[32,2304]{1,0:T(8,128)(2,1)S(1)}, bf16[32,2304]{1,0:T(8,128)(2,1)S(1)}, u32[]{:S(2)}, u32[]{:S(2)}) collective-permute-start(bf16[32,2304]{1,0:T(8,128)(2,1)S(1)} %reshape.57), channel_id=1, source_target_pairs={{0,3},{1,0},{2,1},{3,2},{4,7},{5,4},{6,5},{7,6},{8,11},{9,8},{10,9... | collective-permute-start | bytes 442376 | tf_op jit(solution)/shard_map/ppermute | solution.py:236
  123.9 14.5 %collective-permute-start.19 = (bf16[4,4,2,16,2304]{4,3,2,1,0:T(8,128)(2,1)S(1)}, bf16[4,4,2,16,2304]{4,3,2,1,0:T(8,128)(2,1)}, u32[]{:S(2)}, u32[]{:S(2)}) collective-permute-start(bf16[4,4,2,16,2304]{4,3,2,1,0:T(8,128)(2,1)S(1)} %bitcast.20), channel_id=1, source_target_pairs={{0,64},{64,0},{1,65},{65,1},{2,66},{66,2},{3,67},{67,3},{4,68},{68... | collective-permute-start | bytes 7077896 | tf_op jit(solution)/shard_map/ppermute | solution.py:276

commit v5 on v4

--- a/solution.py
+++ b/solution.py
@@ -16,7 +16,6 @@
 SEND = 2.0**-5
 VMEM = 14 * 1024 * 1024
 LARGE = 44 * 1024 * 1024
-Z = ("zh", "zl")
 LAT = ("zl", "x", "y")
 LAYER = ("zh", "co")
 
@@ -88,7 +87,7 @@
     tile_row = (lax.broadcasted_iota(jnp.int32, (256, BLK), 0) // 4 + zl) % 4 // 2
     q = lax.broadcasted_iota(jnp.int32, (256, 256), 0)
     c = lax.broadcasted_iota(jnp.int32, (256, 256), 1)
-    same = (q // 4 % 4 == (c // 4 + zl) % 4) & (q // 2 % 2 == c // 2 % 2)
+    same = (q // 4 % 4 == c // 4 % 4) & (q // 2 % 2 == c // 2 % 2)
     own = same & (q // 16 == c // 16)
     other = same & (c // 64 == q // 16 % 4) & (c // 16 % 4 == q // 64)
     for h in range(2):
@@ -265,12 +264,15 @@
     partial, base = mine(pos, lat, dec_weight[0], dec_bias, targets)
     partial = (partial + received.astype(jnp.float32)).astype(jnp.float16).reshape(4, 128, D)
     partial = reduce4([partial[k] for k in range(4)], wide).astype(jnp.float16).reshape(4, 32, D)
-    column = reduce4([partial[k] for k in range(4)], narrow).astype(jnp.float16).reshape(8, 4, D)
-    column = lax.all_to_all(column, Z, 0, 0, tiled=True).astype(jnp.float32)
-    errs = (jnp.sum(column, axis=0) * (1.0 / SEND) + base).astype(jnp.bfloat16)
-    recon_error = errs.reshape(2, 2, D)
-    errs = lax.all_to_all(jnp.broadcast_to(errs[None], (8, 4, D)), Z, 0, 0, tiled=True)
-    errs = jnp.concatenate(gather4(errs.reshape(32, D), narrow))
+    column = reduce4([partial[k] for k in range(4)], narrow).astype(jnp.float16).reshape(2, 4, 4, D)
+    column = reduce4([column[:, k] for k in range(4)], z_lines)
+    at_half = jnp.arange(2)[:, None, None] == lax.axis_index("zh")
+    column = (column + jnp.where(at_half, base[None] * SEND, 0.0)).astype(jnp.float16)
+    far = lax.ppermute(column, "zh", swap)
+    errs = ((column.astype(jnp.float32) + far.astype(jnp.float32)) * (1.0 / SEND)).astype(jnp.bfloat16)
+    recon_error = jnp.where(lax.axis_index("zh") == 0, errs[0], errs[1]).reshape(2, 2, D)
+    errs = jnp.stack(gather4(errs, z_lines), axis=1).reshape(32, D)
+    errs = jnp.concatenate(gather4(errs, narrow))
     own = jnp.broadcast_to(errs[None], (4, 128, D))
     own = lax.all_to_all(own, ALL, 0, 0, axis_index_groups=wide, tiled=True).reshape(4, 4, 2, 16, D)
     other = lax.ppermute(own, "co", swap)

time: 143 us -> 141 us (0.986)
  blocking collectives: 43.8 us -> 20.2 us
  starting transfers between devices: 41.3 us -> 52.2 us
  waiting for transfers between devices: 33.2 us -> 44.1 us
    all_to_all x2 -> x0, blocking collectives: 24.5 us -> none  [the longest x1 14 us: local(): column = lax.all_to_all(column, Z, 0, 0, tiled=True).astype(jnp.float32)]
    ppermute x18 -> x24, waiting for transfers between devices: 32.8 us -> 41.2 us  [shift(): return lax.ppermute(block, ALL, perm)]
    ppermute x18 -> x24, starting transfers between devices: 25.8 us -> 31.3 us  [shift(): return lax.ppermute(block, ALL, perm)]
    ppermute x0 -> x1, starting transfers between devices: none -> 4.68 us  [local(): far = lax.ppermute(column, 'zh', swap)]
    ppermute x0 -> x1, waiting for transfers between devices: none -> 2.28 us  [local(): far = lax.ppermute(column, 'zh', swap)]
  transfers between devices with their start and end apart: 20 -> 27, of which waited for: 14 -> 19; matrix products, arithmetic and copies ran while one was open for 2% -> 2% of each run, Pallas kernels for 5% -> 5%
where the time goes in v5:
time: 141 us
  starting transfers between devices  52.2 us (37%)
  waiting for transfers between devices  44.1 us (31%)
  blocking collectives  20.2 us (14%)
  Pallas kernels  15.1 us (11%)
  other arithmetic  4.33 us (3%)
  local copies, waits for them, and re-layouts  3.94 us (3%)
    ppermute x24, waiting for transfers between devices, shift(): return lax.ppermute(block, ALL, perm)  41.2 us
    ppermute x24, starting transfers between devices, shift(): return lax.ppermute(block, ALL, perm)  31.3 us
    all_to_all x1, blocking collectives, local(): lax.all_to_all(own, ALL, 0, 0, axis_index_groups=wide, tiled=True)  20.2 us
    ppermute x1, starting transfers between devices, local(): other = lax.ppermute(own, 'co', swap)  11.2 us
    pallas_call x2, Pallas kernels, gradients(): pl.pallas_call(functools.partial(grad_kernel, which), in_specs=[SM, VM, V...  6.99 us
    ppermute x1, starting transfers between devices, local(): received = lax.ppermute(sent.astype(jnp.float16), 'co', swap)  5.04 us
    ppermute x1, starting transfers between devices, local(): far = lax.ppermute(column, 'zh', swap)  4.68 us
    pallas_call x1, Pallas kernels, away(): pl.pallas_call(away_kernel, in_specs=[SM, ANY, VM, ANY, VM, VM, VM, VM],...  4.13 us
  transfers between devices with their start and end apart: 27, of which 19 were waited for; matrix products, arithmetic and copies ran while one was open for 2% of the time, Pallas kernels for 5%

profile of v5, /device:TPU:1, one launch (start us, length us, event | category | flops | bytes accessed | tf_op | source)
XLA Modules:
  0.0 140.9 jit_solution(7260586383607240683)
XLA Ops:
  1.4 2.5 %collective-permute-start.2 = (bf16[4,2304]{1,0:T(4,128)(2,1)S(1)}, bf16[4,2304]{1,0:T(4,128)(2,1)S(1)}, u32[]{:S(2)}, u32[]{:S(2)}) collective-permute-start(bf16[4,2304]{1,0:T(4,128)(2,1)S(1)} %reshape.64), channel_id=1, source_target_pairs={{0,16},{16,32},{32,48},{48,0},{1,17},{17,33},{33,49},{49,1},{2,18}... | collective-permute-start | bytes 55304 | tf_op jit(solution)/shard_map/ppermute | solution.py:235
  3.9 3.0 %collective-permute-start.1 = (bf16[4,2304]{1,0:T(4,128)(2,1)S(1)}, bf16[4,2304]{1,0:T(4,128)(2,1)S(1)}, u32[]{:S(2)}, u32[]{:S(2)}) collective-permute-start(bf16[4,2304]{1,0:T(4,128)(2,1)S(1)} %reshape.64), channel_id=1, source_target_pairs={{0,32},{16,48},{32,0},{48,16},{1,33},{17,49},{33,1},{49,17},{2,34}... | collective-permute-start | bytes 55304 | tf_op jit(solution)/shard_map/ppermute | solution.py:235
  10.9 2.5 %collective-permute-start.4 = (bf16[16,2304]{1,0:T(8,128)(2,1)S(1)}, bf16[16,2304]{1,0:T(8,128)(2,1)S(1)}, u32[]{:S(2)}, u32[]{:S(2)}) collective-permute-start(bf16[16,2304]{1,0:T(8,128)(2,1)S(1)} %pad_maximum_fusion.2), channel_id=1, source_target_pairs={{0,2},{1,3},{2,0},{3,1},{4,6},{5,7},{6,4},{7,5},{8,10},{9,11},{10,... | collective-permute-start | bytes 221192 | tf_op jit(solution)/shard_map/ppermute | solution.py:235
  18.0 2.9 %collective-permute-start.7 = (bf16[64,2304]{1,0:T(8,128)(2,1)S(1)}, bf16[64,2304]{1,0:T(8,128)(2,1)S(1)}, u32[]{:S(2)}, u32[]{:S(2)}) collective-permute-start(bf16[64,2304]{1,0:T(8,128)(2,1)S(1)} %concatenate.15.g0), channel_id=1, source_target_pairs={{0,8},{4,12},{8,0},{12,4},{1,9},{5,13},{9,1},{13,5},{2,10},{6,14},... | collective-permute-start | bytes 884744 | tf_op jit(solution)/shard_map/ppermute | solution.py:235
  23.8 4.3 %collective-permute-done.7.g2 = bf16[64,2304]{1,0:T(8,128)(2,1)S(1)} collective-permute-done((bf16[64,2304]{1,0:T(8,128)(2,1)S(1)}, bf16[64,2304]{1,0:T(8,128)(2,1)S(1)}, u32[]{:S(2)}, u32[]{:S(2)}) %collective-permute-start.7) | collective-permute-done | bytes 294944 | tf_op jit(solution)/shard_map/ppermute | solution.py:235
  29.4 4.1 %encode_and_decode_away.1 = (bf16[2,2,2,256,128]{4,3,2,1,0:T(8,128)(2,1)S(1)}, f32[16,2,16,2304]{3,2,1,0:T(8,128)S(1)}) custom-call(s32[9]{0:T(128)S(1)} %concatenate.13.pos, bf16[2,2304,128]{2,1,0:T(8,128)(2,1)S(1)} %bitcast.43, f32[2,128]{1,0:T(2,128)S(1)} %bitcast_convert_fusion.bias, bf16[9,128,2304]{2,1,0:T(8,128)(2,1)} %bitcast.44, ...), custom_call_target="tpu_custom_call" | custom-call | flops 1811939328 | bytes 12582912 | tf_op jit(solution)/shard_map/encode_and_decode_away/pallas_call | solution.py:131
  34.0 5.0 %collective-permute-start.9 = (f16[16,2,16,2304]{3,2,1,0:T(8,128)(2,1)S(1)}, f16[16,2,16,2304]{3,2,1,0:T(8,128)(2,1)S(1)}, u32[]{:S(2)}, u32[]{:S(2)}) collective-permute-start(f16[16,2,16,2304]{3,2,1,0:T(8,128)(2,1)S(1)} %convert_element_type.84), channel_id=1, source_target_pairs={{0,64},{64,0},{1,65},{65,1},{2,66},{66,2},{3,67},{67,3},{4,68},{68... | collective-permute-start | bytes 7077896 | tf_op jit(solution)/shard_map/ppermute | solution.py:263
  39.0 4.0 %decode_mine.1 = (f32[16,2,16,2304]{3,2,1,0:T(8,128)S(1)}, f32[4,2304]{1,0:T(4,128)S(1)}) custom-call(s32[9]{0:T(128)S(1)} %concatenate.13.pos, bf16[2,2,2,256,128]{4,3,2,1,0:T(8,128)(2,1)S(1)} %get-tuple-element.6.lat, bf16[9,128,2304]{2,1,0:T(8,128)(2,1)} %bitcast.45, bf16[2,2304]{1,0:T(2,128)(2,1)S(1)} %copy-done.2, bf16[2,2,2304]{2,1,0:T(2,128)(2,1)S(1)} %copy-done.1), custom_call_target="tpu_custom_call" | custom-call | flops 1207959552 | bytes 10485760 | tf_op jit(solution)/shard_map/decode_mine/pallas_call | solution.py:149
  44.5 2.4 %collective-permute-start.12 = (f16[128,2304]{1,0:T(8,128)(2,1)S(1)}, f16[128,2304]{1,0:T(8,128)(2,1)S(1)}, u32[]{:S(2)}, u32[]{:S(2)}) collective-permute-start(f16[128,2304]{1,0:T(8,128)(2,1)S(1)} %bitcast.49), channel_id=1, source_target_pairs={{0,12},{4,0},{8,4},{12,8},{1,13},{5,1},{9,5},{13,9},{2,14},{6,2},{... | collective-permute-start | bytes 1769480 | tf_op jit(solution)/shard_map/ppermute | solution.py:235
  47.5 12.5 %collective-permute-done.12 = f16[128,2304]{1,0:T(8,128)(2,1)S(1)} collective-permute-done((f16[128,2304]{1,0:T(8,128)(2,1)S(1)}, f16[128,2304]{1,0:T(8,128)(2,1)S(1)}, u32[]{:S(2)}, u32[]{:S(2)}) %collective-permute-start.12) | collective-permute-done | bytes 589856 | tf_op jit(solution)/shard_map/ppermute | solution.py:235
  60.0 3.4 %collective-permute-done.10 = f16[128,2304]{1,0:T(8,128)(2,1)S(1)} collective-permute-done((f16[128,2304]{1,0:T(8,128)(2,1)S(1)}, f16[128,2304]{1,0:T(8,128)(2,1)S(1)}, u32[]{:S(2)}, u32[]{:S(2)}) %collective-permute-start.10) | collective-permute-done | bytes 589856 | tf_op jit(solution)/shard_map/ppermute | solution.py:235
  69.6 2.6 %collective-permute-done.14 = f16[32,2304]{1,0:T(8,128)(2,1)S(1)} collective-permute-done((f16[32,2304]{1,0:T(8,128)(2,1)S(1)}, f16[32,2304]{1,0:T(8,128)(2,1)S(1)}, u32[]{:S(2)}, u32[]{:S(2)}) %collective-permute-start.14) | collective-permute-done | bytes 147488 | tf_op jit(solution)/shard_map/ppermute | solution.py:235
  72.5 3.3 %collective-permute-start.18 = (f16[2,4,2304]{2,1,0:T(4,128)(2,1)S(1)}, f16[2,4,2304]{2,1,0:T(4,128)(2,1)S(1)}, u32[]{:S(2)}, u32[]{:S(2)}) collective-permute-start(f16[2,4,2304]{2,1,0:T(4,128)(2,1)S(1)} %get-tuple-element.20), channel_id=1, source_target_pairs={{0,48},{16,0},{32,16},{48,32},{1,49},{17,1},{33,17},{49,33},{2,50}... | collective-permute-start | bytes 110600 | tf_op jit(solution)/shard_map/ppermute | solution.py:235
  77.1 2.5 %collective-permute-done.17 = f16[2,4,2304]{2,1,0:T(4,128)(2,1)S(1)} collective-permute-done((f16[2,4,2304]{2,1,0:T(4,128)(2,1)S(1)}, f16[2,4,2304]{2,1,0:T(4,128)(2,1)S(1)}, u32[]{:S(2)}, u32[]{:S(2)}) %collective-permute-start.17) | collective-permute-done | bytes 36896 | tf_op jit(solution)/shard_map/ppermute | solution.py:235
  79.7 4.7 %collective-permute-start.19 = (f16[2,4,2304]{2,1,0:T(4,128)(2,1)S(1)}, f16[2,4,2304]{2,1,0:T(4,128)(2,1)S(1)}, u32[]{:S(2)}, u32[]{:S(2)}) collective-permute-start(f16[2,4,2304]{2,1,0:T(4,128)(2,1)S(1)} %fusion.6), channel_id=1, source_target_pairs={{0,128},{128,0},{1,129},{129,1},{2,130},{130,2},{3,131},{131,3},{4... | collective-permute-start | bytes 110600 | tf_op jit(solution)/shard_map/ppermute | solution.py:271
  84.3 2.3 %collective-permute-done.19 = f16[2,4,2304]{2,1,0:T(4,128)(2,1)S(1)} collective-permute-done((f16[2,4,2304]{2,1,0:T(4,128)(2,1)S(1)}, f16[2,4,2304]{2,1,0:T(4,128)(2,1)S(1)}, u32[]{:S(2)}, u32[]{:S(2)}) %collective-permute-start.19) | collective-permute-done | bytes 36896 | tf_op jit(solution)/shard_map/ppermute | solution.py:271
  88.8 1.7 %collective-permute-done.21 = bf16[2,4,2304]{2,1,0:T(4,128)(2,1)S(1)} collective-permute-done((bf16[2,4,2304]{2,1,0:T(4,128)(2,1)S(1)}, bf16[2,4,2304]{2,1,0:T(4,128)(2,1)S(1)}, u32[]{:S(2)}, u32[]{:S(2)}) %collective-permute-start.21) | collective-permute-done | bytes 36896 | tf_op jit(solution)/shard_map/ppermute | solution.py:235
  90.5 2.8 %collective-permute-done.22 = bf16[2,4,2304]{2,1,0:T(4,128)(2,1)S(1)} collective-permute-done((bf16[2,4,2304]{2,1,0:T(4,128)(2,1)S(1)}, bf16[2,4,2304]{2,1,0:T(4,128)(2,1)S(1)}, u32[]{:S(2)}, u32[]{:S(2)}) %collective-permute-start.22) | collective-permute-done | bytes 36896 | tf_op jit(solution)/shard_map/ppermute | solution.py:235
  93.7 1.8 %collective-permute-start.24 = (bf16[32,2304]{1,0:T(8,128)(2,1)S(1)}, bf16[32,2304]{1,0:T(8,128)(2,1)S(1)}, u32[]{:S(2)}, u32[]{:S(2)}) collective-permute-start(bf16[32,2304]{1,0:T(8,128)(2,1)S(1)} %reshape.66), channel_id=1, source_target_pairs={{0,2},{1,3},{2,0},{3,1},{4,6},{5,7},{6,4},{7,5},{8,10},{9,11},{10,... | collective-permute-start | bytes 442376 | tf_op jit(solution)/shard_map/ppermute | solution.py:235
  96.9 3.6 %collective-permute-done.25 = bf16[32,2304]{1,0:T(8,128)(2,1)S(1)} collective-permute-done((bf16[32,2304]{1,0:T(8,128)(2,1)S(1)}, bf16[32,2304]{1,0:T(8,128)(2,1)S(1)}, u32[]{:S(2)}, u32[]{:S(2)}) %collective-permute-start.25) | collective-permute-done | bytes 147488 | tf_op jit(solution)/shard_map/ppermute | solution.py:235
  101.2 20.2 %all_to_all.5 = bf16[4,128,2304]{2,1,0:T(8,128)(2,1)S(1)} all-to-all(bf16[4,128,2304]{2,1,0:T(8,128)(2,1)S(1)} %broadcast_in_dim.68), channel_id=1, replica_groups={{0,4,8,12},{1,5,9,13},{2,6,10,14},{3,7,11,15},{16,20,24,28},{17,21,25,2..., dimensions={0} | all-to-all | bytes 4718592 | tf_op jit(solution)/shard_map/all_to_all | solution.py:277
  121.4 11.2 %collective-permute-start.26 = (bf16[4,4,2,16,2304]{4,3,2,1,0:T(8,128)(2,1)S(1)}, bf16[4,4,2,16,2304]{4,3,2,1,0:T(8,128)(2,1)}, u32[]{:S(2)}, u32[]{:S(2)}) collective-permute-start(bf16[4,4,2,16,2304]{4,3,2,1,0:T(8,128)(2,1)S(1)} %bitcast.41), channel_id=1, source_target_pairs={{0,64},{64,0},{1,65},{65,1},{2,66},{66,2},{3,67},{67,3},{4,68},{68... | collective-permute-start | bytes 7077896 | tf_op jit(solution)/shard_map/ppermute | solution.py:278
  133.2 3.2 %gradients.2.rest_0_ = bf16[9,128,2304]{2,1,0:T(8,128)(2,1)} custom-call(s32[9]{0:T(128)S(1)} %concatenate.13.pos, bf16[2,2,2,256,128]{4,3,2,1,0:T(8,128)(2,1)S(1)} %get-tuple-element.6.lat, bf16[4,4,2,16,2304]{4,3,2,1,0:T(8,128)(2,1)S(1)} %bitcast.42), custom_call_target="tpu_custom_call" | custom-call | flops 1207959552 | bytes 8388608 | tf_op jit(solution)/shard_map/gradients/pallas_call | solution.py:204
  136.9 3.8 %gradients.3 = bf16[9,128,2304]{2,1,0:T(8,128)(2,1)} custom-call(s32[9]{0:T(128)S(1)} %concatenate.13.pos, bf16[2,2,2,256,128]{4,3,2,1,0:T(8,128)(2,1)S(1)} %get-tuple-element.6.lat, bf16[4,4,2,16,2304]{4,3,2,1,0:T(8,128)(2,1)} %collective-permute-done.26.errs, bf16[9,128,2304]{2,1,0:T(8,128)(2,1)} %gradients.2.rest_0_), custom_call_target="tpu_custom_call", output_to_operand_aliasing={{}: (3, {})} | custom-call | flops 1207959552 | bytes 8388608 | tf_op jit(solution)/shard_map/gradients/pallas_call | solution.py:204
  (70 shorter events, 29.7 us)
Async XLA Ops:
  1.4 7.8 %collective-permute-start.2 = (bf16[4,2304]{1,0:T(4,128)(2,1)S(1)}, bf16[4,2304]{1,0:T(4,128)(2,1)S(1)}, u32[]{:S(2)}, u32[]{:S(2)}) collective-permute-start(bf16[4,2304]{1,0:T(4,128)(2,1)S(1)} %reshape.64), channel_id=1, source_target_pairs={{0,16},{16,32},{32,48},{48,0},{1,17},{17,33},{33,49},{49,1},{2,18}... | collective-permute-start | bytes 55304 | tf_op jit(solution)/shard_map/ppermute | solution.py:235
  3.9 5.2 %collective-permute-start.1 = (bf16[4,2304]{1,0:T(4,128)(2,1)S(1)}, bf16[4,2304]{1,0:T(4,128)(2,1)S(1)}, u32[]{:S(2)}, u32[]{:S(2)}) collective-permute-start(bf16[4,2304]{1,0:T(4,128)(2,1)S(1)} %reshape.64), channel_id=1, source_target_pairs={{0,32},{16,48},{32,0},{48,16},{1,33},{17,49},{33,1},{49,17},{2,34}... | collective-permute-start | bytes 55304 | tf_op jit(solution)/shard_map/ppermute | solution.py:235
  9.9 4.8 %collective-permute-start.5 = (bf16[16,2304]{1,0:T(8,128)(2,1)S(1)}, bf16[16,2304]{1,0:T(8,128)(2,1)S(1)}, u32[]{:S(2)}, u32[]{:S(2)}) collective-permute-start(bf16[16,2304]{1,0:T(8,128)(2,1)S(1)} %pad_maximum_fusion.2), channel_id=1, source_target_pairs={{0,1},{1,2},{2,3},{3,0},{4,5},{5,6},{6,7},{7,4},{8,9},{9,10},{10,1... | collective-permute-start | bytes 221192 | tf_op jit(solution)/shard_map/ppermute | solution.py:235
  10.9 5.0 %collective-permute-start.4 = (bf16[16,2304]{1,0:T(8,128)(2,1)S(1)}, bf16[16,2304]{1,0:T(8,128)(2,1)S(1)}, u32[]{:S(2)}, u32[]{:S(2)}) collective-permute-start(bf16[16,2304]{1,0:T(8,128)(2,1)S(1)} %pad_maximum_fusion.2), channel_id=1, source_target_pairs={{0,2},{1,3},{2,0},{3,1},{4,6},{5,7},{6,4},{7,5},{8,10},{9,11},{10,... | collective-permute-start | bytes 221192 | tf_op jit(solution)/shard_map/ppermute | solution.py:235
  16.9 6.9 %collective-permute-start.8 = (bf16[64,2304]{1,0:T(8,128)(2,1)S(1)}, bf16[64,2304]{1,0:T(8,128)(2,1)S(1)}, u32[]{:S(2)}, u32[]{:S(2)}) collective-permute-start(bf16[64,2304]{1,0:T(8,128)(2,1)S(1)} %concatenate.15.g0), channel_id=1, source_target_pairs={{0,4},{4,8},{8,12},{12,0},{1,5},{5,9},{9,13},{13,1},{2,6},{6,10},{... | collective-permute-start | bytes 884744 | tf_op jit(solution)/shard_map/ppermute | solution.py:235
  18.0 10.2 %collective-permute-start.7 = (bf16[64,2304]{1,0:T(8,128)(2,1)S(1)}, bf16[64,2304]{1,0:T(8,128)(2,1)S(1)}, u32[]{:S(2)}, u32[]{:S(2)}) collective-permute-start(bf16[64,2304]{1,0:T(8,128)(2,1)S(1)} %concatenate.15.g0), channel_id=1, source_target_pairs={{0,8},{4,12},{8,0},{12,4},{1,9},{5,13},{9,1},{13,5},{2,10},{6,14},... | collective-permute-start | bytes 884744 | tf_op jit(solution)/shard_map/ppermute | solution.py:235
  20.9 7.3 %collective-permute-start.6 = (bf16[64,2304]{1,0:T(8,128)(2,1)S(1)}, bf16[64,2304]{1,0:T(8,128)(2,1)S(1)}, u32[]{:S(2)}, u32[]{:S(2)}) collective-permute-start(bf16[64,2304]{1,0:T(8,128)(2,1)S(1)} %concatenate.15.g0), channel_id=1, source_target_pairs={{0,12},{4,0},{8,4},{12,8},{1,13},{5,1},{9,5},{13,9},{2,14},{6,2},{... | collective-permute-start | bytes 884744 | tf_op jit(solution)/shard_map/ppermute | solution.py:235
  34.0 9.2 %collective-permute-start.9 = (f16[16,2,16,2304]{3,2,1,0:T(8,128)(2,1)S(1)}, f16[16,2,16,2304]{3,2,1,0:T(8,128)(2,1)S(1)}, u32[]{:S(2)}, u32[]{:S(2)}) collective-permute-start(f16[16,2,16,2304]{3,2,1,0:T(8,128)(2,1)S(1)} %convert_element_type.84), channel_id=1, source_target_pairs={{0,64},{64,0},{1,65},{65,1},{2,66},{66,2},{3,67},{67,3},{4,68},{68... | collective-permute-start | bytes 7077896 | tf_op jit(solution)/shard_map/ppermute | solution.py:263
  44.5 15.5 %collective-permute-start.12 = (f16[128,2304]{1,0:T(8,128)(2,1)S(1)}, f16[128,2304]{1,0:T(8,128)(2,1)S(1)}, u32[]{:S(2)}, u32[]{:S(2)}) collective-permute-start(f16[128,2304]{1,0:T(8,128)(2,1)S(1)} %bitcast.49), channel_id=1, source_target_pairs={{0,12},{4,0},{8,4},{12,8},{1,13},{5,1},{9,5},{13,9},{2,14},{6,2},{... | collective-permute-start | bytes 1769480 | tf_op jit(solution)/shard_map/ppermute | solution.py:235
  46.8 13.2 %collective-permute-start.11 = (f16[128,2304]{1,0:T(8,128)(2,1)S(1)}, f16[128,2304]{1,0:T(8,128)(2,1)S(1)}, u32[]{:S(2)}, u32[]{:S(2)}) collective-permute-start(f16[128,2304]{1,0:T(8,128)(2,1)S(1)} %bitcast.48), channel_id=1, source_target_pairs={{0,8},{4,12},{8,0},{12,4},{1,9},{5,13},{9,1},{13,5},{2,10},{6,14},... | collective-permute-start | bytes 1769480 | tf_op jit(solution)/shard_map/ppermute | solution.py:235
  46.8 16.6 %collective-permute-start.10 = (f16[128,2304]{1,0:T(8,128)(2,1)S(1)}, f16[128,2304]{1,0:T(8,128)(2,1)S(1)}, u32[]{:S(2)}, u32[]{:S(2)}) collective-permute-start(f16[128,2304]{1,0:T(8,128)(2,1)S(1)} %bitcast.47), channel_id=1, source_target_pairs={{0,4},{4,8},{8,12},{12,0},{1,5},{5,9},{9,13},{13,1},{2,6},{6,10},{... | collective-permute-start | bytes 1769480 | tf_op jit(solution)/shard_map/ppermute | solution.py:235
  64.0 5.3 %collective-permute-start.13 = (f16[32,2304]{1,0:T(8,128)(2,1)S(1)}, f16[32,2304]{1,0:T(8,128)(2,1)S(1)}, u32[]{:S(2)}, u32[]{:S(2)}) collective-permute-start(f16[32,2304]{1,0:T(8,128)(2,1)S(1)} %get-tuple-element.16), channel_id=1, source_target_pairs={{0,1},{1,2},{2,3},{3,0},{4,5},{5,6},{6,7},{7,4},{8,9},{9,10},{10,1... | collective-permute-start | bytes 442376 | tf_op jit(solution)/shard_map/ppermute | solution.py:235
  65.4 4.3 %collective-permute-start.15 = (f16[32,2304]{1,0:T(8,128)(2,1)S(1)}, f16[32,2304]{1,0:T(8,128)(2,1)S(1)}, u32[]{:S(2)}, u32[]{:S(2)}) collective-permute-start(f16[32,2304]{1,0:T(8,128)(2,1)S(1)} %get-tuple-element.17), channel_id=1, source_target_pairs={{0,3},{1,0},{2,1},{3,2},{4,7},{5,4},{6,5},{7,6},{8,11},{9,8},{10,9... | collective-permute-start | bytes 442376 | tf_op jit(solution)/shard_map/ppermute | solution.py:235
  66.7 5.5 %collective-permute-start.14 = (f16[32,2304]{1,0:T(8,128)(2,1)S(1)}, f16[32,2304]{1,0:T(8,128)(2,1)S(1)}, u32[]{:S(2)}, u32[]{:S(2)}) collective-permute-start(f16[32,2304]{1,0:T(8,128)(2,1)S(1)} %get-tuple-element.18), channel_id=1, source_target_pairs={{0,2},{1,3},{2,0},{3,1},{4,6},{5,7},{6,4},{7,5},{8,10},{9,11},{10,... | collective-permute-start | bytes 442376 | tf_op jit(solution)/shard_map/ppermute | solution.py:235
  72.4 4.7 %collective-permute-start.16 = (f16[2,4,2304]{2,1,0:T(4,128)(2,1)S(1)}, f16[2,4,2304]{2,1,0:T(4,128)(2,1)S(1)}, u32[]{:S(2)}, u32[]{:S(2)}) collective-permute-start(f16[2,4,2304]{2,1,0:T(4,128)(2,1)S(1)} %get-tuple-element.19), channel_id=1, source_target_pairs={{0,16},{16,32},{32,48},{48,0},{1,17},{17,33},{33,49},{49,1},{2,18}... | collective-permute-start | bytes 110600 | tf_op jit(solution)/shard_map/ppermute | solution.py:235
  72.5 4.6 %collective-permute-start.18 = (f16[2,4,2304]{2,1,0:T(4,128)(2,1)S(1)}, f16[2,4,2304]{2,1,0:T(4,128)(2,1)S(1)}, u32[]{:S(2)}, u32[]{:S(2)}) collective-permute-start(f16[2,4,2304]{2,1,0:T(4,128)(2,1)S(1)} %get-tuple-element.20), channel_id=1, source_target_pairs={{0,48},{16,0},{32,16},{48,32},{1,49},{17,1},{33,17},{49,33},{2,50}... | collective-permute-start | bytes 110600 | tf_op jit(solution)/shard_map/ppermute | solution.py:235
  75.8 3.8 %collective-permute-start.17 = (f16[2,4,2304]{2,1,0:T(4,128)(2,1)S(1)}, f16[2,4,2304]{2,1,0:T(4,128)(2,1)S(1)}, u32[]{:S(2)}, u32[]{:S(2)}) collective-permute-start(f16[2,4,2304]{2,1,0:T(4,128)(2,1)S(1)} %get-tuple-element.21), channel_id=1, source_target_pairs={{0,32},{16,48},{32,0},{48,16},{1,33},{17,49},{33,1},{49,17},{2,34}... | collective-permute-start | bytes 110600 | tf_op jit(solution)/shard_map/ppermute | solution.py:235
  79.7 7.0 %collective-permute-start.19 = (f16[2,4,2304]{2,1,0:T(4,128)(2,1)S(1)}, f16[2,4,2304]{2,1,0:T(4,128)(2,1)S(1)}, u32[]{:S(2)}, u32[]{:S(2)}) collective-permute-start(f16[2,4,2304]{2,1,0:T(4,128)(2,1)S(1)} %fusion.6), channel_id=1, source_target_pairs={{0,128},{128,0},{1,129},{129,1},{2,130},{130,2},{3,131},{131,3},{4... | collective-permute-start | bytes 110600 | tf_op jit(solution)/shard_map/ppermute | solution.py:271
  86.7 3.9 %collective-permute-start.21 = (bf16[2,4,2304]{2,1,0:T(4,128)(2,1)S(1)}, bf16[2,4,2304]{2,1,0:T(4,128)(2,1)S(1)}, u32[]{:S(2)}, u32[]{:S(2)}) collective-permute-start(bf16[2,4,2304]{2,1,0:T(4,128)(2,1)S(1)} %multiply_convert_fusion), channel_id=1, source_target_pairs={{0,32},{16,48},{32,0},{48,16},{1,33},{17,49},{33,1},{49,17},{2,34}... | collective-permute-start | bytes 110600 | tf_op jit(solution)/shard_map/ppermute | solution.py:235
  88.6 4.8 %collective-permute-start.22 = (bf16[2,4,2304]{2,1,0:T(4,128)(2,1)S(1)}, bf16[2,4,2304]{2,1,0:T(4,128)(2,1)S(1)}, u32[]{:S(2)}, u32[]{:S(2)}) collective-permute-start(bf16[2,4,2304]{2,1,0:T(4,128)(2,1)S(1)} %multiply_convert_fusion), channel_id=1, source_target_pairs={{0,16},{16,32},{32,48},{48,0},{1,17},{17,33},{33,49},{49,1},{2,18}... | collective-permute-start | bytes 110600 | tf_op jit(solution)/shard_map/ppermute | solution.py:235
  93.6 6.9 %collective-permute-start.25 = (bf16[32,2304]{1,0:T(8,128)(2,1)S(1)}, bf16[32,2304]{1,0:T(8,128)(2,1)S(1)}, u32[]{:S(2)}, u32[]{:S(2)}) collective-permute-start(bf16[32,2304]{1,0:T(8,128)(2,1)S(1)} %reshape.66), channel_id=1, source_target_pairs={{0,1},{1,2},{2,3},{3,0},{4,5},{5,6},{6,7},{7,4},{8,9},{9,10},{10,1... | collective-permute-start | bytes 442376 | tf_op jit(solution)/shard_map/ppermute | solution.py:235
  93.7 6.8 %collective-permute-start.24 = (bf16[32,2304]{1,0:T(8,128)(2,1)S(1)}, bf16[32,2304]{1,0:T(8,128)(2,1)S(1)}, u32[]{:S(2)}, u32[]{:S(2)}) collective-permute-start(bf16[32,2304]{1,0:T(8,128)(2,1)S(1)} %reshape.66), channel_id=1, source_target_pairs={{0,2},{1,3},{2,0},{3,1},{4,6},{5,7},{6,4},{7,5},{8,10},{9,11},{10,... | collective-permute-start | bytes 442376 | tf_op jit(solution)/shard_map/ppermute | solution.py:235
  95.5 5.5 %collective-permute-start.23 = (bf16[32,2304]{1,0:T(8,128)(2,1)S(1)}, bf16[32,2304]{1,0:T(8,128)(2,1)S(1)}, u32[]{:S(2)}, u32[]{:S(2)}) collective-permute-start(bf16[32,2304]{1,0:T(8,128)(2,1)S(1)} %reshape.66), channel_id=1, source_target_pairs={{0,3},{1,0},{2,1},{3,2},{4,7},{5,4},{6,5},{7,6},{8,11},{9,8},{10,9... | collective-permute-start | bytes 442376 | tf_op jit(solution)/shard_map/ppermute | solution.py:235
  121.4 15.5 %collective-permute-start.26 = (bf16[4,4,2,16,2304]{4,3,2,1,0:T(8,128)(2,1)S(1)}, bf16[4,4,2,16,2304]{4,3,2,1,0:T(8,128)(2,1)}, u32[]{:S(2)}, u32[]{:S(2)}) collective-permute-start(bf16[4,4,2,16,2304]{4,3,2,1,0:T(8,128)(2,1)S(1)} %bitcast.41), channel_id=1, source_target_pairs={{0,64},{64,0},{1,65},{65,1},{2,66},{66,2},{3,67},{67,3},{4,68},{68... | collective-permute-start | bytes 7077896 | tf_op jit(solution)/shard_map/ppermute | solution.py:278
  (6 other events, 21.8 us)

commit v6 on v5

--- a/solution.py
+++ b/solution.py
@@ -125,6 +125,7 @@
 
 HELD = [pltpu.VMEM((8, BLK, D), jnp.bfloat16)]
 SEMS = [pltpu.SemaphoreType.DMA((8,))]
+FAR = [pltpu.VMEM((2, 4, 4, 16, D), jnp.bfloat16), pltpu.SemaphoreType.DMA((2,))]
 
 
 def away(pos, enc, bias, dec, rows):
@@ -161,12 +162,22 @@
 
 
 def grad_kernel(which, pos, lat, errs, *rest):
-    out, held, sems = rest[-3:]
+    if which == 0:
+        out, held, sems = rest
+        halves = [errs.at[:, :, zh] for zh in range(2)]
+    else:
+        out, held, sems, halves, in_sems = rest[1:]
+        reads = [pltpu.make_async_copy(errs.at[:, :, zh], halves.at[zh], in_sems.at[zh]) for zh in range(2)]
+        for read in reads:
+            read.start()
+        halves = [halves.at[zh] for zh in range(2)]
     owner = pos[0]
     core = pos[1] if which == 0 else 1 - pos[1]
     place = pos[3 + which]
     writes = []
     for zh in range(2):
+        if which == 1:
+            reads[zh].wait()
         first = 2 * (2 * zh + core)
         slots = decoder_slots(zh, core, owner)
         for h in range(2):
@@ -183,7 +194,7 @@
                 lhs = jnp.concatenate([lat[which, h, 0], lat[which, h, 1]], axis=1)
                 for d in range(0, D, DC):
                     rows = [
-                        errs[(place + k) % 4, :, zh, :, d : d + DC].reshape(64, DC) for k in range(4)
+                        halves[zh][(place + k) % 4, :, :, d : d + DC].reshape(64, DC) for k in range(4)
                     ]
                     total = lax.dot_general(
                         lhs,
@@ -203,10 +214,10 @@
 def gradients(which, pos, lat, errs, *before):
     return pl.pallas_call(
         functools.partial(grad_kernel, which),
-        in_specs=[SM, VM, VM] + [ANY] * len(before),
+        in_specs=[SM, VM, ANY if before else VM] + [ANY] * len(before),
         out_specs=ANY,
         out_shape=jax.ShapeDtypeStruct((PAIRS, BLK, D), jnp.bfloat16),
-        scratch_shapes=HELD + SEMS,
+        scratch_shapes=HELD + SEMS + (FAR if before else []),
         input_output_aliases={3: 0} if before else {},
         cost_estimate=pl.CostEstimate(
             flops=4 * 2 * 256 * 256 * D, bytes_accessed=8 * 2**20, transcendentals=0

time: 141 us -> 141 us (level)
  no operation moved by 1% of the time
where the time goes in v6:
time: 141 us
  starting transfers between devices  52.2 us (37%)
  waiting for transfers between devices  44.1 us (31%)
  blocking collectives  20.2 us (14%)
  Pallas kernels  15.2 us (11%)
  other arithmetic  4.33 us (3%)
  local copies, waits for them, and re-layouts  3.94 us (3%)
    ppermute x24, waiting for transfers between devices, shift(): return lax.ppermute(block, ALL, perm)  41.2 us
    ppermute x24, starting transfers between devices, shift(): return lax.ppermute(block, ALL, perm)  31.3 us
    all_to_all x1, blocking collectives, local(): lax.all_to_all(own, ALL, 0, 0, axis_index_groups=wide, tiled=True)  20.2 us
    ppermute x1, starting transfers between devices, local(): other = lax.ppermute(own, 'co', swap)  11.2 us
    pallas_call x2, Pallas kernels, gradients(): pl.pallas_call(functools.partial(grad_kernel, which), in_specs=[SM, VM, A...  7.13 us
    ppermute x1, starting transfers between devices, local(): received = lax.ppermute(sent.astype(jnp.float16), 'co', swap)  5.04 us
    ppermute x1, starting transfers between devices, local(): far = lax.ppermute(column, 'zh', swap)  4.68 us
    pallas_call x1, Pallas kernels, away(): pl.pallas_call(away_kernel, in_specs=[SM, ANY, VM, ANY, VM, VM, VM, VM],...  4.13 us
  transfers between devices with their start and end apart: 27, of which 19 were waited for; matrix products, arithmetic and copies ran while one was open for 2% of the time, Pallas kernels for 5%

profile of v6, /device:TPU:1, one launch (start us, length us, event | category | flops | bytes accessed | tf_op | source)
XLA Modules:
  0.0 141.0 jit_solution(8788962062631363181)
XLA Ops:
  1.4 2.5 %collective-permute-start.2 = (bf16[4,2304]{1,0:T(4,128)(2,1)S(1)}, bf16[4,2304]{1,0:T(4,128)(2,1)S(1)}, u32[]{:S(2)}, u32[]{:S(2)}) collective-permute-start(bf16[4,2304]{1,0:T(4,128)(2,1)S(1)} %reshape.64), channel_id=1, source_target_pairs={{0,16},{16,32},{32,48},{48,0},{1,17},{17,33},{33,49},{49,1},{2,18}... | collective-permute-start | bytes 55304 | tf_op jit(solution)/shard_map/ppermute | solution.py:246
  3.9 3.0 %collective-permute-start.1 = (bf16[4,2304]{1,0:T(4,128)(2,1)S(1)}, bf16[4,2304]{1,0:T(4,128)(2,1)S(1)}, u32[]{:S(2)}, u32[]{:S(2)}) collective-permute-start(bf16[4,2304]{1,0:T(4,128)(2,1)S(1)} %reshape.64), channel_id=1, source_target_pairs={{0,32},{16,48},{32,0},{48,16},{1,33},{17,49},{33,1},{49,17},{2,34}... | collective-permute-start | bytes 55304 | tf_op jit(solution)/shard_map/ppermute | solution.py:246
  10.9 2.5 %collective-permute-start.4 = (bf16[16,2304]{1,0:T(8,128)(2,1)S(1)}, bf16[16,2304]{1,0:T(8,128)(2,1)S(1)}, u32[]{:S(2)}, u32[]{:S(2)}) collective-permute-start(bf16[16,2304]{1,0:T(8,128)(2,1)S(1)} %pad_maximum_fusion.2), channel_id=1, source_target_pairs={{0,2},{1,3},{2,0},{3,1},{4,6},{5,7},{6,4},{7,5},{8,10},{9,11},{10,... | collective-permute-start | bytes 221192 | tf_op jit(solution)/shard_map/ppermute | solution.py:246
  18.0 2.9 %collective-permute-start.7 = (bf16[64,2304]{1,0:T(8,128)(2,1)S(1)}, bf16[64,2304]{1,0:T(8,128)(2,1)S(1)}, u32[]{:S(2)}, u32[]{:S(2)}) collective-permute-start(bf16[64,2304]{1,0:T(8,128)(2,1)S(1)} %concatenate.15.g0), channel_id=1, source_target_pairs={{0,8},{4,12},{8,0},{12,4},{1,9},{5,13},{9,1},{13,5},{2,10},{6,14},... | collective-permute-start | bytes 884744 | tf_op jit(solution)/shard_map/ppermute | solution.py:246
  23.8 4.3 %collective-permute-done.7.g2 = bf16[64,2304]{1,0:T(8,128)(2,1)S(1)} collective-permute-done((bf16[64,2304]{1,0:T(8,128)(2,1)S(1)}, bf16[64,2304]{1,0:T(8,128)(2,1)S(1)}, u32[]{:S(2)}, u32[]{:S(2)}) %collective-permute-start.7) | collective-permute-done | bytes 294944 | tf_op jit(solution)/shard_map/ppermute | solution.py:246
  29.4 4.1 %encode_and_decode_away.1 = (bf16[2,2,2,256,128]{4,3,2,1,0:T(8,128)(2,1)S(1)}, f32[16,2,16,2304]{3,2,1,0:T(8,128)S(1)}) custom-call(s32[9]{0:T(128)S(1)} %concatenate.13.pos, bf16[2,2304,128]{2,1,0:T(8,128)(2,1)S(1)} %bitcast.43, f32[2,128]{1,0:T(2,128)S(1)} %bitcast_convert_fusion.bias, bf16[9,128,2304]{2,1,0:T(8,128)(2,1)} %bitcast.44, ...), custom_call_target="tpu_custom_call" | custom-call | flops 1811939328 | bytes 12582912 | tf_op jit(solution)/shard_map/encode_and_decode_away/pallas_call | solution.py:132
  34.0 5.0 %collective-permute-start.9 = (f16[16,2,16,2304]{3,2,1,0:T(8,128)(2,1)S(1)}, f16[16,2,16,2304]{3,2,1,0:T(8,128)(2,1)S(1)}, u32[]{:S(2)}, u32[]{:S(2)}) collective-permute-start(f16[16,2,16,2304]{3,2,1,0:T(8,128)(2,1)S(1)} %convert_element_type.84), channel_id=1, source_target_pairs={{0,64},{64,0},{1,65},{65,1},{2,66},{66,2},{3,67},{67,3},{4,68},{68... | collective-permute-start | bytes 7077896 | tf_op jit(solution)/shard_map/ppermute | solution.py:274
  39.0 4.0 %decode_mine.1 = (f32[16,2,16,2304]{3,2,1,0:T(8,128)S(1)}, f32[4,2304]{1,0:T(4,128)S(1)}) custom-call(s32[9]{0:T(128)S(1)} %concatenate.13.pos, bf16[2,2,2,256,128]{4,3,2,1,0:T(8,128)(2,1)S(1)} %get-tuple-element.6.lat, bf16[9,128,2304]{2,1,0:T(8,128)(2,1)} %bitcast.45, bf16[2,2304]{1,0:T(2,128)(2,1)S(1)} %copy-done.2, bf16[2,2,2304]{2,1,0:T(2,128)(2,1)S(1)} %copy-done.1), custom_call_target="tpu_custom_call" | custom-call | flops 1207959552 | bytes 10485760 | tf_op jit(solution)/shard_map/decode_mine/pallas_call | solution.py:150
  44.5 2.4 %collective-permute-start.12 = (f16[128,2304]{1,0:T(8,128)(2,1)S(1)}, f16[128,2304]{1,0:T(8,128)(2,1)S(1)}, u32[]{:S(2)}, u32[]{:S(2)}) collective-permute-start(f16[128,2304]{1,0:T(8,128)(2,1)S(1)} %bitcast.49), channel_id=1, source_target_pairs={{0,12},{4,0},{8,4},{12,8},{1,13},{5,1},{9,5},{13,9},{2,14},{6,2},{... | collective-permute-start | bytes 1769480 | tf_op jit(solution)/shard_map/ppermute | solution.py:246
  47.5 12.5 %collective-permute-done.12 = f16[128,2304]{1,0:T(8,128)(2,1)S(1)} collective-permute-done((f16[128,2304]{1,0:T(8,128)(2,1)S(1)}, f16[128,2304]{1,0:T(8,128)(2,1)S(1)}, u32[]{:S(2)}, u32[]{:S(2)}) %collective-permute-start.12) | collective-permute-done | bytes 589856 | tf_op jit(solution)/shard_map/ppermute | solution.py:246
  60.0 3.4 %collective-permute-done.10 = f16[128,2304]{1,0:T(8,128)(2,1)S(1)} collective-permute-done((f16[128,2304]{1,0:T(8,128)(2,1)S(1)}, f16[128,2304]{1,0:T(8,128)(2,1)S(1)}, u32[]{:S(2)}, u32[]{:S(2)}) %collective-permute-start.10) | collective-permute-done | bytes 589856 | tf_op jit(solution)/shard_map/ppermute | solution.py:246
  69.6 2.6 %collective-permute-done.14 = f16[32,2304]{1,0:T(8,128)(2,1)S(1)} collective-permute-done((f16[32,2304]{1,0:T(8,128)(2,1)S(1)}, f16[32,2304]{1,0:T(8,128)(2,1)S(1)}, u32[]{:S(2)}, u32[]{:S(2)}) %collective-permute-start.14) | collective-permute-done | bytes 147488 | tf_op jit(solution)/shard_map/ppermute | solution.py:246
  72.5 3.3 %collective-permute-start.18 = (f16[2,4,2304]{2,1,0:T(4,128)(2,1)S(1)}, f16[2,4,2304]{2,1,0:T(4,128)(2,1)S(1)}, u32[]{:S(2)}, u32[]{:S(2)}) collective-permute-start(f16[2,4,2304]{2,1,0:T(4,128)(2,1)S(1)} %get-tuple-element.20), channel_id=1, source_target_pairs={{0,48},{16,0},{32,16},{48,32},{1,49},{17,1},{33,17},{49,33},{2,50}... | collective-permute-start | bytes 110600 | tf_op jit(solution)/shard_map/ppermute | solution.py:246
  77.1 2.5 %collective-permute-done.17 = f16[2,4,2304]{2,1,0:T(4,128)(2,1)S(1)} collective-permute-done((f16[2,4,2304]{2,1,0:T(4,128)(2,1)S(1)}, f16[2,4,2304]{2,1,0:T(4,128)(2,1)S(1)}, u32[]{:S(2)}, u32[]{:S(2)}) %collective-permute-start.17) | collective-permute-done | bytes 36896 | tf_op jit(solution)/shard_map/ppermute | solution.py:246
  79.7 4.7 %collective-permute-start.19 = (f16[2,4,2304]{2,1,0:T(4,128)(2,1)S(1)}, f16[2,4,2304]{2,1,0:T(4,128)(2,1)S(1)}, u32[]{:S(2)}, u32[]{:S(2)}) collective-permute-start(f16[2,4,2304]{2,1,0:T(4,128)(2,1)S(1)} %fusion.6), channel_id=1, source_target_pairs={{0,128},{128,0},{1,129},{129,1},{2,130},{130,2},{3,131},{131,3},{4... | collective-permute-start | bytes 110600 | tf_op jit(solution)/shard_map/ppermute | solution.py:282
  84.3 2.3 %collective-permute-done.19 = f16[2,4,2304]{2,1,0:T(4,128)(2,1)S(1)} collective-permute-done((f16[2,4,2304]{2,1,0:T(4,128)(2,1)S(1)}, f16[2,4,2304]{2,1,0:T(4,128)(2,1)S(1)}, u32[]{:S(2)}, u32[]{:S(2)}) %collective-permute-start.19) | collective-permute-done | bytes 36896 | tf_op jit(solution)/shard_map/ppermute | solution.py:282
  88.8 1.7 %collective-permute-done.21 = bf16[2,4,2304]{2,1,0:T(4,128)(2,1)S(1)} collective-permute-done((bf16[2,4,2304]{2,1,0:T(4,128)(2,1)S(1)}, bf16[2,4,2304]{2,1,0:T(4,128)(2,1)S(1)}, u32[]{:S(2)}, u32[]{:S(2)}) %collective-permute-start.21) | collective-permute-done | bytes 36896 | tf_op jit(solution)/shard_map/ppermute | solution.py:246
  90.5 2.8 %collective-permute-done.22 = bf16[2,4,2304]{2,1,0:T(4,128)(2,1)S(1)} collective-permute-done((bf16[2,4,2304]{2,1,0:T(4,128)(2,1)S(1)}, bf16[2,4,2304]{2,1,0:T(4,128)(2,1)S(1)}, u32[]{:S(2)}, u32[]{:S(2)}) %collective-permute-start.22) | collective-permute-done | bytes 36896 | tf_op jit(solution)/shard_map/ppermute | solution.py:246
  93.7 1.8 %collective-permute-start.24 = (bf16[32,2304]{1,0:T(8,128)(2,1)S(1)}, bf16[32,2304]{1,0:T(8,128)(2,1)S(1)}, u32[]{:S(2)}, u32[]{:S(2)}) collective-permute-start(bf16[32,2304]{1,0:T(8,128)(2,1)S(1)} %reshape.66), channel_id=1, source_target_pairs={{0,2},{1,3},{2,0},{3,1},{4,6},{5,7},{6,4},{7,5},{8,10},{9,11},{10,... | collective-permute-start | bytes 442376 | tf_op jit(solution)/shard_map/ppermute | solution.py:246
  96.9 3.6 %collective-permute-done.25 = bf16[32,2304]{1,0:T(8,128)(2,1)S(1)} collective-permute-done((bf16[32,2304]{1,0:T(8,128)(2,1)S(1)}, bf16[32,2304]{1,0:T(8,128)(2,1)S(1)}, u32[]{:S(2)}, u32[]{:S(2)}) %collective-permute-start.25) | collective-permute-done | bytes 147488 | tf_op jit(solution)/shard_map/ppermute | solution.py:246
  101.2 20.2 %all_to_all.5 = bf16[4,128,2304]{2,1,0:T(8,128)(2,1)S(1)} all-to-all(bf16[4,128,2304]{2,1,0:T(8,128)(2,1)S(1)} %broadcast_in_dim.68), channel_id=1, replica_groups={{0,4,8,12},{1,5,9,13},{2,6,10,14},{3,7,11,15},{16,20,24,28},{17,21,25,2..., dimensions={0} | all-to-all | bytes 4718592 | tf_op jit(solution)/shard_map/all_to_all | solution.py:288
  121.4 11.2 %collective-permute-start.26 = (bf16[4,4,2,16,2304]{4,3,2,1,0:T(8,128)(2,1)S(1)}, bf16[4,4,2,16,2304]{4,3,2,1,0:T(8,128)(2,1)}, u32[]{:S(2)}, u32[]{:S(2)}) collective-permute-start(bf16[4,4,2,16,2304]{4,3,2,1,0:T(8,128)(2,1)S(1)} %bitcast.41), channel_id=1, source_target_pairs={{0,64},{64,0},{1,65},{65,1},{2,66},{66,2},{3,67},{67,3},{4,68},{68... | collective-permute-start | bytes 7077896 | tf_op jit(solution)/shard_map/ppermute | solution.py:289
  133.2 3.2 %gradients.2.rest_0_ = bf16[9,128,2304]{2,1,0:T(8,128)(2,1)} custom-call(s32[9]{0:T(128)S(1)} %concatenate.13.pos, bf16[2,2,2,256,128]{4,3,2,1,0:T(8,128)(2,1)S(1)} %get-tuple-element.6.lat, bf16[4,4,2,16,2304]{4,3,2,1,0:T(8,128)(2,1)S(1)} %bitcast.42), custom_call_target="tpu_custom_call" | custom-call | flops 1207959552 | bytes 8388608 | tf_op jit(solution)/shard_map/gradients/pallas_call | solution.py:215
  136.9 3.9 %gradients.3 = bf16[9,128,2304]{2,1,0:T(8,128)(2,1)} custom-call(s32[9]{0:T(128)S(1)} %concatenate.13.pos, bf16[2,2,2,256,128]{4,3,2,1,0:T(8,128)(2,1)S(1)} %get-tuple-element.6.lat, bf16[4,4,2,16,2304]{4,3,2,1,0:T(8,128)(2,1)} %collective-permute-done.26.errs, bf16[9,128,2304]{2,1,0:T(8,128)(2,1)} %gradients.2.rest_0_), custom_call_target="tpu_custom_call", output_to_operand_aliasing={{}: (3, {})} | custom-call | flops 1207959552 | bytes 8388608 | tf_op jit(solution)/shard_map/gradients/pallas_call | solution.py:215
  (70 shorter events, 29.7 us)
Async XLA Ops:
  1.4 7.8 %collective-permute-start.2 = (bf16[4,2304]{1,0:T(4,128)(2,1)S(1)}, bf16[4,2304]{1,0:T(4,128)(2,1)S(1)}, u32[]{:S(2)}, u32[]{:S(2)}) collective-permute-start(bf16[4,2304]{1,0:T(4,128)(2,1)S(1)} %reshape.64), channel_id=1, source_target_pairs={{0,16},{16,32},{32,48},{48,0},{1,17},{17,33},{33,49},{49,1},{2,18}... | collective-permute-start | bytes 55304 | tf_op jit(solution)/shard_map/ppermute | solution.py:246
  3.9 5.2 %collective-permute-start.1 = (bf16[4,2304]{1,0:T(4,128)(2,1)S(1)}, bf16[4,2304]{1,0:T(4,128)(2,1)S(1)}, u32[]{:S(2)}, u32[]{:S(2)}) collective-permute-start(bf16[4,2304]{1,0:T(4,128)(2,1)S(1)} %reshape.64), channel_id=1, source_target_pairs={{0,32},{16,48},{32,0},{48,16},{1,33},{17,49},{33,1},{49,17},{2,34}... | collective-permute-start | bytes 55304 | tf_op jit(solution)/shard_map/ppermute | solution.py:246
  9.9 4.8 %collective-permute-start.5 = (bf16[16,2304]{1,0:T(8,128)(2,1)S(1)}, bf16[16,2304]{1,0:T(8,128)(2,1)S(1)}, u32[]{:S(2)}, u32[]{:S(2)}) collective-permute-start(bf16[16,2304]{1,0:T(8,128)(2,1)S(1)} %pad_maximum_fusion.2), channel_id=1, source_target_pairs={{0,1},{1,2},{2,3},{3,0},{4,5},{5,6},{6,7},{7,4},{8,9},{9,10},{10,1... | collective-permute-start | bytes 221192 | tf_op jit(solution)/shard_map/ppermute | solution.py:246
  10.9 5.0 %collective-permute-start.4 = (bf16[16,2304]{1,0:T(8,128)(2,1)S(1)}, bf16[16,2304]{1,0:T(8,128)(2,1)S(1)}, u32[]{:S(2)}, u32[]{:S(2)}) collective-permute-start(bf16[16,2304]{1,0:T(8,128)(2,1)S(1)} %pad_maximum_fusion.2), channel_id=1, source_target_pairs={{0,2},{1,3},{2,0},{3,1},{4,6},{5,7},{6,4},{7,5},{8,10},{9,11},{10,... | collective-permute-start | bytes 221192 | tf_op jit(solution)/shard_map/ppermute | solution.py:246
  16.9 6.9 %collective-permute-start.8 = (bf16[64,2304]{1,0:T(8,128)(2,1)S(1)}, bf16[64,2304]{1,0:T(8,128)(2,1)S(1)}, u32[]{:S(2)}, u32[]{:S(2)}) collective-permute-start(bf16[64,2304]{1,0:T(8,128)(2,1)S(1)} %concatenate.15.g0), channel_id=1, source_target_pairs={{0,4},{4,8},{8,12},{12,0},{1,5},{5,9},{9,13},{13,1},{2,6},{6,10},{... | collective-permute-start | bytes 884744 | tf_op jit(solution)/shard_map/ppermute | solution.py:246
  18.0 10.2 %collective-permute-start.7 = (bf16[64,2304]{1,0:T(8,128)(2,1)S(1)}, bf16[64,2304]{1,0:T(8,128)(2,1)S(1)}, u32[]{:S(2)}, u32[]{:S(2)}) collective-permute-start(bf16[64,2304]{1,0:T(8,128)(2,1)S(1)} %concatenate.15.g0), channel_id=1, source_target_pairs={{0,8},{4,12},{8,0},{12,4},{1,9},{5,13},{9,1},{13,5},{2,10},{6,14},... | collective-permute-start | bytes 884744 | tf_op jit(solution)/shard_map/ppermute | solution.py:246
  20.9 7.3 %collective-permute-start.6 = (bf16[64,2304]{1,0:T(8,128)(2,1)S(1)}, bf16[64,2304]{1,0:T(8,128)(2,1)S(1)}, u32[]{:S(2)}, u32[]{:S(2)}) collective-permute-start(bf16[64,2304]{1,0:T(8,128)(2,1)S(1)} %concatenate.15.g0), channel_id=1, source_target_pairs={{0,12},{4,0},{8,4},{12,8},{1,13},{5,1},{9,5},{13,9},{2,14},{6,2},{... | collective-permute-start | bytes 884744 | tf_op jit(solution)/shard_map/ppermute | solution.py:246
  34.0 9.2 %collective-permute-start.9 = (f16[16,2,16,2304]{3,2,1,0:T(8,128)(2,1)S(1)}, f16[16,2,16,2304]{3,2,1,0:T(8,128)(2,1)S(1)}, u32[]{:S(2)}, u32[]{:S(2)}) collective-permute-start(f16[16,2,16,2304]{3,2,1,0:T(8,128)(2,1)S(1)} %convert_element_type.84), channel_id=1, source_target_pairs={{0,64},{64,0},{1,65},{65,1},{2,66},{66,2},{3,67},{67,3},{4,68},{68... | collective-permute-start | bytes 7077896 | tf_op jit(solution)/shard_map/ppermute | solution.py:274
  44.5 15.5 %collective-permute-start.12 = (f16[128,2304]{1,0:T(8,128)(2,1)S(1)}, f16[128,2304]{1,0:T(8,128)(2,1)S(1)}, u32[]{:S(2)}, u32[]{:S(2)}) collective-permute-start(f16[128,2304]{1,0:T(8,128)(2,1)S(1)} %bitcast.49), channel_id=1, source_target_pairs={{0,12},{4,0},{8,4},{12,8},{1,13},{5,1},{9,5},{13,9},{2,14},{6,2},{... | collective-permute-start | bytes 1769480 | tf_op jit(solution)/shard_map/ppermute | solution.py:246
  46.8 13.2 %collective-permute-start.11 = (f16[128,2304]{1,0:T(8,128)(2,1)S(1)}, f16[128,2304]{1,0:T(8,128)(2,1)S(1)}, u32[]{:S(2)}, u32[]{:S(2)}) collective-permute-start(f16[128,2304]{1,0:T(8,128)(2,1)S(1)} %bitcast.48), channel_id=1, source_target_pairs={{0,8},{4,12},{8,0},{12,4},{1,9},{5,13},{9,1},{13,5},{2,10},{6,14},... | collective-permute-start | bytes 1769480 | tf_op jit(solution)/shard_map/ppermute | solution.py:246
  46.8 16.6 %collective-permute-start.10 = (f16[128,2304]{1,0:T(8,128)(2,1)S(1)}, f16[128,2304]{1,0:T(8,128)(2,1)S(1)}, u32[]{:S(2)}, u32[]{:S(2)}) collective-permute-start(f16[128,2304]{1,0:T(8,128)(2,1)S(1)} %bitcast.47), channel_id=1, source_target_pairs={{0,4},{4,8},{8,12},{12,0},{1,5},{5,9},{9,13},{13,1},{2,6},{6,10},{... | collective-permute-start | bytes 1769480 | tf_op jit(solution)/shard_map/ppermute | solution.py:246
  64.0 5.3 %collective-permute-start.13 = (f16[32,2304]{1,0:T(8,128)(2,1)S(1)}, f16[32,2304]{1,0:T(8,128)(2,1)S(1)}, u32[]{:S(2)}, u32[]{:S(2)}) collective-permute-start(f16[32,2304]{1,0:T(8,128)(2,1)S(1)} %get-tuple-element.16), channel_id=1, source_target_pairs={{0,1},{1,2},{2,3},{3,0},{4,5},{5,6},{6,7},{7,4},{8,9},{9,10},{10,1... | collective-permute-start | bytes 442376 | tf_op jit(solution)/shard_map/ppermute | solution.py:246
  65.4 4.3 %collective-permute-start.15 = (f16[32,2304]{1,0:T(8,128)(2,1)S(1)}, f16[32,2304]{1,0:T(8,128)(2,1)S(1)}, u32[]{:S(2)}, u32[]{:S(2)}) collective-permute-start(f16[32,2304]{1,0:T(8,128)(2,1)S(1)} %get-tuple-element.17), channel_id=1, source_target_pairs={{0,3},{1,0},{2,1},{3,2},{4,7},{5,4},{6,5},{7,6},{8,11},{9,8},{10,9... | collective-permute-start | bytes 442376 | tf_op jit(solution)/shard_map/ppermute | solution.py:246
  66.7 5.5 %collective-permute-start.14 = (f16[32,2304]{1,0:T(8,128)(2,1)S(1)}, f16[32,2304]{1,0:T(8,128)(2,1)S(1)}, u32[]{:S(2)}, u32[]{:S(2)}) collective-permute-start(f16[32,2304]{1,0:T(8,128)(2,1)S(1)} %get-tuple-element.18), channel_id=1, source_target_pairs={{0,2},{1,3},{2,0},{3,1},{4,6},{5,7},{6,4},{7,5},{8,10},{9,11},{10,... | collective-permute-start | bytes 442376 | tf_op jit(solution)/shard_map/ppermute | solution.py:246
  72.4 4.7 %collective-permute-start.16 = (f16[2,4,2304]{2,1,0:T(4,128)(2,1)S(1)}, f16[2,4,2304]{2,1,0:T(4,128)(2,1)S(1)}, u32[]{:S(2)}, u32[]{:S(2)}) collective-permute-start(f16[2,4,2304]{2,1,0:T(4,128)(2,1)S(1)} %get-tuple-element.19), channel_id=1, source_target_pairs={{0,16},{16,32},{32,48},{48,0},{1,17},{17,33},{33,49},{49,1},{2,18}... | collective-permute-start | bytes 110600 | tf_op jit(solution)/shard_map/ppermute | solution.py:246
  72.5 4.6 %collective-permute-start.18 = (f16[2,4,2304]{2,1,0:T(4,128)(2,1)S(1)}, f16[2,4,2304]{2,1,0:T(4,128)(2,1)S(1)}, u32[]{:S(2)}, u32[]{:S(2)}) collective-permute-start(f16[2,4,2304]{2,1,0:T(4,128)(2,1)S(1)} %get-tuple-element.20), channel_id=1, source_target_pairs={{0,48},{16,0},{32,16},{48,32},{1,49},{17,1},{33,17},{49,33},{2,50}... | collective-permute-start | bytes 110600 | tf_op jit(solution)/shard_map/ppermute | solution.py:246
  75.8 3.8 %collective-permute-start.17 = (f16[2,4,2304]{2,1,0:T(4,128)(2,1)S(1)}, f16[2,4,2304]{2,1,0:T(4,128)(2,1)S(1)}, u32[]{:S(2)}, u32[]{:S(2)}) collective-permute-start(f16[2,4,2304]{2,1,0:T(4,128)(2,1)S(1)} %get-tuple-element.21), channel_id=1, source_target_pairs={{0,32},{16,48},{32,0},{48,16},{1,33},{17,49},{33,1},{49,17},{2,34}... | collective-permute-start | bytes 110600 | tf_op jit(solution)/shard_map/ppermute | solution.py:246
  79.7 7.0 %collective-permute-start.19 = (f16[2,4,2304]{2,1,0:T(4,128)(2,1)S(1)}, f16[2,4,2304]{2,1,0:T(4,128)(2,1)S(1)}, u32[]{:S(2)}, u32[]{:S(2)}) collective-permute-start(f16[2,4,2304]{2,1,0:T(4,128)(2,1)S(1)} %fusion.6), channel_id=1, source_target_pairs={{0,128},{128,0},{1,129},{129,1},{2,130},{130,2},{3,131},{131,3},{4... | collective-permute-start | bytes 110600 | tf_op jit(solution)/shard_map/ppermute | solution.py:282
  86.7 3.9 %collective-permute-start.21 = (bf16[2,4,2304]{2,1,0:T(4,128)(2,1)S(1)}, bf16[2,4,2304]{2,1,0:T(4,128)(2,1)S(1)}, u32[]{:S(2)}, u32[]{:S(2)}) collective-permute-start(bf16[2,4,2304]{2,1,0:T(4,128)(2,1)S(1)} %multiply_convert_fusion), channel_id=1, source_target_pairs={{0,32},{16,48},{32,0},{48,16},{1,33},{17,49},{33,1},{49,17},{2,34}... | collective-permute-start | bytes 110600 | tf_op jit(solution)/shard_map/ppermute | solution.py:246
  88.6 4.8 %collective-permute-start.22 = (bf16[2,4,2304]{2,1,0:T(4,128)(2,1)S(1)}, bf16[2,4,2304]{2,1,0:T(4,128)(2,1)S(1)}, u32[]{:S(2)}, u32[]{:S(2)}) collective-permute-start(bf16[2,4,2304]{2,1,0:T(4,128)(2,1)S(1)} %multiply_convert_fusion), channel_id=1, source_target_pairs={{0,16},{16,32},{32,48},{48,0},{1,17},{17,33},{33,49},{49,1},{2,18}... | collective-permute-start | bytes 110600 | tf_op jit(solution)/shard_map/ppermute | solution.py:246
  93.6 6.9 %collective-permute-start.25 = (bf16[32,2304]{1,0:T(8,128)(2,1)S(1)}, bf16[32,2304]{1,0:T(8,128)(2,1)S(1)}, u32[]{:S(2)}, u32[]{:S(2)}) collective-permute-start(bf16[32,2304]{1,0:T(8,128)(2,1)S(1)} %reshape.66), channel_id=1, source_target_pairs={{0,1},{1,2},{2,3},{3,0},{4,5},{5,6},{6,7},{7,4},{8,9},{9,10},{10,1... | collective-permute-start | bytes 442376 | tf_op jit(solution)/shard_map/ppermute | solution.py:246
  93.7 6.8 %collective-permute-start.24 = (bf16[32,2304]{1,0:T(8,128)(2,1)S(1)}, bf16[32,2304]{1,0:T(8,128)(2,1)S(1)}, u32[]{:S(2)}, u32[]{:S(2)}) collective-permute-start(bf16[32,2304]{1,0:T(8,128)(2,1)S(1)} %reshape.66), channel_id=1, source_target_pairs={{0,2},{1,3},{2,0},{3,1},{4,6},{5,7},{6,4},{7,5},{8,10},{9,11},{10,... | collective-permute-start | bytes 442376 | tf_op jit(solution)/shard_map/ppermute | solution.py:246
  95.5 5.5 %collective-permute-start.23 = (bf16[32,2304]{1,0:T(8,128)(2,1)S(1)}, bf16[32,2304]{1,0:T(8,128)(2,1)S(1)}, u32[]{:S(2)}, u32[]{:S(2)}) collective-permute-start(bf16[32,2304]{1,0:T(8,128)(2,1)S(1)} %reshape.66), channel_id=1, source_target_pairs={{0,3},{1,0},{2,1},{3,2},{4,7},{5,4},{6,5},{7,6},{8,11},{9,8},{10,9... | collective-permute-start | bytes 442376 | tf_op jit(solution)/shard_map/ppermute | solution.py:246
  121.4 15.5 %collective-permute-start.26 = (bf16[4,4,2,16,2304]{4,3,2,1,0:T(8,128)(2,1)S(1)}, bf16[4,4,2,16,2304]{4,3,2,1,0:T(8,128)(2,1)}, u32[]{:S(2)}, u32[]{:S(2)}) collective-permute-start(bf16[4,4,2,16,2304]{4,3,2,1,0:T(8,128)(2,1)S(1)} %bitcast.41), channel_id=1, source_target_pairs={{0,64},{64,0},{1,65},{65,1},{2,66},{66,2},{3,67},{67,3},{4,68},{68... | collective-permute-start | bytes 7077896 | tf_op jit(solution)/shard_map/ppermute | solution.py:289
  (6 other events, 21.8 us)
